TPU v7x, 32 devices: a whole 2x2x4 slice. The times are simulated.
32 devices in a mesh: grp: 2 (over x), pts: 16 (over z, y, core).
Axes of the slice: x: 2, y: 2, z: 4, core: 2. Of those that a mesh axis runs over, the one named last changes fastest.
Arguments:
- points: bfloat16 [131072, 256], P(('grp', 'pts')), parts along dimension 0, may hold values from -24 to 24
- hil_dest: int32 [1024], P(('grp', 'pts')), parts along dimension 0, may hold values from 0 to 15, as said below
- hil_slot: int32 [1024], P(('grp', 'pts')), parts along dimension 0, may hold values from 0 to 31, as said below
- patch_ids: int32 [128, 1024], P(('grp', 'pts')), parts along dimension 0, may hold values from 0 to 3, never falling along the last dimension, each value on 1 to 512 neighbouring positions
- child_counts: int32 [32, 1024], P(('grp', 'pts')), parts along dimension 0, may hold values from 1 to 8, 4096 in all within a row
- parent_order: int32 [32, 1024], P(('grp', 'pts')), parts along dimension 0, may hold values from 0 to 1023, each once within a row
- w_qkv: bfloat16 [256, 768], replicated, may hold values from -0.375 to 0.375
- w_out: bfloat16 [256, 256], replicated, may hold values from -0.375 to 0.375
- w_pool: bfloat16 [256, 512], replicated, may hold values from -0.375 to 0.375
- norm_gain: float32 [512], replicated, may hold values from 0.1 to 1.9
- norm_shift: float32 [512], replicated, may hold values from -3 to 3
- cotangent: bfloat16 [32768, 512], P(('grp', 'pts')), parts along dimension 0, may hold values from -6 to 6
Outputs:
- pooled: bfloat16 [32768, 512], P(('grp', 'pts')), parts along dimension 0
- grad_points: bfloat16 [131072, 256], P(('grp', 'pts')), parts along dimension 0
- grad_weight: float32 [512, 512], P('grp'), parts along dimension 0
- grad_norm: float32 [4, 512], P('grp'), parts along dimension 0
There are 2 independent parts, one for each index of `grp`. A program takes and returns all parts, laid end to end along the dimension named above; an argument that names none is the same for every part. Nothing has to cross between parts.
Inputs may be any that keep to these rules, and one draw needn't show every extreme that they name: `hil_dest`: every device is the destination of exactly 32 blocks; no device sends more than 2 blocks to one device, and some device sends exactly 2 to one. `hil_slot`: the blocks sent to one device take each of its positions once.
All inputs are finite; a program needn't handle non-finite values.
Results may differ from a plain program's by a relative error of at most 0.012.
Values may be sent and summed in bfloat16 or wider, within the bound.
No kernel may reach another device: no remote copies, remote signals or barrier semaphores. Data moves between devices by JAX's collectives and lax.ppermute only.
A program may use at most 128 MiB of HBM per device.

v0:
```python
import jax
import jax.numpy as jnp
from jax import lax
from jax.sharding import PartitionSpec as P

HDIM = 16


inv_sqrt_two = 0.7071067811865476
inv_sqrt_tau = 0.3989422804014327
norm_eps = 1e-05


def parent_index(child_total, rows):
    run_ends = jnp.cumsum(child_total)
    run_starts = run_ends - child_total
    run_marks = jnp.zeros((rows,), jnp.int32).at[run_starts].add(1)
    return jnp.cumsum(run_marks) - 1


def attend_core(qkv_rows, patch_index):
    patch_rows = qkv_rows.shape[0]
    width = qkv_rows.shape[1] // 3
    groups = width // (4 * HDIM)

    def split_heads(which):
        columns = qkv_rows[:, which * width : (which + 1) * width]
        return columns.reshape(patch_rows, groups, 4, HDIM).transpose(1, 0, 2, 3)

    queries = split_heads(0)
    key_heads = split_heads(1)
    values = split_heads(2)
    allowed = patch_index[:, None] == patch_index[None, :]

    def one_group(triple):
        query_g, key_g, value_g = triple
        scores = jnp.einsum(
            "qhd,khd->hqk", query_g, key_g, preferred_element_type=jnp.float32
        ) * HDIM ** (-0.5)
        scores = jnp.where(allowed[None], scores, -jnp.inf)
        row_max = jnp.max(scores, axis=-1, keepdims=True)
        weights_exp = jnp.exp(scores - row_max)
        probability = (weights_exp / jnp.sum(weights_exp, axis=-1, keepdims=True)).astype(
            jnp.bfloat16
        )
        return jnp.einsum("hqk,khd->qhd", probability, value_g, preferred_element_type=jnp.float32)

    attended = lax.map(one_group, (queries, key_heads, values))
    return attended.transpose(1, 0, 2, 3).reshape(patch_rows, width).astype(jnp.bfloat16)


def route_rows(source, send_place, slots_total):
    return jnp.zeros((slots_total, source.shape[1]), jnp.bfloat16).at[send_place].set(source)


def local(
    points,
    hil_dest,
    hil_slot,
    patch_ids,
    child_counts,
    parent_order,
    w_qkv,
    w_out,
    w_pool,
    norm_gain,
    norm_shift,
    cotangent,
):
    devices = lax.axis_size("pts")
    count_blocks = hil_dest.shape[0]
    width = points.shape[1]
    patch_rows = patch_ids.shape[1]
    capacity = (count_blocks + devices - 1) // devices
    counter = jnp.arange(count_blocks)
    same_dest = hil_dest[:, None] == hil_dest[None, :]
    earlier = counter[:, None] > counter[None, :]
    slot_rank = jnp.sum(same_dest & earlier, axis=1)
    send_place = hil_dest * capacity + slot_rank
    slot_tags = (
        jnp.zeros((devices * capacity,), jnp.bfloat16)
        .at[send_place]
        .set((hil_slot + 1).astype(jnp.bfloat16))
    )
    payload = route_rows(points.reshape(count_blocks, -1), send_place, devices * capacity)
    received, got_tags = (
        lax.all_to_all(payload, "pts", split_axis=0, concat_axis=0, tiled=True),
        lax.all_to_all(slot_tags, "pts", split_axis=0, concat_axis=0, tiled=True),
    )
    got_slots = got_tags.astype(jnp.int32) - 1
    filled = got_slots >= 0
    target = jnp.where(filled, got_slots, count_blocks)
    ordered = (
        jnp.zeros((count_blocks, received.shape[1]), jnp.bfloat16)
        .at[target]
        .set(received, mode="drop")
    )
    patch_tiles = ordered.reshape(patch_ids.shape[0], patch_rows, -1)

    def full_tile(pair):
        tile_rows, patch_index = pair
        qkv_rows = jnp.dot(tile_rows, w_qkv, preferred_element_type=jnp.float32).astype(
            jnp.bfloat16
        )
        attended = attend_core(qkv_rows, patch_index)
        return (
            tile_rows.astype(jnp.float32)
            + jnp.dot(attended, w_out, preferred_element_type=jnp.float32)
        ).astype(jnp.bfloat16)

    result_tiles = lax.map(full_tile, (patch_tiles, patch_ids))
    result_blocks = result_tiles.reshape(count_blocks, -1)
    outgoing = jnp.where(filled[:, None], result_blocks[jnp.minimum(target, count_blocks - 1)], 0)
    returned = lax.all_to_all(outgoing, "pts", split_axis=0, concat_axis=0, tiled=True)
    home_rows = returned[send_place].reshape(-1, width)
    child_total = child_counts[0]
    send_order = parent_order[0]
    parents = child_total.shape[0]
    per_owner = parents // devices
    parent_ids = parent_index(child_total, home_rows.shape[0])
    child_sums = jax.ops.segment_sum(
        home_rows.astype(jnp.float32), parent_ids, num_segments=parents
    )
    parent_means = (child_sums / child_total.astype(jnp.float32)[:, None]).astype(jnp.bfloat16)
    outbound = parent_means[send_order].reshape(devices, per_owner, width)
    parent_in = lax.all_to_all(outbound, "pts", split_axis=0, concat_axis=0, tiled=True).reshape(
        parents, width
    )
    projected = jnp.dot(parent_in, w_pool, preferred_element_type=jnp.float32)
    centred = projected - jnp.mean(projected, axis=-1, keepdims=True)
    variance = jnp.mean(centred * centred, axis=-1, keepdims=True)
    inv_std = lax.rsqrt(variance + norm_eps)
    normed = centred * inv_std
    shifted = normed * norm_gain + norm_shift
    normal_cdf = 0.5 * (1.0 + jax.scipy.special.erf(shifted * inv_sqrt_two))
    pooled = (shifted * normal_cdf).astype(jnp.bfloat16)
    grad_act = cotangent.astype(jnp.float32) * (
        normal_cdf + shifted * jnp.exp(-0.5 * shifted * shifted) * inv_sqrt_tau
    )
    local_norm = jnp.stack([jnp.sum(grad_act * normed, axis=0), jnp.sum(grad_act, axis=0)])
    grad_scaled = grad_act * norm_gain
    grad_proj = (
        (
            grad_scaled
            - jnp.mean(grad_scaled, axis=-1, keepdims=True)
            - normed * jnp.mean(grad_scaled * normed, axis=-1, keepdims=True)
        )
        * inv_std
    ).astype(jnp.bfloat16)
    local_weight = jnp.dot(parent_in.T, grad_proj, preferred_element_type=jnp.float32)
    grad_weight, grad_norm = lax.psum((local_weight, local_norm), "pts")
    grad_parent_in = jnp.dot(grad_proj, w_pool.T, preferred_element_type=jnp.float32)
    grad_back = lax.all_to_all(
        grad_parent_in.reshape(devices, per_owner, width),
        "pts",
        split_axis=0,
        concat_axis=0,
        tiled=True,
    ).reshape(parents, width)
    placed = jnp.zeros((parents, width), jnp.float32).at[send_order].set(grad_back)
    grad_points = (
        placed[parent_ids] / child_total.astype(jnp.float32)[parent_ids][:, None]
    ).astype(jnp.bfloat16)
    return (pooled, grad_points, grad_weight, grad_norm)


def solution(mesh):
    in_specs = (
        P(("grp", "pts"), None),
        P(("grp", "pts")),
        P(("grp", "pts")),
        P(("grp", "pts"), None),
        P(("grp", "pts"), None),
        P(("grp", "pts"), None),
        P(),
        P(),
        P(),
        P(),
        P(),
        P(("grp", "pts"), None),
    )
    out_specs = (P(("grp", "pts"), None), P(("grp", "pts"), None), P("grp", None), P("grp", None))
    return jax.shard_map(local, mesh=mesh, in_specs=in_specs, out_specs=out_specs, check_vma=False)
```

profile of v0, /device:TPU:0, one launch (start us, length us, event | category | flops | bytes accessed | tf_op | source)
XLA Modules:
  0.0 654.7 jit_solution(3189090664272351027)
XLA Ops:
  37.0 39.5 %all-to-all-done.1 = bf16[16,2,32768]{2,1,0:T(2,128)(2,1)S(1)} async-done(((bf16[16,2,32768]{2,1,0:T(2,128)(2,1)}), bf16[16,2,32768]{2,1,0:T(2,128)(2,1)S(1)}, u32[]{:S(2)}, u32[]{:S(2)}) %all-to-all-start.1) | async-done | bytes 2097184 | tf_op jit(solution)/shard_map/all_to_all | solution.py:87
  86.4 309.0 %while.22 = (s32[]{:T(128)}, bf16[4,1024,256]{2,1,0:T(8,128)(2,1)}, bf16[4,1024,256]{2,1,0:T(8,128)(2,1)}, bf16[256,768]{1,0:T(8,128)(2,1)S(1)}, s32[4,1024]{1,0...) while((s32[]{:T(128)}, bf16[4,1024,256]{2,1,0:T(8,128)(2,1)}, ...), condition=%wide.region_14.15_spmd, body=%wide.region_9.14_spmd.sunk | while | flops 833094656 | bytes 43695340 | solution.py:111
  88.9 72.4 %while.23 = (s32[]{:T(128)}, bf16[4,1024,4,16]{1,3,2,0:T(8,128)(2,1)}, bf16[4,1024,4,16]{1,3,2,0:T(8,128)(2,1)S(1)}, bf16[4,1024,4,16]{1,3,2,0:T(8,128)(2,1)S(1)...) while((s32[]{:T(128)}, bf16[4,1024,4,16]{1,3,2,0:T(8,128)(2,1)}, ...), condition=%wide.region_13.13_spmd.clone, body=%wide.region_10.12_spmd.clone.sunk | while | flops 294650880 | bytes 36345932 | solution.py:48
  89.5 9.8 %fusion.109 = (f32[4,1024]{1,0:T(4,128)S(1)}, f32[4,1024,1024]{1,2,0:T(8,128)}) fusion(pred[1024,1024]{0,1:T(8,128)(4,1)S(1)} %broadcast_compare_fusion.2, bf16[4,1024,4,16]{1,3,2,0:T(8,128)(2,1)S(1)} %get-tuple-element.264, s32[]{:T(128)} %get-tuple-element.253, bf16[4,1024,4,16]{1,3,2,0:T(8,128)(2,1)S(1)} %get-tuple-element.263), kind=kOutput, calls=%fused_computation.110.clone.1 | convolution fusion | flops 150995968 | bytes 18105344 | tf_op jit(solution)/shard_map/while/body/eval_jaxpr/while/body/eval_jaxpr/sub | solution.py:42
  99.3 7.6 %fusion.110 = bf16[4,1024,4,16]{1,3,2,0:T(8,128)(2,1)} fusion(bf16[4,1024,4,16]{1,3,2,0:T(8,128)(2,1)} %get-tuple-element.254, s32[]{:T(128)} %get-tuple-element.253, f32[4,1024,1024]{1,2,0:T(8,128)} %get-tuple-element.244, f32[4,1024]{1,0:T(4,128)S(1)} %get-tuple-element.245, bf16[4,1024,4,16]{1,3,2,0:T(8,128)(2,1)S(1)} %get-tuple-element.262), kind=kOutput, calls=%fused_computation.24.clone.1 | convolution fusion | flops 142606336 | bytes 17187840 | tf_op jit(solution)/shard_map/while/body/eval_jaxpr/while/body/eval_jaxpr/hqk,khd->qhd/dot_general | solution.py:46
  107.6 9.8 %fusion.109 = (f32[4,1024]{1,0:T(4,128)S(1)}, f32[4,1024,1024]{1,2,0:T(8,128)}) fusion(pred[1024,1024]{0,1:T(8,128)(4,1)S(1)} %broadcast_compare_fusion.2, bf16[4,1024,4,16]{1,3,2,0:T(8,128)(2,1)S(1)} %get-tuple-element.264, s32[]{:T(128)} %get-tuple-element.253, bf16[4,1024,4,16]{1,3,2,0:T(8,128)(2,1)S(1)} %get-tuple-element.263), kind=kOutput, calls=%fused_computation.110.clone.1 | convolution fusion | flops 150995968 | bytes 18105344 | tf_op jit(solution)/shard_map/while/body/eval_jaxpr/while/body/eval_jaxpr/sub | solution.py:42
  117.4 7.6 %fusion.110 = bf16[4,1024,4,16]{1,3,2,0:T(8,128)(2,1)} fusion(bf16[4,1024,4,16]{1,3,2,0:T(8,128)(2,1)} %get-tuple-element.254, s32[]{:T(128)} %get-tuple-element.253, f32[4,1024,1024]{1,2,0:T(8,128)} %get-tuple-element.244, f32[4,1024]{1,0:T(4,128)S(1)} %get-tuple-element.245, bf16[4,1024,4,16]{1,3,2,0:T(8,128)(2,1)S(1)} %get-tuple-element.262), kind=kOutput, calls=%fused_computation.24.clone.1 | convolution fusion | flops 142606336 | bytes 17187840 | tf_op jit(solution)/shard_map/while/body/eval_jaxpr/while/body/eval_jaxpr/hqk,khd->qhd/dot_general | solution.py:46
  125.7 9.8 %fusion.109 = (f32[4,1024]{1,0:T(4,128)S(1)}, f32[4,1024,1024]{1,2,0:T(8,128)}) fusion(pred[1024,1024]{0,1:T(8,128)(4,1)S(1)} %broadcast_compare_fusion.2, bf16[4,1024,4,16]{1,3,2,0:T(8,128)(2,1)S(1)} %get-tuple-element.264, s32[]{:T(128)} %get-tuple-element.253, bf16[4,1024,4,16]{1,3,2,0:T(8,128)(2,1)S(1)} %get-tuple-element.263), kind=kOutput, calls=%fused_computation.110.clone.1 | convolution fusion | flops 150995968 | bytes 18105344 | tf_op jit(solution)/shard_map/while/body/eval_jaxpr/while/body/eval_jaxpr/sub | solution.py:42
  135.5 7.6 %fusion.110 = bf16[4,1024,4,16]{1,3,2,0:T(8,128)(2,1)} fusion(bf16[4,1024,4,16]{1,3,2,0:T(8,128)(2,1)} %get-tuple-element.254, s32[]{:T(128)} %get-tuple-element.253, f32[4,1024,1024]{1,2,0:T(8,128)} %get-tuple-element.244, f32[4,1024]{1,0:T(4,128)S(1)} %get-tuple-element.245, bf16[4,1024,4,16]{1,3,2,0:T(8,128)(2,1)S(1)} %get-tuple-element.262), kind=kOutput, calls=%fused_computation.24.clone.1 | convolution fusion | flops 142606336 | bytes 17187840 | tf_op jit(solution)/shard_map/while/body/eval_jaxpr/while/body/eval_jaxpr/hqk,khd->qhd/dot_general | solution.py:46
  143.8 9.8 %fusion.109 = (f32[4,1024]{1,0:T(4,128)S(1)}, f32[4,1024,1024]{1,2,0:T(8,128)}) fusion(pred[1024,1024]{0,1:T(8,128)(4,1)S(1)} %broadcast_compare_fusion.2, bf16[4,1024,4,16]{1,3,2,0:T(8,128)(2,1)S(1)} %get-tuple-element.264, s32[]{:T(128)} %get-tuple-element.253, bf16[4,1024,4,16]{1,3,2,0:T(8,128)(2,1)S(1)} %get-tuple-element.263), kind=kOutput, calls=%fused_computation.110.clone.1 | convolution fusion | flops 150995968 | bytes 18105344 | tf_op jit(solution)/shard_map/while/body/eval_jaxpr/while/body/eval_jaxpr/sub | solution.py:42
  153.6 7.6 %fusion.110 = bf16[4,1024,4,16]{1,3,2,0:T(8,128)(2,1)} fusion(bf16[4,1024,4,16]{1,3,2,0:T(8,128)(2,1)} %get-tuple-element.254, s32[]{:T(128)} %get-tuple-element.253, f32[4,1024,1024]{1,2,0:T(8,128)} %get-tuple-element.244, f32[4,1024]{1,0:T(4,128)S(1)} %get-tuple-element.245, bf16[4,1024,4,16]{1,3,2,0:T(8,128)(2,1)S(1)} %get-tuple-element.262), kind=kOutput, calls=%fused_computation.24.clone.1 | convolution fusion | flops 142606336 | bytes 17187840 | tf_op jit(solution)/shard_map/while/body/eval_jaxpr/while/body/eval_jaxpr/hqk,khd->qhd/dot_general | solution.py:46
  166.1 72.4 %while.23 = (s32[]{:T(128)}, bf16[4,1024,4,16]{1,3,2,0:T(8,128)(2,1)}, bf16[4,1024,4,16]{1,3,2,0:T(8,128)(2,1)S(1)}, bf16[4,1024,4,16]{1,3,2,0:T(8,128)(2,1)S(1)...) while((s32[]{:T(128)}, bf16[4,1024,4,16]{1,3,2,0:T(8,128)(2,1)}, ...), condition=%wide.region_13.13_spmd.clone, body=%wide.region_10.12_spmd.clone.sunk | while | flops 294650880 | bytes 36345932 | solution.py:48
  166.8 9.8 %fusion.109 = (f32[4,1024]{1,0:T(4,128)S(1)}, f32[4,1024,1024]{1,2,0:T(8,128)}) fusion(pred[1024,1024]{0,1:T(8,128)(4,1)S(1)} %broadcast_compare_fusion.2, bf16[4,1024,4,16]{1,3,2,0:T(8,128)(2,1)S(1)} %get-tuple-element.264, s32[]{:T(128)} %get-tuple-element.253, bf16[4,1024,4,16]{1,3,2,0:T(8,128)(2,1)S(1)} %get-tuple-element.263), kind=kOutput, calls=%fused_computation.110.clone.1 | convolution fusion | flops 150995968 | bytes 18105344 | tf_op jit(solution)/shard_map/while/body/eval_jaxpr/while/body/eval_jaxpr/sub | solution.py:42
  176.6 7.6 %fusion.110 = bf16[4,1024,4,16]{1,3,2,0:T(8,128)(2,1)} fusion(bf16[4,1024,4,16]{1,3,2,0:T(8,128)(2,1)} %get-tuple-element.254, s32[]{:T(128)} %get-tuple-element.253, f32[4,1024,1024]{1,2,0:T(8,128)} %get-tuple-element.244, f32[4,1024]{1,0:T(4,128)S(1)} %get-tuple-element.245, bf16[4,1024,4,16]{1,3,2,0:T(8,128)(2,1)S(1)} %get-tuple-element.262), kind=kOutput, calls=%fused_computation.24.clone.1 | convolution fusion | flops 142606336 | bytes 17187840 | tf_op jit(solution)/shard_map/while/body/eval_jaxpr/while/body/eval_jaxpr/hqk,khd->qhd/dot_general | solution.py:46
  184.9 9.8 %fusion.109 = (f32[4,1024]{1,0:T(4,128)S(1)}, f32[4,1024,1024]{1,2,0:T(8,128)}) fusion(pred[1024,1024]{0,1:T(8,128)(4,1)S(1)} %broadcast_compare_fusion.2, bf16[4,1024,4,16]{1,3,2,0:T(8,128)(2,1)S(1)} %get-tuple-element.264, s32[]{:T(128)} %get-tuple-element.253, bf16[4,1024,4,16]{1,3,2,0:T(8,128)(2,1)S(1)} %get-tuple-element.263), kind=kOutput, calls=%fused_computation.110.clone.1 | convolution fusion | flops 150995968 | bytes 18105344 | tf_op jit(solution)/shard_map/while/body/eval_jaxpr/while/body/eval_jaxpr/sub | solution.py:42
  194.7 7.6 %fusion.110 = bf16[4,1024,4,16]{1,3,2,0:T(8,128)(2,1)} fusion(bf16[4,1024,4,16]{1,3,2,0:T(8,128)(2,1)} %get-tuple-element.254, s32[]{:T(128)} %get-tuple-element.253, f32[4,1024,1024]{1,2,0:T(8,128)} %get-tuple-element.244, f32[4,1024]{1,0:T(4,128)S(1)} %get-tuple-element.245, bf16[4,1024,4,16]{1,3,2,0:T(8,128)(2,1)S(1)} %get-tuple-element.262), kind=kOutput, calls=%fused_computation.24.clone.1 | convolution fusion | flops 142606336 | bytes 17187840 | tf_op jit(solution)/shard_map/while/body/eval_jaxpr/while/body/eval_jaxpr/hqk,khd->qhd/dot_general | solution.py:46
  203.0 9.8 %fusion.109 = (f32[4,1024]{1,0:T(4,128)S(1)}, f32[4,1024,1024]{1,2,0:T(8,128)}) fusion(pred[1024,1024]{0,1:T(8,128)(4,1)S(1)} %broadcast_compare_fusion.2, bf16[4,1024,4,16]{1,3,2,0:T(8,128)(2,1)S(1)} %get-tuple-element.264, s32[]{:T(128)} %get-tuple-element.253, bf16[4,1024,4,16]{1,3,2,0:T(8,128)(2,1)S(1)} %get-tuple-element.263), kind=kOutput, calls=%fused_computation.110.clone.1 | convolution fusion | flops 150995968 | bytes 18105344 | tf_op jit(solution)/shard_map/while/body/eval_jaxpr/while/body/eval_jaxpr/sub | solution.py:42
  212.8 7.6 %fusion.110 = bf16[4,1024,4,16]{1,3,2,0:T(8,128)(2,1)} fusion(bf16[4,1024,4,16]{1,3,2,0:T(8,128)(2,1)} %get-tuple-element.254, s32[]{:T(128)} %get-tuple-element.253, f32[4,1024,1024]{1,2,0:T(8,128)} %get-tuple-element.244, f32[4,1024]{1,0:T(4,128)S(1)} %get-tuple-element.245, bf16[4,1024,4,16]{1,3,2,0:T(8,128)(2,1)S(1)} %get-tuple-element.262), kind=kOutput, calls=%fused_computation.24.clone.1 | convolution fusion | flops 142606336 | bytes 17187840 | tf_op jit(solution)/shard_map/while/body/eval_jaxpr/while/body/eval_jaxpr/hqk,khd->qhd/dot_general | solution.py:46
  221.1 9.8 %fusion.109 = (f32[4,1024]{1,0:T(4,128)S(1)}, f32[4,1024,1024]{1,2,0:T(8,128)}) fusion(pred[1024,1024]{0,1:T(8,128)(4,1)S(1)} %broadcast_compare_fusion.2, bf16[4,1024,4,16]{1,3,2,0:T(8,128)(2,1)S(1)} %get-tuple-element.264, s32[]{:T(128)} %get-tuple-element.253, bf16[4,1024,4,16]{1,3,2,0:T(8,128)(2,1)S(1)} %get-tuple-element.263), kind=kOutput, calls=%fused_computation.110.clone.1 | convolution fusion | flops 150995968 | bytes 18105344 | tf_op jit(solution)/shard_map/while/body/eval_jaxpr/while/body/eval_jaxpr/sub | solution.py:42
  230.9 7.6 %fusion.110 = bf16[4,1024,4,16]{1,3,2,0:T(8,128)(2,1)} fusion(bf16[4,1024,4,16]{1,3,2,0:T(8,128)(2,1)} %get-tuple-element.254, s32[]{:T(128)} %get-tuple-element.253, f32[4,1024,1024]{1,2,0:T(8,128)} %get-tuple-element.244, f32[4,1024]{1,0:T(4,128)S(1)} %get-tuple-element.245, bf16[4,1024,4,16]{1,3,2,0:T(8,128)(2,1)S(1)} %get-tuple-element.262), kind=kOutput, calls=%fused_computation.24.clone.1 | convolution fusion | flops 142606336 | bytes 17187840 | tf_op jit(solution)/shard_map/while/body/eval_jaxpr/while/body/eval_jaxpr/hqk,khd->qhd/dot_general | solution.py:46
  243.4 72.4 %while.23 = (s32[]{:T(128)}, bf16[4,1024,4,16]{1,3,2,0:T(8,128)(2,1)}, bf16[4,1024,4,16]{1,3,2,0:T(8,128)(2,1)S(1)}, bf16[4,1024,4,16]{1,3,2,0:T(8,128)(2,1)S(1)...) while((s32[]{:T(128)}, bf16[4,1024,4,16]{1,3,2,0:T(8,128)(2,1)}, ...), condition=%wide.region_13.13_spmd.clone, body=%wide.region_10.12_spmd.clone.sunk | while | flops 294650880 | bytes 36345932 | solution.py:48
  244.0 9.8 %fusion.109 = (f32[4,1024]{1,0:T(4,128)S(1)}, f32[4,1024,1024]{1,2,0:T(8,128)}) fusion(pred[1024,1024]{0,1:T(8,128)(4,1)S(1)} %broadcast_compare_fusion.2, bf16[4,1024,4,16]{1,3,2,0:T(8,128)(2,1)S(1)} %get-tuple-element.264, s32[]{:T(128)} %get-tuple-element.253, bf16[4,1024,4,16]{1,3,2,0:T(8,128)(2,1)S(1)} %get-tuple-element.263), kind=kOutput, calls=%fused_computation.110.clone.1 | convolution fusion | flops 150995968 | bytes 18105344 | tf_op jit(solution)/shard_map/while/body/eval_jaxpr/while/body/eval_jaxpr/sub | solution.py:42
  253.8 7.6 %fusion.110 = bf16[4,1024,4,16]{1,3,2,0:T(8,128)(2,1)} fusion(bf16[4,1024,4,16]{1,3,2,0:T(8,128)(2,1)} %get-tuple-element.254, s32[]{:T(128)} %get-tuple-element.253, f32[4,1024,1024]{1,2,0:T(8,128)} %get-tuple-element.244, f32[4,1024]{1,0:T(4,128)S(1)} %get-tuple-element.245, bf16[4,1024,4,16]{1,3,2,0:T(8,128)(2,1)S(1)} %get-tuple-element.262), kind=kOutput, calls=%fused_computation.24.clone.1 | convolution fusion | flops 142606336 | bytes 17187840 | tf_op jit(solution)/shard_map/while/body/eval_jaxpr/while/body/eval_jaxpr/hqk,khd->qhd/dot_general | solution.py:46
  262.1 9.8 %fusion.109 = (f32[4,1024]{1,0:T(4,128)S(1)}, f32[4,1024,1024]{1,2,0:T(8,128)}) fusion(pred[1024,1024]{0,1:T(8,128)(4,1)S(1)} %broadcast_compare_fusion.2, bf16[4,1024,4,16]{1,3,2,0:T(8,128)(2,1)S(1)} %get-tuple-element.264, s32[]{:T(128)} %get-tuple-element.253, bf16[4,1024,4,16]{1,3,2,0:T(8,128)(2,1)S(1)} %get-tuple-element.263), kind=kOutput, calls=%fused_computation.110.clone.1 | convolution fusion | flops 150995968 | bytes 18105344 | tf_op jit(solution)/shard_map/while/body/eval_jaxpr/while/body/eval_jaxpr/sub | solution.py:42
  271.9 7.6 %fusion.110 = bf16[4,1024,4,16]{1,3,2,0:T(8,128)(2,1)} fusion(bf16[4,1024,4,16]{1,3,2,0:T(8,128)(2,1)} %get-tuple-element.254, s32[]{:T(128)} %get-tuple-element.253, f32[4,1024,1024]{1,2,0:T(8,128)} %get-tuple-element.244, f32[4,1024]{1,0:T(4,128)S(1)} %get-tuple-element.245, bf16[4,1024,4,16]{1,3,2,0:T(8,128)(2,1)S(1)} %get-tuple-element.262), kind=kOutput, calls=%fused_computation.24.clone.1 | convolution fusion | flops 142606336 | bytes 17187840 | tf_op jit(solution)/shard_map/while/body/eval_jaxpr/while/body/eval_jaxpr/hqk,khd->qhd/dot_general | solution.py:46
  280.2 9.8 %fusion.109 = (f32[4,1024]{1,0:T(4,128)S(1)}, f32[4,1024,1024]{1,2,0:T(8,128)}) fusion(pred[1024,1024]{0,1:T(8,128)(4,1)S(1)} %broadcast_compare_fusion.2, bf16[4,1024,4,16]{1,3,2,0:T(8,128)(2,1)S(1)} %get-tuple-element.264, s32[]{:T(128)} %get-tuple-element.253, bf16[4,1024,4,16]{1,3,2,0:T(8,128)(2,1)S(1)} %get-tuple-element.263), kind=kOutput, calls=%fused_computation.110.clone.1 | convolution fusion | flops 150995968 | bytes 18105344 | tf_op jit(solution)/shard_map/while/body/eval_jaxpr/while/body/eval_jaxpr/sub | solution.py:42
  290.0 7.6 %fusion.110 = bf16[4,1024,4,16]{1,3,2,0:T(8,128)(2,1)} fusion(bf16[4,1024,4,16]{1,3,2,0:T(8,128)(2,1)} %get-tuple-element.254, s32[]{:T(128)} %get-tuple-element.253, f32[4,1024,1024]{1,2,0:T(8,128)} %get-tuple-element.244, f32[4,1024]{1,0:T(4,128)S(1)} %get-tuple-element.245, bf16[4,1024,4,16]{1,3,2,0:T(8,128)(2,1)S(1)} %get-tuple-element.262), kind=kOutput, calls=%fused_computation.24.clone.1 | convolution fusion | flops 142606336 | bytes 17187840 | tf_op jit(solution)/shard_map/while/body/eval_jaxpr/while/body/eval_jaxpr/hqk,khd->qhd/dot_general | solution.py:46
  298.3 9.8 %fusion.109 = (f32[4,1024]{1,0:T(4,128)S(1)}, f32[4,1024,1024]{1,2,0:T(8,128)}) fusion(pred[1024,1024]{0,1:T(8,128)(4,1)S(1)} %broadcast_compare_fusion.2, bf16[4,1024,4,16]{1,3,2,0:T(8,128)(2,1)S(1)} %get-tuple-element.264, s32[]{:T(128)} %get-tuple-element.253, bf16[4,1024,4,16]{1,3,2,0:T(8,128)(2,1)S(1)} %get-tuple-element.263), kind=kOutput, calls=%fused_computation.110.clone.1 | convolution fusion | flops 150995968 | bytes 18105344 | tf_op jit(solution)/shard_map/while/body/eval_jaxpr/while/body/eval_jaxpr/sub | solution.py:42
  308.1 7.6 %fusion.110 = bf16[4,1024,4,16]{1,3,2,0:T(8,128)(2,1)} fusion(bf16[4,1024,4,16]{1,3,2,0:T(8,128)(2,1)} %get-tuple-element.254, s32[]{:T(128)} %get-tuple-element.253, f32[4,1024,1024]{1,2,0:T(8,128)} %get-tuple-element.244, f32[4,1024]{1,0:T(4,128)S(1)} %get-tuple-element.245, bf16[4,1024,4,16]{1,3,2,0:T(8,128)(2,1)S(1)} %get-tuple-element.262), kind=kOutput, calls=%fused_computation.24.clone.1 | convolution fusion | flops 142606336 | bytes 17187840 | tf_op jit(solution)/shard_map/while/body/eval_jaxpr/while/body/eval_jaxpr/hqk,khd->qhd/dot_general | solution.py:46
  320.6 72.4 %while.23 = (s32[]{:T(128)}, bf16[4,1024,4,16]{1,3,2,0:T(8,128)(2,1)}, bf16[4,1024,4,16]{1,3,2,0:T(8,128)(2,1)S(1)}, bf16[4,1024,4,16]{1,3,2,0:T(8,128)(2,1)S(1)...) while((s32[]{:T(128)}, bf16[4,1024,4,16]{1,3,2,0:T(8,128)(2,1)}, ...), condition=%wide.region_13.13_spmd.clone, body=%wide.region_10.12_spmd.clone.sunk | while | flops 294650880 | bytes 36345932 | solution.py:48
  321.3 9.8 %fusion.109 = (f32[4,1024]{1,0:T(4,128)S(1)}, f32[4,1024,1024]{1,2,0:T(8,128)}) fusion(pred[1024,1024]{0,1:T(8,128)(4,1)S(1)} %broadcast_compare_fusion.2, bf16[4,1024,4,16]{1,3,2,0:T(8,128)(2,1)S(1)} %get-tuple-element.264, s32[]{:T(128)} %get-tuple-element.253, bf16[4,1024,4,16]{1,3,2,0:T(8,128)(2,1)S(1)} %get-tuple-element.263), kind=kOutput, calls=%fused_computation.110.clone.1 | convolution fusion | flops 150995968 | bytes 18105344 | tf_op jit(solution)/shard_map/while/body/eval_jaxpr/while/body/eval_jaxpr/sub | solution.py:42
  331.1 7.6 %fusion.110 = bf16[4,1024,4,16]{1,3,2,0:T(8,128)(2,1)} fusion(bf16[4,1024,4,16]{1,3,2,0:T(8,128)(2,1)} %get-tuple-element.254, s32[]{:T(128)} %get-tuple-element.253, f32[4,1024,1024]{1,2,0:T(8,128)} %get-tuple-element.244, f32[4,1024]{1,0:T(4,128)S(1)} %get-tuple-element.245, bf16[4,1024,4,16]{1,3,2,0:T(8,128)(2,1)S(1)} %get-tuple-element.262), kind=kOutput, calls=%fused_computation.24.clone.1 | convolution fusion | flops 142606336 | bytes 17187840 | tf_op jit(solution)/shard_map/while/body/eval_jaxpr/while/body/eval_jaxpr/hqk,khd->qhd/dot_general | solution.py:46
  339.4 9.8 %fusion.109 = (f32[4,1024]{1,0:T(4,128)S(1)}, f32[4,1024,1024]{1,2,0:T(8,128)}) fusion(pred[1024,1024]{0,1:T(8,128)(4,1)S(1)} %broadcast_compare_fusion.2, bf16[4,1024,4,16]{1,3,2,0:T(8,128)(2,1)S(1)} %get-tuple-element.264, s32[]{:T(128)} %get-tuple-element.253, bf16[4,1024,4,16]{1,3,2,0:T(8,128)(2,1)S(1)} %get-tuple-element.263), kind=kOutput, calls=%fused_computation.110.clone.1 | convolution fusion | flops 150995968 | bytes 18105344 | tf_op jit(solution)/shard_map/while/body/eval_jaxpr/while/body/eval_jaxpr/sub | solution.py:42
  349.2 7.6 %fusion.110 = bf16[4,1024,4,16]{1,3,2,0:T(8,128)(2,1)} fusion(bf16[4,1024,4,16]{1,3,2,0:T(8,128)(2,1)} %get-tuple-element.254, s32[]{:T(128)} %get-tuple-element.253, f32[4,1024,1024]{1,2,0:T(8,128)} %get-tuple-element.244, f32[4,1024]{1,0:T(4,128)S(1)} %get-tuple-element.245, bf16[4,1024,4,16]{1,3,2,0:T(8,128)(2,1)S(1)} %get-tuple-element.262), kind=kOutput, calls=%fused_computation.24.clone.1 | convolution fusion | flops 142606336 | bytes 17187840 | tf_op jit(solution)/shard_map/while/body/eval_jaxpr/while/body/eval_jaxpr/hqk,khd->qhd/dot_general | solution.py:46
  357.5 9.8 %fusion.109 = (f32[4,1024]{1,0:T(4,128)S(1)}, f32[4,1024,1024]{1,2,0:T(8,128)}) fusion(pred[1024,1024]{0,1:T(8,128)(4,1)S(1)} %broadcast_compare_fusion.2, bf16[4,1024,4,16]{1,3,2,0:T(8,128)(2,1)S(1)} %get-tuple-element.264, s32[]{:T(128)} %get-tuple-element.253, bf16[4,1024,4,16]{1,3,2,0:T(8,128)(2,1)S(1)} %get-tuple-element.263), kind=kOutput, calls=%fused_computation.110.clone.1 | convolution fusion | flops 150995968 | bytes 18105344 | tf_op jit(solution)/shard_map/while/body/eval_jaxpr/while/body/eval_jaxpr/sub | solution.py:42
  367.3 7.6 %fusion.110 = bf16[4,1024,4,16]{1,3,2,0:T(8,128)(2,1)} fusion(bf16[4,1024,4,16]{1,3,2,0:T(8,128)(2,1)} %get-tuple-element.254, s32[]{:T(128)} %get-tuple-element.253, f32[4,1024,1024]{1,2,0:T(8,128)} %get-tuple-element.244, f32[4,1024]{1,0:T(4,128)S(1)} %get-tuple-element.245, bf16[4,1024,4,16]{1,3,2,0:T(8,128)(2,1)S(1)} %get-tuple-element.262), kind=kOutput, calls=%fused_computation.24.clone.1 | convolution fusion | flops 142606336 | bytes 17187840 | tf_op jit(solution)/shard_map/while/body/eval_jaxpr/while/body/eval_jaxpr/hqk,khd->qhd/dot_general | solution.py:46
  375.6 9.8 %fusion.109 = (f32[4,1024]{1,0:T(4,128)S(1)}, f32[4,1024,1024]{1,2,0:T(8,128)}) fusion(pred[1024,1024]{0,1:T(8,128)(4,1)S(1)} %broadcast_compare_fusion.2, bf16[4,1024,4,16]{1,3,2,0:T(8,128)(2,1)S(1)} %get-tuple-element.264, s32[]{:T(128)} %get-tuple-element.253, bf16[4,1024,4,16]{1,3,2,0:T(8,128)(2,1)S(1)} %get-tuple-element.263), kind=kOutput, calls=%fused_computation.110.clone.1 | convolution fusion | flops 150995968 | bytes 18105344 | tf_op jit(solution)/shard_map/while/body/eval_jaxpr/while/body/eval_jaxpr/sub | solution.py:42
  385.4 7.6 %fusion.110 = bf16[4,1024,4,16]{1,3,2,0:T(8,128)(2,1)} fusion(bf16[4,1024,4,16]{1,3,2,0:T(8,128)(2,1)} %get-tuple-element.254, s32[]{:T(128)} %get-tuple-element.253, f32[4,1024,1024]{1,2,0:T(8,128)} %get-tuple-element.244, f32[4,1024]{1,0:T(4,128)S(1)} %get-tuple-element.245, bf16[4,1024,4,16]{1,3,2,0:T(8,128)(2,1)S(1)} %get-tuple-element.262), kind=kOutput, calls=%fused_computation.24.clone.1 | convolution fusion | flops 142606336 | bytes 17187840 | tf_op jit(solution)/shard_map/while/body/eval_jaxpr/while/body/eval_jaxpr/hqk,khd->qhd/dot_general | solution.py:46
  407.9 11.4 %all-to-all-start.2 = ((bf16[16,2,32768]{2,1,0:T(2,128)(2,1)}), bf16[16,2,32768]{2,1,0:T(2,128)(2,1)}, u32[]{:S(2)}, u32[]{:S(2)}) async-start(bf16[16,2,32768]{2,1,0:T(2,128)(2,1)} %broadcast_select_fusion), calls=%async_computation.2 | async-start | bytes 4194304 | tf_op jit(solution)/shard_map/all_to_all | solution.py:114
  419.9 7.8 %scatter_custom_fusion = s32[4096]{0:T(1024)S(1)} fusion(s32[1024]{0:T(1024)S(1)} %bitcast.142, s32[1024]{0:T(1024)S(1)} %broadcast.251, s32[]{:T(128)} %constant.39.clone.1), kind=kCustom, calls=%fused_computation.86 | custom fusion | flops 1024 | bytes 16388 | tf_op jit(solution)/shard_map/scatter-add | solution.py:17
  428.4 32.0 %all-to-all-done.2 = bf16[16,2,32768]{2,1,0:T(2,128)(2,1)} async-done(((bf16[16,2,32768]{2,1,0:T(2,128)(2,1)}), bf16[16,2,32768]{2,1,0:T(2,128)(2,1)}, u32[]{:S(2)}, u32[]{:S(2)}) %all-to-all-start.2) | async-done | bytes 2097184 | tf_op jit(solution)/shard_map/all_to_all | solution.py:114
  470.9 24.7 %scatter_custom_fusion.4 = f32[1024,256]{1,0:T(8,128)S(1)} fusion(s32[4096]{0:T(1024)S(1)} %bitcast.132, f32[4096,256]{1,0:T(8,128)} %reshape.368, f32[]{:T(128)} %constant.29.clone.1), kind=kCustom, calls=%fused_computation.74 | custom fusion | flops 1048576 | bytes 1049088 | tf_op jit(solution)/shard_map/scatter-add | solution.py:121
  500.8 11.2 %all-to-all-start.3 = ((bf16[16,64,256]{2,1,0:T(8,128)(2,1)}), bf16[16,64,256]{2,1,0:T(8,128)(2,1)S(1)}, u32[]{:S(2)}, u32[]{:S(2)}) async-start(bf16[16,64,256]{2,1,0:T(8,128)(2,1)} %bitcast.23), calls=%async_computation.3 | async-start | bytes 1048576 | tf_op jit(solution)/shard_map/all_to_all | solution.py:126
  512.6 13.9 %all-to-all-done.3 = bf16[16,64,256]{2,1,0:T(8,128)(2,1)S(1)} async-done(((bf16[16,64,256]{2,1,0:T(8,128)(2,1)}), bf16[16,64,256]{2,1,0:T(8,128)(2,1)S(1)}, u32[]{:S(2)}, u32[]{:S(2)}) %all-to-all-start.3) | async-done | bytes 524320 | tf_op jit(solution)/shard_map/all_to_all | solution.py:126
  536.5 16.7 %gather_fusion.4 = f32[4096]{0:T(1024)S(1)} fusion(f32[1024]{0:T(1024)S(1)} %bitcast.124, s32[4096]{0:T(1024)S(1)} %broadcast_clamp_fusion), kind=kCustom, calls=%fused_computation.4 | custom fusion | bytes 49152 | tf_op jit(solution)/shard_map/gather | solution.py:162
  555.8 34.6 %psum.15 = f32[2,512]{1,0:T(2,128)} all-reduce(f32[2,512]{1,0:T(2,128)S(1)} %pad_maximum_fusion), channel_id=1, replica_groups=mesh['grp'=2,'pts'=16] {'pts'}, use_global_device_ids=true, to_apply=%region_24.25 | all-reduce | flops 1024 | bytes 8192 | tf_op jit(solution)/shard_map/psum | solution.py:151
  596.0 16.1 %gather_fusion.3 = f32[4096,256]{1,0:T(8,128)} fusion(f32[1024,256]{1,0:T(8,128)S(1)} %scatter_custom_fusion.5, s32[4096]{0:T(1024)S(1)} %broadcast_clamp_fusion), kind=kCustom, calls=%fused_computation.3 | custom fusion | bytes 8404992 | tf_op jit(solution)/shard_map/gather | solution.py:162
  615.6 30.4 %all-reduce.2.cloned.1.call-done = f32[256,512]{1,0:T(8,128)} async-done(((f32[256,512]{1,0:T(8,128)}), f32[256,512]{1,0:T(8,128)}) %all-reduce.2.cloned.1.call-update) | async-done | bytes 524304 | tf_op jit(solution)/shard_map/psum | solution.py:151
  (127 shorter events, 122.9 us)
Async XLA Ops:
  7.2 519.3 %copy-start = (bf16[256,512]{1,0:T(8,128)(2,1)S(1)}, bf16[256,512]{1,0:T(8,128)(2,1)}, u32[]{:S(2)}) copy-start(bf16[256,512]{1,0:T(8,128)(2,1)} %param.24) | copy-start | bytes 786436
  8.8 13.1 %copy-start.8 = (s32[32]{0:T(128)}, s32[32]{0:T(128)S(1)}, u32[]{:S(2)}) copy-start(s32[32]{0:T(128)S(1)} %get-tuple-element.145) | copy-start | bytes 388
  10.2 19.2 %all-to-all-start = ((bf16[16,2,1]{1,2,0:T(2,128)(2,1)}), bf16[16,2,1]{1,2,0:T(2,128)(2,1)S(1)}, u32[]{:S(2)}, u32[]{:S(2)}) async-start(bf16[16,2,1]{1,2,0:T(2,128)(2,1)} %all_to_all.35), calls=%async_computation | async-start | bytes 16384 | tf_op jit(solution)/shard_map/all_to_all | solution.py:88
  29.4 47.1 %all-to-all-start.1 = ((bf16[16,2,32768]{2,1,0:T(2,128)(2,1)}), bf16[16,2,32768]{2,1,0:T(2,128)(2,1)S(1)}, u32[]{:S(2)}, u32[]{:S(2)}) async-start(bf16[16,2,32768]{2,1,0:T(2,128)(2,1)} %all_to_all.28), calls=%async_computation.1 | async-start | bytes 4194304 | tf_op jit(solution)/shard_map/all_to_all | solution.py:87
  83.9 2.4 copy-start.1
  84.0 2.4 copy-start.10
  401.6 3.2 copy-start.5
  407.9 11.4 %copy-start.3 = (s32[1,1024]{1,0:T(1,128)S(1)}, s32[1,1024]{1,0:T(1,128)}, u32[]{:S(2)}) copy-start(s32[1,1024]{1,0:T(1,128)} %param.20) | copy-start | bytes 12292
  407.9 20.3 %copy-start.9 = (s32[32]{0:T(128)S(1)}, s32[32]{0:T(128)}, u32[]{:S(2)}) copy-start(s32[32]{0:T(128)} %copy-done.8) | copy-start | bytes 388
  407.9 20.4 %copy-start.6 = (s32[1,1024]{1,0:T(1,128)S(1)}, s32[1,1024]{1,0:T(1,128)}, u32[]{:S(2)}) copy-start(s32[1,1024]{1,0:T(1,128)} %param.21) | copy-start | bytes 12292
  407.9 52.6 %all-to-all-start.2 = ((bf16[16,2,32768]{2,1,0:T(2,128)(2,1)}), bf16[16,2,32768]{2,1,0:T(2,128)(2,1)}, u32[]{:S(2)}, u32[]{:S(2)}) async-start(bf16[16,2,32768]{2,1,0:T(2,128)(2,1)} %broadcast_select_fusion), calls=%async_computation.2 | async-start | bytes 4194304 | tf_op jit(solution)/shard_map/all_to_all | solution.py:114
  495.8 16.2 %copy-start.2 = (bf16[1024,512]{1,0:T(8,128)(2,1)S(1)}, bf16[1024,512]{1,0:T(8,128)(2,1)}, u32[]{:S(2)}) copy-start(bf16[1024,512]{1,0:T(8,128)(2,1)} %param.27) | copy-start | bytes 3145732
  500.8 25.7 %all-to-all-start.3 = ((bf16[16,64,256]{2,1,0:T(8,128)(2,1)}), bf16[16,64,256]{2,1,0:T(8,128)(2,1)S(1)}, u32[]{:S(2)}, u32[]{:S(2)}) async-start(bf16[16,64,256]{2,1,0:T(8,128)(2,1)} %bitcast.23), calls=%async_computation.3 | async-start | bytes 1048576 | tf_op jit(solution)/shard_map/all_to_all | solution.py:126
  526.5 0.8 copy-start.4
  526.5 0.8 copy-start.7
  532.0 58.4 %all-to-all-start.4 = ((f32[16,64,256]{2,1,0:T(8,128)}), f32[16,64,256]{2,1,0:T(8,128)}, u32[]{:S(2)}, u32[]{:S(2)}) async-start(f32[16,64,256]{2,1,0:T(8,128)} %bitcast.25), calls=%async_computation.4 | async-start | bytes 2097152 | tf_op jit(solution)/shard_map/all_to_all | solution.py:153
  536.4 109.6 %all-reduce.2.cloned.1.call-start = ((), (), s32[]{:S(2)}) async-start(), calls=%async_computation.5 | async-start | bytes 1048576 | tf_op jit(solution)/shard_map/psum | solution.py:151
Sparse Core Ops, SparseCore 0:
  554.6 91.3 all-reduce.1
where the time goes:
time: 657 us; the launch traced here: 655 us
  matrix products  298 us (45%)
  waiting for transfers between devices  116 us (18%)
  local copies, waits for them, and re-layouts  94.7 us (14%)
  other arithmetic  56.3 us (9%)
  starting transfers between devices  40.4 us (6%)
  blocking collectives  34.6 us (5%)
  between operations  14.4 us (2%)
    sub x16, matrix products, one_group(): weights_exp = jnp.exp(scores - row_max)  157 us
    dot_general x16, matrix products, one_group(): jnp.einsum('hqk,khd->qhd', probability, value_g, preferred_element_type=j...  122 us
    all_to_all x1, waiting for transfers between devices, local(): lax.all_to_all(payload, 'pts', split_axis=0, concat_axis=0, tiled=True)  39.5 us
    psum x1, blocking collectives, local(): grad_weight, grad_norm = lax.psum((local_weight, local_norm), 'pts')  34.6 us
    all_to_all x1, waiting for transfers between devices, local(): lax.all_to_all(outgoing, 'pts', split_axis=0, concat_axis=0, tiled=True)  32 us
    psum x1, waiting for transfers between devices, local(): grad_weight, grad_norm = lax.psum((local_weight, local_norm), 'pts')  30.4 us
    scatter-add x1, other arithmetic, local(): jax.ops.segment_sum(home_rows.astype(jnp.float32), parent_ids, num_segmen...  24.7 us
    gather x1, local copies, waits for them, and re-layouts, local(): child_total.astype(jnp.float32)[parent_ids][:, None]  16.7 us
  transfers between devices with their start and end apart: 6, of which 4 were waited for; matrix products, arithmetic and copies ran while one was open for 10% of the time, Pallas kernels for 0%

commit v1 on v0

v1 whole, which is shorter than its diff:
```python
import functools
import math

import jax
import jax.numpy as jnp
from jax import lax
from jax.experimental import pallas as pl
from jax.experimental.pallas import tpu as pltpu
from jax.sharding import PartitionSpec as P

HDIM = 16
HEAD_GROUP = 8
ROWS = 128
WINDOW = 256
PATCHES = 4
FAR = 2.0**100
SCORE_SCALE = HDIM**-0.5 * math.log2(math.e)
SCORE_SAFE = 98.0

inv_sqrt_two = 0.7071067811865476
inv_sqrt_tau = 0.3989422804014327
norm_eps = 1e-05

BF = jnp.bfloat16
F32 = jnp.float32
NT = (((1,), (1,)), ((), ()))
TN = (((0,), (0,)), ((), ()))
VMEM = pl.BlockSpec(memory_space=pltpu.VMEM)
SMEM = pl.BlockSpec(memory_space=pltpu.SMEM)
ANY = pl.BlockSpec(memory_space=pl.ANY)
ROOM = pltpu.CompilerParams(vmem_limit_bytes=48 << 20)


def iota(shape, dim):
    return lax.broadcasted_iota(jnp.int32, shape, dim)


def mm(a, b, dims=(((1,), (0,)), ((), ()))):
    return lax.dot_general(a, b, dims, preferred_element_type=F32)


def cost(flops, bytes_accessed, transcendentals=0):
    return pl.CostEstimate(
        flops=int(flops), bytes_accessed=int(bytes_accessed), transcendentals=int(transcendentals)
    )


def pack_kernel(capacity, dest_ref, points_ref, payload_ref, place_ref, used, sem):
    blocks = dest_ref.shape[0]

    def clear(d, _):
        used[d] = 0
        return 0

    lax.fori_loop(0, used.shape[0], clear, 0)

    def send(b, _):
        d = dest_ref[b]
        place = d * capacity + used[d]
        used[d] = used[d] + 1
        place_ref[b] = place
        pltpu.make_async_copy(
            points_ref.at[pl.ds(pl.multiple_of(b * ROWS, ROWS), ROWS)],
            payload_ref.at[pl.ds(pl.multiple_of(place * ROWS, ROWS), ROWS)],
            sem,
        ).start()
        return 0

    lax.fori_loop(0, blocks, send, 0)
    whole = pl.ds(0, blocks * ROWS)
    pltpu.make_async_copy(points_ref.at[whole], payload_ref.at[whole], sem).wait()


def pack_blocks(hil_dest, points, devices, capacity):
    return pl.pallas_call(
        functools.partial(pack_kernel, capacity),
        out_shape=(
            jax.ShapeDtypeStruct((devices * capacity * ROWS, points.shape[1]), BF),
            jax.ShapeDtypeStruct(hil_dest.shape, jnp.int32),
        ),
        in_specs=[SMEM, ANY],
        out_specs=(ANY, SMEM),
        scratch_shapes=[pltpu.SMEM((devices,), jnp.int32), pltpu.SemaphoreType.DMA],
        compiler_params=ROOM,
        cost_estimate=cost(0, 4 * points.size),
    )(hil_dest, points)


def attend_kernel(
    group, index_ref, low_ref, count_ref, ids_ref, w_ref, rows_ref, out_ref, x, qx, kx, vx, sems
):
    tiles, span = ids_ref.shape
    width = w_ref.shape[0]
    cols = HEAD_GROUP * HDIM
    per_tile = span // ROWS

    for t in range(tiles):
        for b in range(per_tile):
            s = t * per_tile + b
            pltpu.make_async_copy(
                rows_ref.at[pl.ds(pl.multiple_of(index_ref[s] * ROWS, ROWS), ROWS)],
                x.at[pl.ds(s * ROWS, ROWS)],
                sems.at[t],
            ).start()

    lane = iota((ROWS, 2 * cols), 1)
    of_head = [(lane // HDIM == h) | (lane >= cols) for h in range(HEAD_GROUP)]
    lane_out = iota((ROWS, 2 * cols), 1) % cols // HDIM
    vx[:, cols:] = jnp.ones((span, cols), BF)
    r_i = iota((cols, cols), 0)
    c_i = iota((cols, cols), 1)
    far = jnp.where((r_i != c_i) & (c_i < PATCHES), -FAR, 0.0).astype(BF)
    first = group * cols

    def tile(t, _):
        at = pl.ds(pl.multiple_of(t * span, span), span)
        pltpu.make_async_copy(rows_ref.at[pl.ds(0, span)], x.at[at], sems.at[t]).wait()
        tile_rows = x[at, :]
        same = ids_ref[pl.ds(t, 1), :] == iota((cols, span), 0)
        patch_hot = jnp.where(same, 1.0, 0.0).astype(BF)
        query = mm(tile_rows, w_ref[:, first : first + cols])
        keys = mm(
            w_ref[:, width + first : width + first + cols], tile_rows, (((0,), (1,)), ((), ()))
        )
        qx[:, :cols] = query.astype(BF)
        qx[:, cols:] = mm(patch_hot, far, TN).astype(BF)
        kx[:cols, :] = keys.astype(BF)
        kx[cols:, :] = patch_hot
        vx[:, :cols] = mm(tile_rows, w_ref[:, 2 * width + first : 2 * width + first + cols]).astype(BF)
        query_most = jnp.max(jnp.abs(query), axis=0, keepdims=True)
        key_most = jnp.max(jnp.abs(keys), axis=1, keepdims=True)
        by_head = jnp.where(iota((8, cols), 1) // HDIM == iota((8, cols), 0), query_most, 0.0)
        bound = jnp.max(mm(by_head.astype(BF), jnp.broadcast_to(key_most, (cols, cols)).astype(BF)))
        safe = bound * SCORE_SCALE < SCORE_SAFE

        def block(b, _):
            s_id = t * per_tile + b
            low = pl.multiple_of(low_ref[s_id], ROWS)
            steps = count_ref[s_id]
            put = pl.ds(pl.multiple_of(index_ref[s_id] * ROWS, ROWS), ROWS)

            def run(start, length, exact):
                q = qx[pl.ds(pl.multiple_of(b * ROWS, ROWS), ROWS), :]
                stacked = jnp.concatenate(
                    [jnp.where(of_head[h], q, jnp.zeros_like(q)) for h in range(HEAD_GROUP)], axis=0
                )
                scores = mm(stacked, kx[:, pl.ds(start, length)]) * SCORE_SCALE
                if exact:
                    scores = scores - jnp.max(scores, axis=1, keepdims=True)
                weights = jnp.exp2(scores).astype(BF)
                mixed = mm(weights, vx[pl.ds(start, length), :]).reshape(HEAD_GROUP, ROWS, 2 * cols)
                own = mixed[0]
                for h in range(1, HEAD_GROUP):
                    own = jnp.where(lane_out == h, mixed[h], own)
                out_ref[put, :] = (own[:, :cols] / own[:, cols:]).astype(BF)

            for i in range(span // WINDOW):
                pl.when(safe & (steps == i + 1))(
                    functools.partial(run, low, (i + 1) * WINDOW, False)
                )
            pl.when(jnp.logical_not(safe))(functools.partial(run, 0, span, True))
            return 0

        lax.fori_loop(0, per_tile, block, 0)
        return 0

    lax.fori_loop(0, tiles, tile, 0)


def attend(group, index, low, count, ids, w_qkv, rows):
    tiles, span = ids.shape
    cols = HEAD_GROUP * HDIM
    pairs = tiles * span * span * HEAD_GROUP // 2
    return pl.pallas_call(
        functools.partial(attend_kernel, group),
        out_shape=jax.ShapeDtypeStruct((rows.shape[0], cols), BF),
        in_specs=[SMEM, SMEM, SMEM, VMEM, VMEM, ANY],
        out_specs=VMEM,
        scratch_shapes=[
            pltpu.VMEM((tiles * span, rows.shape[1]), BF),
            pltpu.VMEM((span, 2 * cols), BF),
            pltpu.VMEM((2 * cols, span), BF),
            pltpu.VMEM((span, 2 * cols), BF),
            pltpu.SemaphoreType.DMA((tiles,)),
        ],
        compiler_params=ROOM,
        cost_estimate=cost(pairs * 1024, 4 * rows.size, pairs),
    )(index, low, count, ids, w_qkv, rows)


def home_kernel(
    counts_ref, order_ref, points_ref, spread_ref, base_ref, length_ref, first_row, last_row, acc
):
    step = pl.program_id(0)
    chunk, parents = spread_ref.shape

    @pl.when(step == 0)
    def _():
        counts = jnp.broadcast_to(counts_ref[...], (8, parents)).astype(F32)
        upper = jnp.where(iota((parents, parents), 0) <= iota((parents, parents), 1), 1.0, 0.0)
        starts = mm(counts.astype(BF), upper.astype(BF)) - counts
        coarse = jnp.floor(starts * (1.0 / 64.0))
        which = iota((8, parents), 0)
        fields = jnp.where(
            which == 0, coarse, jnp.where(which == 1, starts - 64.0 * coarse, counts)
        ).astype(BF)
        pick = jnp.where(iota((parents, parents), 0) == order_ref[...], 1.0, 0.0).astype(BF)
        ordered = mm(fields, pick)
        first_row[...] = (64.0 * ordered[0:1] + ordered[1:2]).astype(jnp.int32)
        last_row[...] = (64.0 * ordered[0:1] + ordered[1:2] + ordered[2:3]).astype(jnp.int32)
        select = jnp.where(iota((8, 128), 0) == 2, 1.0, 0.0).astype(BF)
        length_ref[...] = mm(ordered.astype(BF), select, TN)
        acc[...] = jnp.zeros_like(acc)

    row = iota((chunk, parents), 0) + step * chunk
    inside = (row >= first_row[...]) & (row < last_row[...])
    spread = jnp.where(inside, 1.0, 0.0).astype(BF)
    spread_ref[...] = spread
    acc[...] += mm(spread, points_ref[...], TN)

    @pl.when(step == pl.num_programs(0) - 1)
    def _():
        base_ref[...] = acc[...]


def home_tables(child_counts, parent_order, points):
    rows, width = points.shape
    parents = child_counts.shape[1]
    chunk = 512
    return pl.pallas_call(
        home_kernel,
        grid=(rows // chunk,),
        out_shape=(
            jax.ShapeDtypeStruct((rows, parents), BF),
            jax.ShapeDtypeStruct((parents, width), F32),
            jax.ShapeDtypeStruct((parents, 128), F32),
        ),
        in_specs=[
            pl.BlockSpec((1, parents), lambda i: (0, 0)),
            pl.BlockSpec((1, parents), lambda i: (0, 0)),
            pl.BlockSpec((chunk, width), lambda i: (i, 0)),
        ],
        out_specs=(
            pl.BlockSpec((chunk, parents), lambda i: (i, 0)),
            pl.BlockSpec((parents, width), lambda i: (0, 0)),
            pl.BlockSpec((parents, 128), lambda i: (0, 0)),
        ),
        scratch_shapes=[
            pltpu.VMEM((1, parents), jnp.int32),
            pltpu.VMEM((1, parents), jnp.int32),
            pltpu.VMEM((parents, width), F32),
        ],
        compiler_params=ROOM,
        cost_estimate=cost(2 * rows * parents * width, 2 * rows * parents),
    )(child_counts, parent_order, points)


def gather_kernel(
    last, place_ref, spread_ref, returned_ref, base_ref, w_ref, length_ref, out_ref, rows, acc, sem
):
    step = pl.program_id(0)
    chunk = spread_ref.shape[0]
    blocks = place_ref.shape[0]

    @pl.when(step == 0)
    def _():
        for b in range(blocks):
            pltpu.make_async_copy(
                returned_ref.at[pl.ds(pl.multiple_of(place_ref[b] * ROWS, ROWS), ROWS)],
                rows.at[pl.ds(b * ROWS, ROWS)],
                sem,
            ).start()
        acc[...] = jnp.zeros_like(acc)
        pltpu.make_async_copy(returned_ref.at[pl.ds(0, blocks * ROWS)], rows, sem).wait()

    acc[...] += mm(
        spread_ref[...], rows[pl.ds(pl.multiple_of(step * chunk, chunk), chunk), :], TN
    )

    @pl.when(step == pl.num_programs(0) - 1)
    def _():
        total = base_ref[...] + mm(acc[...].astype(BF), w_ref[...])
        if last:
            total = total / jnp.concatenate([length_ref[...]] * (total.shape[1] // 128), axis=1)
        out_ref[...] = total.astype(out_ref.dtype)


def gather_means(last, place, spread, returned, base, w_out, length, group):
    rows, parents = spread.shape
    width = base.shape[1]
    cols = returned.shape[1]
    chunk = 512
    fixed = lambda i: (0, 0)
    return pl.pallas_call(
        functools.partial(gather_kernel, last),
        grid=(rows // chunk,),
        out_shape=jax.ShapeDtypeStruct((parents, width), BF if last else F32),
        in_specs=[
            SMEM,
            pl.BlockSpec((chunk, parents), lambda i: (i, 0)),
            ANY,
            pl.BlockSpec((parents, width), fixed),
            pl.BlockSpec((cols, width), lambda i: (group, 0)),
            pl.BlockSpec((parents, 128), fixed),
        ],
        out_specs=pl.BlockSpec((parents, width), fixed),
        scratch_shapes=[
            pltpu.VMEM((rows, cols), BF),
            pltpu.VMEM((parents, cols), F32),
            pltpu.SemaphoreType.DMA,
        ],
        compiler_params=ROOM,
        cost_estimate=cost(2 * rows * parents * cols, 2 * rows * parents),
    )(place, spread, returned, base, w_out, length)


def pool_kernel(
    in_ref, w_ref, gain_ref, shift_ref, cot_ref, pooled_ref, back_ref, weight_ref, norm_ref, acc, sums
):
    step = pl.program_id(0)

    @pl.when(step == 0)
    def _():
        acc[...] = jnp.zeros_like(acc)
        sums[...] = jnp.zeros_like(sums)

    parent_in = in_ref[...]
    w_pool = w_ref[...]
    gain = gain_ref[...]
    projected = mm(parent_in, w_pool)
    centred = projected - jnp.mean(projected, axis=-1, keepdims=True)
    variance = jnp.mean(centred * centred, axis=-1, keepdims=True)
    inv_std = lax.rsqrt(variance + norm_eps)
    normed = centred * inv_std
    shifted = normed * gain + shift_ref[...]
    normal_cdf = 0.5 * (1.0 + lax.erf(shifted * inv_sqrt_two))
    pooled_ref[...] = (shifted * normal_cdf).astype(BF)
    grad_act = cot_ref[...].astype(F32) * (
        normal_cdf + shifted * jnp.exp(-0.5 * shifted * shifted) * inv_sqrt_tau
    )
    sums[0:1, :] += jnp.sum(grad_act * normed, axis=0, keepdims=True)
    sums[1:2, :] += jnp.sum(grad_act, axis=0, keepdims=True)
    scaled = grad_act * gain
    grad_proj = (
        (
            scaled
            - jnp.mean(scaled, axis=-1, keepdims=True)
            - normed * jnp.mean(scaled * normed, axis=-1, keepdims=True)
        )
        * inv_std
    ).astype(BF)
    acc[...] += mm(parent_in, grad_proj, TN)
    back_ref[...] = mm(grad_proj, w_pool, NT).astype(BF)

    @pl.when(step == pl.num_programs(0) - 1)
    def _():
        weight_ref[...] = acc[...].astype(BF)
        norm_ref[...] = sums[...]


def pool(parent_in, w_pool, gain, shift, cotangent):
    parents, width = parent_in.shape
    wide = w_pool.shape[1]
    chunk = 256
    fixed = lambda i: (0, 0)
    along = lambda i: (i, 0)
    return pl.pallas_call(
        pool_kernel,
        grid=(parents // chunk,),
        out_shape=(
            jax.ShapeDtypeStruct((parents, wide), BF),
            jax.ShapeDtypeStruct((parents, width), BF),
            jax.ShapeDtypeStruct((width, wide), BF),
            jax.ShapeDtypeStruct((8, wide), F32),
        ),
        in_specs=[
            pl.BlockSpec((chunk, width), along),
            pl.BlockSpec((width, wide), fixed),
            pl.BlockSpec((1, wide), fixed),
            pl.BlockSpec((1, wide), fixed),
            pl.BlockSpec((chunk, wide), along),
        ],
        out_specs=(
            pl.BlockSpec((chunk, wide), along),
            pl.BlockSpec((chunk, width), along),
            pl.BlockSpec((width, wide), fixed),
            pl.BlockSpec((8, wide), fixed),
        ),
        scratch_shapes=[pltpu.VMEM((width, wide), F32), pltpu.VMEM((8, wide), F32)],
        compiler_params=ROOM,
        cost_estimate=cost(6 * parents * width * wide, 8 * parents * wide, 2 * parents * wide),
    )(parent_in, w_pool, gain, shift, cotangent)


def spread_kernel(spread_ref, grad_ref, length_ref, out_ref, share):
    @pl.when(pl.program_id(0) == 0)
    def _():
        lengths = jnp.concatenate([length_ref[...]] * (share.shape[1] // 128), axis=1)
        share[...] = (grad_ref[...].astype(F32) / lengths).astype(BF)

    out_ref[...] = mm(spread_ref[...], share[...]).astype(BF)


def spread_grads(spread, grad_back, length):
    rows, parents = spread.shape
    width = grad_back.shape[1]
    chunk = 512
    fixed = lambda i: (0, 0)
    return pl.pallas_call(
        spread_kernel,
        grid=(rows // chunk,),
        out_shape=jax.ShapeDtypeStruct((rows, width), BF),
        in_specs=[
            pl.BlockSpec((chunk, parents), lambda i: (i, 0)),
            pl.BlockSpec((parents, width), fixed),
            pl.BlockSpec((parents, 128), fixed),
        ],
        out_specs=pl.BlockSpec((chunk, width), lambda i: (i, 0)),
        scratch_shapes=[pltpu.VMEM((parents, width), BF)],
        compiler_params=ROOM,
        cost_estimate=cost(2 * rows * parents * width, 2 * rows * parents),
    )(spread, grad_back, length)


def exchange(rows, devices):
    parts = rows.reshape(devices, rows.shape[0] // devices, rows.shape[1])
    moved = lax.all_to_all(parts, "pts", split_axis=0, concat_axis=0, tiled=True)
    return moved.reshape(rows.shape)


def received_index(hil_dest, hil_slot, devices, capacity):
    blocks = hil_dest.shape[0]
    codes = lax.all_gather(hil_dest * blocks + hil_slot, "pts")
    mine = codes // blocks == lax.axis_index("pts")
    slots = codes % blocks
    earlier = jnp.arange(blocks)[None, :] < jnp.arange(blocks)[:, None]
    rank = jnp.sum(mine[:, None, :] & earlier[None], axis=2)
    index = jnp.arange(devices)[:, None] * capacity + rank
    hit = mine[:, :, None] & (slots[:, :, None] == jnp.arange(blocks)[None, None, :])
    return jnp.sum(jnp.where(hit, index[:, :, None], 0), axis=(0, 1)).astype(jnp.int32)


def key_windows(patch_ids):
    tiles, span = patch_ids.shape
    patch = jnp.arange(PATCHES + 1)
    starts = jnp.sum(patch_ids[:, None, :] < patch[None, :, None], axis=2)
    by_block = patch_ids.reshape(tiles, span // ROWS, ROWS)
    first, last = by_block[:, :, 0], by_block[:, :, -1]
    pick = lambda which: jnp.sum(
        jnp.where(which[:, :, None] == patch[None, None, :], starts[:, None, :], 0), axis=2
    )
    low = pick(first) // ROWS * ROWS
    count = (pick(last + 1) - low + WINDOW - 1) // WINDOW
    low = jnp.minimum(low, span - count * WINDOW)
    return low.reshape(-1).astype(jnp.int32), count.reshape(-1).astype(jnp.int32)


def local(
    points,
    hil_dest,
    hil_slot,
    patch_ids,
    child_counts,
    parent_order,
    w_qkv,
    w_out,
    w_pool,
    norm_gain,
    norm_shift,
    cotangent,
):
    devices = lax.axis_size("pts")
    blocks = hil_dest.shape[0]
    width = points.shape[1]
    wide = w_pool.shape[1]
    parents = child_counts.shape[1]
    capacity = (blocks + devices - 1) // devices

    index = received_index(hil_dest, hil_slot, devices, capacity)
    payload, place = pack_blocks(hil_dest, points, devices, capacity)
    received = exchange(payload, devices)
    low, count = key_windows(patch_ids)
    spread, total, length = home_tables(child_counts, parent_order, points)

    groups = width // (HEAD_GROUP * HDIM)
    for group in range(groups):
        attended = attend(group, index, low, count, patch_ids, w_qkv, received)
        returned = exchange(attended, devices)
        total = gather_means(
            group == groups - 1, place, spread, returned, total, w_out, length, group
        )

    parent_in = exchange(total, devices)
    pooled, back, weight, norm = pool(
        parent_in, w_pool, norm_gain[None], norm_shift[None], cotangent
    )
    norm_high = norm.astype(BF)
    norm_low = (norm - norm_high.astype(F32)).astype(BF)
    norm_parts = jnp.concatenate([norm_high[:2], norm_low[:2]], axis=0).reshape(1, -1, width)
    outgoing = jnp.concatenate(
        [
            back.reshape(devices, -1, width),
            weight.reshape(devices, -1, width),
            jnp.broadcast_to(norm_parts, (devices,) + norm_parts.shape[1:]),
        ],
        axis=1,
    )
    arrived = lax.all_to_all(outgoing, "pts", split_axis=0, concat_axis=0, tiled=True)
    per_owner = parents // devices
    weight_rows = width * wide // width // devices
    grad_back = arrived[:, :per_owner].reshape(parents, width)
    weight_sum = jnp.sum(arrived[:, per_owner : per_owner + weight_rows].astype(F32), axis=0)
    norm_sum = jnp.sum(arrived[:, per_owner + weight_rows :].astype(F32), axis=0)
    norm_sum = norm_sum.reshape(4, wide)
    grad_norm = norm_sum[:2] + norm_sum[2:]
    shared = jnp.broadcast_to(weight_sum.astype(BF)[None], (devices,) + weight_sum.shape)
    grad_weight = (
        lax.all_to_all(shared, "pts", split_axis=0, concat_axis=0, tiled=True)
        .reshape(width, wide)
        .astype(F32)
    )
    grad_points = spread_grads(spread, grad_back, length)
    return (pooled, grad_points, grad_weight, grad_norm)


def solution(mesh):
    in_specs = (
        P(("grp", "pts"), None),
        P(("grp", "pts")),
        P(("grp", "pts")),
        P(("grp", "pts"), None),
        P(("grp", "pts"), None),
        P(("grp", "pts"), None),
        P(),
        P(),
        P(),
        P(),
        P(),
        P(("grp", "pts"), None),
    )
    out_specs = (P(("grp", "pts"), None), P(("grp", "pts"), None), P("grp", None), P("grp", None))
    return jax.shard_map(local, mesh=mesh, in_specs=in_specs, out_specs=out_specs, check_vma=False)
```

time: 657 us -> 350 us (0.53)
  matrix products: 298 us -> 0 us
  Pallas kernels: 0 us -> 216 us
  waiting for transfers between devices: 116 us -> 3.78 us
  local copies, waits for them, and re-layouts: 94.7 us -> 10.2 us
  blocking collectives: 34.6 us -> 94.3 us
  other arithmetic: 56.3 us -> 1.35 us
  starting transfers between devices: 40.4 us -> 21.5 us
  between operations: 14.4 us -> 1.63 us
    pallas_call x0 -> x8, Pallas kernels: none -> 216 us  [the longest x2 169 us: attend(): pl.pallas_call(functools.partial(attend_kernel, group), out_shape=jax.Sha...]
    sub x16 -> x0, matrix products: 157 us -> none  [one_group(): weights_exp = jnp.exp(scores - row_max)]
    dot_general x27 -> x0, matrix products: 142 us -> none  [the longest x16 122 us: one_group(): jnp.einsum('hqk,khd->qhd', probability, value_g, preferred_element_type=j...]
    all_to_all x5 -> x4, waiting for transfers between devices: 85.5 us -> 3.78 us  [the longest x3 3.05 us: exchange(): lax.all_to_all(parts, 'pts', split_axis=0, concat_axis=0, tiled=True)]
    unnamed x0 -> x1, blocking collectives: none -> 47.9 us
    gather x6 -> x0, local copies, waits for them, and re-layouts: 47.5 us -> none  [the longest x1 16.7 us: local(): child_total.astype(jnp.float32)[parent_ids][:, None]]
    all_to_all x0 -> x2, blocking collectives: none -> 46.4 us  [the longest x1 25.3 us: local(): lax.all_to_all(outgoing, 'pts', split_axis=0, concat_axis=0, tiled=True)]
    psum x1 -> x0, blocking collectives: 34.6 us -> none  [local(): grad_weight, grad_norm = lax.psum((local_weight, local_norm), 'pts')]
  transfers between devices with their start and end apart: 6 -> 4, of which waited for: 4 -> 2; matrix products, arithmetic and copies ran while one was open for 10% -> 1% of each run, Pallas kernels for 0% -> 32%
where the time goes in v1:
time: 350 us; the launch traced here: 348 us
  Pallas kernels  216 us (62%)
  blocking collectives  94.3 us (27%)
  starting transfers between devices  21.5 us (6%)
  local copies, waits for them, and re-layouts  10.2 us (3%)
  waiting for transfers between devices  3.78 us (1%)
    pallas_call x2, Pallas kernels, attend(): pl.pallas_call(functools.partial(attend_kernel, group), out_shape=jax.Sha...  169 us
    unnamed x1, blocking collectives  47.9 us
    all_to_all x1, blocking collectives, local(): lax.all_to_all(outgoing, 'pts', split_axis=0, concat_axis=0, tiled=True)  25.3 us
    all_to_all x1, blocking collectives, exchange(): lax.all_to_all(parts, 'pts', split_axis=0, concat_axis=0, tiled=True)  21.1 us
    pallas_call x2, Pallas kernels, gather_means(): pl.pallas_call(functools.partial(gather_kernel, last), grid=(rows // chun...  19 us
    all_to_all x3, starting transfers between devices, exchange(): lax.all_to_all(parts, 'pts', split_axis=0, concat_axis=0, tiled=True)  17.3 us
    pallas_call x1, Pallas kernels, home_tables(): pl.pallas_call(home_kernel, grid=(rows // chunk,), out_shape=(jax.ShapeDt...  8.71 us
    pallas_call x1, Pallas kernels, spread_grads(): pl.pallas_call(spread_kernel, grid=(rows // chunk,), out_shape=jax.ShapeD...  8.62 us
  transfers between devices with their start and end apart: 4, of which 2 were waited for; matrix products, arithmetic and copies ran while one was open for 1% of the time, Pallas kernels for 32%

profile of v1, /device:TPU:0, one launch (start us, length us, event | category | flops | bytes accessed | tf_op | source)
XLA Modules:
  0.0 348.5 jit_solution(4113336912001096252)
XLA Ops:
  0.6 0.0 copy-start
  0.6 1.6 copy-done
  2.2 0.7 copy-done.7
  2.9 4.3 %shard_map.147 = (bf16[4096,256]{1,0:T(8,128)(2,1)S(1)}, s32[32]{0:T(128)S(1)}) custom-call(s32[32]{0:T(128)S(1)} %copy-done.7, bf16[4096,256]{1,0:T(8,128)(2,1)S(1)} %copy-done), custom_call_target="tpu_custom_call" | custom-call | bytes 4194304 | tf_op jit(solution)/shard_map/pallas_call | solution.py:75
  7.2 0.0 copy-start.4
  7.2 1.3 copy-done.4
  8.5 0.0 copy-start.10
  8.6 7.5 %all-to-all-start = ((bf16[16,256,256]{2,1,0:T(8,128)(2,1)}), bf16[16,256,256]{2,1,0:T(8,128)(2,1)S(1)}, u32[]{:S(2)}, u32[]{:S(2)}) async-start(bf16[16,256,256]{2,1,0:T(8,128)(2,1)} %bitcast.24), calls=%async_computation | async-start | bytes 4194304 | tf_op jit(solution)/shard_map/all_to_all | solution.py:427
  16.1 0.6 dynamic-slice
  17.4 0.1 add_dynamic-update-slice_fusion
  17.5 47.9 %all-reduce = s32[512]{0:T(512)S(1)} all-reduce(s32[512]{0:T(512)S(1)} %add_dynamic-update-slice_fusion), channel_id=2, replica_groups=mesh['grp'=2,'pts'=16] {'pts'}, use_global_device_ids=true, to_apply=%add | all-reduce | flops 512 | bytes 4096
  65.3 0.1 reshape.112
  65.4 0.1 fusion.6
  65.5 0.1 copy.20
  65.6 0.1 copy.23
  65.7 0.2 convert_reduce_fusion.2
  65.9 0.1 select_reduce_fusion.1
  66.0 0.1 reduce_sum.76
  66.1 0.1 reduce_sum.74
  66.2 0.3 convert_reduce_fusion
  66.5 0.1 add_select_fusion
  66.6 0.3 select_reduce_fusion.index_ref
  66.9 0.0 copy-start.2
  66.9 84.6 %shard_map.150 = bf16[4096,128]{1,0:T(8,128)(2,1)} custom-call(s32[32]{0:T(128)S(1)} %select_reduce_fusion.index_ref, s32[32]{0:T(128)S(1)} %get-tuple-element.24.low_ref, s32[32]{0:T(128)S(1)} %get-tuple-element.25.count_ref, s32[4,1024]{1,0:T(4,128)S(1)} %copy-done.6, bf16[256,768]{1,0:T(8,128)(2,1)S(1)} %copy-done.10, bf16[4096,256]{1,0:T(8,128)(2,1)S(1)} %bitcast.22), custom_call_target="tpu_custom_call" | custom-call | flops 17179869184 | bytes 4194304 | tf_op jit(solution)/shard_map/pallas_call | solution.py:174
  151.6 3.9 %all-to-all-start.2 = ((bf16[16,256,128]{2,1,0:T(8,128)(2,1)}), bf16[16,256,128]{2,1,0:T(8,128)(2,1)S(1)}, u32[]{:S(2)}, u32[]{:S(2)}) async-start(bf16[16,256,128]{2,1,0:T(8,128)(2,1)} %bitcast.7), calls=%async_computation.2 | async-start | bytes 2097152 | tf_op jit(solution)/shard_map/all_to_all | solution.py:427
  155.4 0.0 copy-start.3
  155.4 1.6 copy-done.3
  157.0 84.6 %shard_map.149 = bf16[4096,128]{1,0:T(8,128)(2,1)} custom-call(s32[32]{0:T(128)S(1)} %select_reduce_fusion.index_ref, s32[32]{0:T(128)S(1)} %get-tuple-element.24.low_ref, s32[32]{0:T(128)S(1)} %get-tuple-element.25.count_ref, s32[4,1024]{1,0:T(4,128)S(1)} %copy-done.6, bf16[256,768]{1,0:T(8,128)(2,1)S(1)} %copy-done.10, bf16[4096,256]{1,0:T(8,128)(2,1)S(1)} %bitcast.23), custom_call_target="tpu_custom_call" | custom-call | flops 17179869184 | bytes 4194304 | tf_op jit(solution)/shard_map/pallas_call | solution.py:174
  241.6 0.0 copy-start.12
  241.7 0.0 copy-start.13
  241.7 5.9 %all-to-all-start.1 = ((bf16[16,256,128]{2,1,0:T(8,128)(2,1)}), bf16[16,256,128]{2,1,0:T(8,128)(2,1)}, u32[]{:S(2)}, u32[]{:S(2)}) async-start(bf16[16,256,128]{2,1,0:T(8,128)(2,1)} %bitcast.5), calls=%async_computation.1 | async-start | bytes 2097152 | tf_op jit(solution)/shard_map/all_to_all | solution.py:427
  247.6 0.0 copy-start.1
  247.6 1.6 copy-done.1
  249.2 8.7 %shard_map.148 = (bf16[4096,1024]{1,0:T(8,128)(2,1)}, f32[1024,256]{1,0:T(8,128)S(1)}, f32[1024,128]{1,0:T(8,128)S(1)}) custom-call(s32[1,1024]{1,0:T(1,128)S(1)} %copy-done.12, s32[1,1024]{1,0:T(1,128)S(1)} %copy-done.13, bf16[4096,256]{1,0:T(8,128)(2,1)S(1)} %copy-done.1), custom_call_target="tpu_custom_call" | custom-call | flops 2147483648 | bytes 8388608 | tf_op jit(solution)/shard_map/pallas_call | solution.py:230
  257.9 9.6 %shard_map.151.base_ref = f32[1024,256]{1,0:T(8,128)S(1)} custom-call(s32[32]{0:T(128)S(1)} %get-tuple-element.13.place_ref, bf16[4096,1024]{1,0:T(8,128)(2,1)} %get-tuple-element.14.spread_ref, bf16[4096,128]{1,0:T(8,128)(2,1)S(1)} %bitcast.19, f32[1024,256]{1,0:T(8,128)S(1)} %get-tuple-element.16.base_ref, bf16[256,256]{1,0:T(8,128)(2,1)S(1)} %copy-done.5, ...), custom_call_target="tpu_custom_call" | custom-call | flops 1073741824 | bytes 8388608 | tf_op jit(solution)/shard_map/pallas_call | solution.py:294
  267.6 3.0 all-to-all-done.1
  270.6 9.4 %shard_map.152 = bf16[1024,256]{1,0:T(8,128)(2,1)S(1)} custom-call(s32[32]{0:T(128)S(1)} %get-tuple-element.13.place_ref, bf16[4096,1024]{1,0:T(8,128)(2,1)} %get-tuple-element.14.spread_ref, bf16[4096,128]{1,0:T(8,128)(2,1)} %bitcast.6.returned_ref, f32[1024,256]{1,0:T(8,128)S(1)} %shard_map.151.base_ref, bf16[256,256]{1,0:T(8,128)(2,1)S(1)} %copy-done.5, ...), custom_call_target="tpu_custom_call" | custom-call | flops 1073741824 | bytes 8388608 | tf_op jit(solution)/shard_map/pallas_call | solution.py:294
  280.0 21.1 %all_to_all.30 = bf16[16,64,256]{2,1,0:T(8,128)(2,1)S(1)} all-to-all(bf16[16,64,256]{2,1,0:T(8,128)(2,1)S(1)} %bitcast.20), channel_id=1, replica_groups=mesh['grp'=2,'pts'=16] {'pts'}, dimensions={0} | all-to-all | bytes 1048576 | tf_op jit(solution)/shard_map/all_to_all | solution.py:427
  301.2 5.9 %shard_map.153 = (bf16[1024,512]{1,0:T(8,128)(2,1)}, bf16[1024,256]{1,0:T(8,128)(2,1)S(1)}, bf16[256,512]{1,0:T(8,128)(2,1)S(1)}, f32[8,512]{1,0:T(8,128)S(1)}) custom-call(bf16[1024,256]{1,0:T(8,128)(2,1)S(1)} %bitcast.26, bf16[256,512]{1,0:T(8,128)(2,1)S(1)} %copy-done.11, f32[1,512]{1,0:T(1,128)S(1)} %bitcast.28, f32[1,512]{1,0:T(1,128)S(1)} %bitcast.29, ...), custom_call_target="tpu_custom_call" | custom-call | flops 805306368 | bytes 4194304 | tf_op jit(solution)/shard_map/pallas_call | solution.py:367
  307.1 0.1 reshape.109
  307.2 0.1 pad_maximum_fusion
  307.3 25.3 %all_to_all.31 = bf16[16,104,256]{2,1,0:T(8,128)(2,1)S(1)} all-to-all(bf16[16,104,256]{2,1,0:T(8,128)(2,1)S(1)} %pad_maximum_fusion), channel_id=1, replica_groups=mesh['grp'=2,'pts'=16] {'pts'}, dimensions={0} | all-to-all | bytes 1703936 | tf_op jit(solution)/shard_map/all_to_all | solution.py:508
  332.6 0.7 broadcast_in_dim.71
  333.3 4.2 %all-to-all-start.5 = ((bf16[16,32,256]{2,1,0:T(8,128)(2,1)}), bf16[16,32,256]{2,1,0:T(8,128)(2,1)S(1)}, u32[]{:S(2)}, u32[]{:S(2)}) async-start(bf16[16,32,256]{2,1,0:T(8,128)(2,1)} %broadcast_in_dim.71), calls=%async_computation.5 | async-start | bytes 524288 | tf_op jit(solution)/shard_map/all_to_all | solution.py:518
  337.6 0.6 add.52
  338.3 8.6 %shard_map.154 = bf16[4096,256]{1,0:T(8,128)(2,1)} custom-call(bf16[4096,1024]{1,0:T(8,128)(2,1)} %get-tuple-element.14.spread_ref, bf16[1024,256]{1,0:T(8,128)(2,1)S(1)} %bitcast.21, f32[1024,128]{1,0:T(8,128)S(1)} %get-tuple-element.17.length_ref), custom_call_target="tpu_custom_call" | custom-call | flops 2147483648 | bytes 8388608 | tf_op jit(solution)/shard_map/pallas_call | solution.py:409
  346.9 0.7 all-to-all-done.5
  347.6 0.9 reshape.111
  (41 shorter events, 0.3 us)
Async XLA Ops:
  0.6 1.6 copy-start
  2.2 0.7 copy-start.7
  7.2 1.3 copy-start.4
  8.5 7.6 %copy-start.17 = (u32[32]{0:T(128)S(1)}, u32[32]{0:T(128)}, u32[]{:S(2)}) copy-start(u32[32]{0:T(128)} %constant.78) | copy-start | bytes 388
  8.5 8.8 %copy-start.8 = (s32[32]{0:T(128)S(1)}, s32[32]{0:T(128)}, u32[]{:S(2)}) copy-start(s32[32]{0:T(128)} %dest_ref.1) | copy-start | bytes 388
  8.5 8.8 %copy-start.16 = (s32[32]{0:T(128)S(1)}, s32[32]{0:T(128)}, u32[]{:S(2)}) copy-start(s32[32]{0:T(128)} %param.14) | copy-start | bytes 388
  8.5 56.9 %copy-start.6 = (s32[4,1024]{1,0:T(4,128)S(1)}, s32[4,1024]{1,0:T(4,128)}, u32[]{:S(2)}) copy-start(s32[4,1024]{1,0:T(4,128)} %ids_ref.3) | copy-start | bytes 49156
  8.5 58.4 %copy-start.10 = (bf16[256,768]{1,0:T(8,128)(2,1)S(1)}, bf16[256,768]{1,0:T(8,128)(2,1)}, u32[]{:S(2)}) copy-start(bf16[256,768]{1,0:T(8,128)(2,1)} %w_ref.6) | copy-start | bytes 1179652
  8.6 58.4 %all-to-all-start = ((bf16[16,256,256]{2,1,0:T(8,128)(2,1)}), bf16[16,256,256]{2,1,0:T(8,128)(2,1)S(1)}, u32[]{:S(2)}, u32[]{:S(2)}) async-start(bf16[16,256,256]{2,1,0:T(8,128)(2,1)} %bitcast.24), calls=%async_computation | async-start | bytes 4194304 | tf_op jit(solution)/shard_map/all_to_all | solution.py:427
  66.9 84.6 %copy-start.2 = (bf16[16,256,256]{2,1,0:T(8,128)(2,1)}, bf16[16,256,256]{2,1,0:T(8,128)(2,1)S(1)}, u32[]{:S(2)}) copy-start(bf16[16,256,256]{2,1,0:T(8,128)(2,1)S(1)} %all-to-all-done) | copy-start | bytes 6291460
  151.6 90.1 %all-to-all-start.2 = ((bf16[16,256,128]{2,1,0:T(8,128)(2,1)}), bf16[16,256,128]{2,1,0:T(8,128)(2,1)S(1)}, u32[]{:S(2)}, u32[]{:S(2)}) async-start(bf16[16,256,128]{2,1,0:T(8,128)(2,1)} %bitcast.7), calls=%async_computation.2 | async-start | bytes 2097152 | tf_op jit(solution)/shard_map/all_to_all | solution.py:427
  155.4 1.6 copy-start.3
  241.6 6.0 %copy-start.12 = (s32[1,1024]{1,0:T(1,128)S(1)}, s32[1,1024]{1,0:T(1,128)}, u32[]{:S(2)}) copy-start(s32[1,1024]{1,0:T(1,128)} %counts_ref.1) | copy-start | bytes 12292
  241.7 6.0 %copy-start.13 = (s32[1,1024]{1,0:T(1,128)S(1)}, s32[1,1024]{1,0:T(1,128)}, u32[]{:S(2)}) copy-start(s32[1,1024]{1,0:T(1,128)} %order_ref.1) | copy-start | bytes 12292
  241.7 28.9 %all-to-all-start.1 = ((bf16[16,256,128]{2,1,0:T(8,128)(2,1)}), bf16[16,256,128]{2,1,0:T(8,128)(2,1)}, u32[]{:S(2)}, u32[]{:S(2)}) async-start(bf16[16,256,128]{2,1,0:T(8,128)(2,1)} %bitcast.5), calls=%async_computation.1 | async-start | bytes 2097152 | tf_op jit(solution)/shard_map/all_to_all | solution.py:427
  247.6 1.6 copy-start.1
  249.2 8.7 %copy-start.5 = (bf16[256,256]{1,0:T(8,128)(2,1)S(1)}, bf16[256,256]{1,0:T(8,128)(2,1)}, u32[]{:S(2)}) copy-start(bf16[256,256]{1,0:T(8,128)(2,1)} %w_ref.8) | copy-start | bytes 393220
  270.6 30.5 %copy-start.9 = (bf16[1024,512]{1,0:T(8,128)(2,1)S(1)}, bf16[1024,512]{1,0:T(8,128)(2,1)}, u32[]{:S(2)}) copy-start(bf16[1024,512]{1,0:T(8,128)(2,1)} %cot_ref.1) | copy-start | bytes 3145732
  270.6 30.5 %copy-start.11 = (bf16[256,512]{1,0:T(8,128)(2,1)S(1)}, bf16[256,512]{1,0:T(8,128)(2,1)}, u32[]{:S(2)}) copy-start(bf16[256,512]{1,0:T(8,128)(2,1)} %w_ref.9) | copy-start | bytes 786436
  270.6 30.5 %copy-start.14 = (f32[512]{0:T(512)S(1)}, f32[512]{0:T(512)}, u32[]{:S(2)}) copy-start(f32[512]{0:T(512)} %param.21) | copy-start | bytes 6148
  270.6 30.5 %copy-start.15 = (f32[512]{0:T(512)S(1)}, f32[512]{0:T(512)}, u32[]{:S(2)}) copy-start(f32[512]{0:T(512)} %param.22) | copy-start | bytes 6148
  333.3 14.3 %all-to-all-start.5 = ((bf16[16,32,256]{2,1,0:T(8,128)(2,1)}), bf16[16,32,256]{2,1,0:T(8,128)(2,1)S(1)}, u32[]{:S(2)}, u32[]{:S(2)}) async-start(bf16[16,32,256]{2,1,0:T(8,128)(2,1)} %broadcast_in_dim.71), calls=%async_computation.5 | async-start | bytes 524288 | tf_op jit(solution)/shard_map/all_to_all | solution.py:518

commit v2 on v1

v2 whole, which is shorter than its diff:
```python
import functools
import math

import jax
import jax.numpy as jnp
from jax import lax
from jax.experimental import pallas as pl
from jax.experimental.pallas import tpu as pltpu
from jax.sharding import PartitionSpec as P

HDIM = 16
HEAD_GROUP = 8
ROWS = 128
SEAT = 128
SEATS = 112
INFO = 16
WINDOW = 256
PATCHES = 4
FAR = 2.0**100
SCORE_SCALE = HDIM**-0.5 * math.log2(math.e)
SCORE_SAFE = 98.0

inv_sqrt_two = 0.7071067811865476
inv_sqrt_tau = 0.3989422804014327
norm_eps = 1e-05

BF = jnp.bfloat16
F32 = jnp.float32
NT = (((1,), (1,)), ((), ()))
TN = (((0,), (0,)), ((), ()))
VMEM = pl.BlockSpec(memory_space=pltpu.VMEM)
HBM = pl.BlockSpec(memory_space=pltpu.HBM)
SMEM = pl.BlockSpec(memory_space=pltpu.SMEM)
ANY = pl.BlockSpec(memory_space=pl.ANY)
ROOM = pltpu.CompilerParams(vmem_limit_bytes=48 << 20)


def iota(shape, dim):
    return lax.broadcasted_iota(jnp.int32, shape, dim)


def mm(a, b, dims=(((1,), (0,)), ((), ()))):
    return lax.dot_general(a, b, dims, preferred_element_type=F32)


def cost(flops, bytes_accessed, transcendentals=0):
    return pl.CostEstimate(
        flops=int(flops), bytes_accessed=int(bytes_accessed), transcendentals=int(transcendentals)
    )


def pack_kernel(capacity, dest_ref, points_ref, payload_ref, used, sem):
    blocks = dest_ref.shape[0]

    def clear(d, _):
        used[d] = 0
        return 0

    lax.fori_loop(0, used.shape[0], clear, 0)

    def send(b, _):
        d = dest_ref[b]
        place = d * capacity + used[d]
        used[d] = used[d] + 1
        pltpu.make_async_copy(
            points_ref.at[pl.ds(pl.multiple_of(b * ROWS, ROWS), ROWS)],
            payload_ref.at[pl.ds(pl.multiple_of(place * ROWS, ROWS), ROWS)],
            sem,
        ).start()
        return 0

    lax.fori_loop(0, blocks, send, 0)
    whole = pl.ds(0, blocks * ROWS)
    pltpu.make_async_copy(points_ref.at[whole], payload_ref.at[whole], sem).wait()


def pack_blocks(hil_dest, points, devices, capacity):
    return pl.pallas_call(
        functools.partial(pack_kernel, capacity),
        out_shape=jax.ShapeDtypeStruct((devices * capacity * ROWS, points.shape[1]), BF),
        in_specs=[SMEM, HBM],
        out_specs=HBM,
        scratch_shapes=[pltpu.SMEM((devices,), jnp.int32), pltpu.SemaphoreType.DMA],
        compiler_params=ROOM,
        cost_estimate=cost(0, 4 * points.size),
    )(hil_dest, points)


def order_kernel(counts_ref, order_ref, dest_ref, slot_ref, info_ref, span_ref, code):
    parents = counts_ref.shape[1]
    blocks = dest_ref.shape[1]
    counts = jnp.broadcast_to(counts_ref[...], (8, parents)).astype(F32)
    upper = jnp.where(iota((parents, parents), 0) <= iota((parents, parents), 1), 1.0, 0.0)
    starts = mm(counts.astype(BF), upper.astype(BF)) - counts
    coarse = jnp.floor(starts * (1.0 / 64.0))
    which = iota((8, parents), 0)
    fields = jnp.where(which == 0, coarse, jnp.where(which == 1, starts - 64.0 * coarse, counts))
    pick = jnp.where(iota((parents, parents), 0) == order_ref[...], 1.0, 0.0).astype(BF)
    ordered = mm(fields.astype(BF), pick).astype(jnp.int32)
    first = 64 * ordered[0:1] + ordered[1:2]
    length = ordered[2:3]
    span_ref[...] = jnp.where(which == 0, first, jnp.where(which == 1, first + length, length))
    both = 16 * first + length
    code[...] = jnp.zeros_like(code)
    code[0:1, :blocks] = dest_ref[...] * blocks + slot_ref[...]
    tile = jnp.concatenate(
        [both[:, i * 128 : (i + 1) * 128] for i in range(parents // 128)] + [code[...]], axis=0
    )
    for d in range(info_ref.shape[0]):
        info_ref[d] = tile


def order_tables(child_counts, parent_order, hil_dest, hil_slot, devices):
    parents = child_counts.shape[1]
    return pl.pallas_call(
        order_kernel,
        out_shape=(
            jax.ShapeDtypeStruct((devices, INFO, 128), jnp.int32),
            jax.ShapeDtypeStruct((8, parents), jnp.int32),
        ),
        in_specs=[VMEM] * 4,
        out_specs=(VMEM, VMEM),
        scratch_shapes=[pltpu.VMEM((INFO - parents // 128, 128), jnp.int32)],
        compiler_params=ROOM,
        cost_estimate=cost(32 * parents * parents, 8 * parents),
    )(child_counts, parent_order, hil_dest[None], hil_slot[None])


def seat_kernel(per_owner, source_ref, block_ref, info_ref, seat_ref, most_ref, owner, place, origin):
    blocks = owner.shape[0]
    parents = 128 * 8
    devices = info_ref.shape[0] // INFO
    which = iota((16, parents), 0)
    rank = iota((16, parents), 1)
    fields = jnp.where(which == 0, rank // per_owner, jnp.where(which == 1, rank % per_owner, 0))
    fields = fields.astype(F32).astype(BF)

    def one(v, _):
        source = source_ref[v]
        packed = info_ref[pl.ds(pl.multiple_of(source * INFO, INFO), 8), :]
        line = jnp.concatenate([packed[i : i + 1] for i in range(8)], axis=1)
        first = line // 16
        row = block_ref[v] * ROWS + iota((ROWS, parents), 0)
        inside = (row >= first) & (row < first + line % 16)
        found = mm(fields, jnp.where(inside, 1.0, 0.0).astype(BF), NT)
        owner[pl.ds(v, 1), :] = found[0:1]
        place[pl.ds(v, 1), :] = found[1:2]
        origin[pl.ds(v, 1), :] = jnp.full((1, ROWS), source, jnp.int32).astype(F32)
        return 0

    lax.fori_loop(0, blocks, one, 0)
    own = owner[...]
    own_place = place[...]
    run = own * per_owner + own_place
    opens = (iota((blocks, ROWS), 1) == 0) | (run != pltpu.roll(run, 1, 1))
    opened = jnp.where(opens, 1.0, 0.0)
    upper = jnp.where(iota((ROWS, ROWS), 0) <= iota((ROWS, ROWS), 1), 1.0, 0.0).astype(BF)
    every = jnp.ones((ROWS, ROWS), BF)
    before = jnp.where(iota((blocks, blocks), 1) < iota((blocks, blocks), 0), 1.0, 0.0).astype(BF)

    def count(e, carry):
        seat, most = carry
        here = own == e.astype(F32)
        marks = jnp.where(here, opened, 0.0).astype(BF)
        total = mm(marks, upper) + mm(before, mm(marks, every).astype(BF))
        return jnp.where(here, total - 1.0, seat), jnp.maximum(most, total)

    zero = jnp.zeros((blocks, ROWS), F32)
    seat, most = lax.fori_loop(0, devices, count, (zero, zero))
    seat_ref[...] = jnp.zeros_like(seat_ref)
    for i, value in enumerate((own, seat, opened * origin[...], opened * own_place)):
        for v in range(blocks):
            seat_ref[i : i + 1, v * ROWS : (v + 1) * ROWS] = value[v : v + 1]
    most_ref[...] = jnp.full((8, 128), jnp.max(most), F32)


def seat_rows(source, block, info, per_owner):
    blocks = source.shape[0]
    rows = blocks * ROWS
    return pl.pallas_call(
        functools.partial(seat_kernel, per_owner),
        out_shape=(jax.ShapeDtypeStruct((8, rows), F32), jax.ShapeDtypeStruct((8, 128), F32)),
        in_specs=[SMEM, SMEM, VMEM],
        out_specs=(VMEM, VMEM),
        scratch_shapes=[pltpu.VMEM((blocks, ROWS), F32)] * 3,
        compiler_params=ROOM,
        cost_estimate=cost(40 * rows * 1024, 8 * rows),
    )(source, block, info)


def attend_kernel(
    index_ref, low_ref, count_ref, ids_ref, w_ref, wo_ref, rows_ref, out_ref, x, qx, kx, vx, att, sems
):
    tiles, span = ids_ref.shape
    width = w_ref.shape[0]
    cols = HEAD_GROUP * HDIM
    groups = width // cols
    heads = width // HDIM
    per_tile = span // ROWS

    for t in range(tiles):
        for b in range(per_tile):
            s = t * per_tile + b
            pltpu.make_async_copy(
                rows_ref.at[pl.ds(pl.multiple_of(index_ref[s] * ROWS, ROWS), ROWS)],
                x.at[pl.ds(s * ROWS, ROWS)],
                sems.at[t],
            ).start()

    lane = iota((ROWS, 2 * cols), 1)
    of_head = [(lane // HDIM == h) | (lane >= cols) for h in range(HEAD_GROUP)]
    lane_out = lane % cols // HDIM
    for g in range(groups):
        vx[g, :, cols:] = jnp.ones((span, cols), BF)
    r_i = iota((cols, cols), 0)
    c_i = iota((cols, cols), 1)
    far = jnp.where((r_i != c_i) & (c_i < PATCHES), -FAR, 0.0).astype(BF)

    def tile(t, _):
        at = pl.ds(pl.multiple_of(t * span, span), span)
        pltpu.make_async_copy(rows_ref.at[pl.ds(0, span)], x.at[at], sems.at[t]).wait()
        tile_rows = x[at, :]
        same = ids_ref[pl.ds(t, 1), :] == iota((cols, span), 0)
        patch_hot = jnp.where(same, 1.0, 0.0).astype(BF)
        query = mm(tile_rows, w_ref[:, :width])
        keys = mm(w_ref[:, width : 2 * width], tile_rows, (((0,), (1,)), ((), ())))
        value = mm(tile_rows, w_ref[:, 2 * width :]).astype(BF)
        patch_far = mm(patch_hot, far, TN).astype(BF)
        for g in range(groups):
            some = slice(g * cols, (g + 1) * cols)
            qx[g, :, :cols] = query[:, some].astype(BF)
            qx[g, :, cols:] = patch_far
            kx[g, :cols, :] = keys[some].astype(BF)
            kx[g, cols:, :] = patch_hot
            vx[g, :, :cols] = value[:, some]
        query_most = jnp.max(jnp.abs(query), axis=0, keepdims=True)
        key_most = jnp.max(jnp.abs(keys), axis=1, keepdims=True)
        by_head = jnp.where(
            iota((heads, width), 1) // HDIM == iota((heads, width), 0), query_most, 0.0
        )
        bound = jnp.max(mm(by_head.astype(BF), jnp.broadcast_to(key_most, (width, 128)).astype(BF)))
        safe = bound * SCORE_SCALE < SCORE_SAFE

        def block(b, _):
            low = pl.multiple_of(low_ref[t * per_tile + b], ROWS)
            steps = count_ref[t * per_tile + b]
            here = pl.ds(pl.multiple_of(b * ROWS, ROWS), ROWS)

            def run(start, length, exact):
                scores = []
                for g in range(groups):
                    q = qx[g, here, :]
                    stacked = jnp.concatenate(
                        [jnp.where(of_head[h], q, jnp.zeros_like(q)) for h in range(HEAD_GROUP)],
                        axis=0,
                    )
                    scores.append(mm(stacked, kx[g, :, pl.ds(start, length)]))
                for g in range(groups):
                    level = scores[g] * SCORE_SCALE
                    if exact:
                        level = level - jnp.max(level, axis=1, keepdims=True)
                    weights = jnp.exp2(level).astype(BF)
                    mixed = mm(weights, vx[g, pl.ds(start, length), :])
                    mixed = mixed.reshape(HEAD_GROUP, ROWS, 2 * cols)
                    own = mixed[0]
                    for h in range(1, HEAD_GROUP):
                        own = jnp.where(lane_out == h, mixed[h], own)
                    att[here, g * cols : (g + 1) * cols] = (own[:, :cols] / own[:, cols:]).astype(BF)

            for i in range(span // WINDOW):
                pl.when(safe & (steps == i + 1))(
                    functools.partial(run, low, (i + 1) * WINDOW, False)
                )
            pl.when(jnp.logical_not(safe))(functools.partial(run, 0, span, True))
            return 0

        lax.fori_loop(0, per_tile, block, 0)
        out_ref[at, :] = (tile_rows.astype(F32) + mm(att[...], wo_ref[...])).astype(BF)
        return 0

    lax.fori_loop(0, tiles, tile, 0)


def attend(index, low, count, ids, w_qkv, w_out, rows):
    tiles, span = ids.shape
    width = rows.shape[1]
    cols = HEAD_GROUP * HDIM
    groups = width // cols
    pairs = tiles * span * span * HEAD_GROUP
    return pl.pallas_call(
        attend_kernel,
        out_shape=jax.ShapeDtypeStruct((tiles * span, width), BF),
        in_specs=[SMEM, SMEM, SMEM, VMEM, VMEM, VMEM, HBM],
        out_specs=VMEM,
        scratch_shapes=[
            pltpu.VMEM((tiles * span, width), BF),
            pltpu.VMEM((groups, span, 2 * cols), BF),
            pltpu.VMEM((groups, 2 * cols, span), BF),
            pltpu.VMEM((groups, span, 2 * cols), BF),
            pltpu.VMEM((span, width), BF),
            pltpu.SemaphoreType.DMA((tiles,)),
        ],
        compiler_params=ROOM,
        cost_estimate=cost(pairs * 1024, 4 * rows.size, pairs),
    )(index, low, count, ids, w_qkv, w_out, rows)


def sum_kernel(round_ref, seat_ref, most_ref, rows_ref, out_ref):
    chunk = out_ref.shape[0]
    first = SEATS * round_ref[0].astype(F32)
    owner = seat_ref[0:1, :]
    seat = seat_ref[1:2, :] - first
    seated = (seat >= 0.0) & (seat < float(SEATS))
    code = jnp.where(seated, owner * float(SEAT) + seat, -1.0).astype(jnp.int32)
    mine = iota((chunk, 1), 0) + pl.program_id(0) * chunk
    member = jnp.where(mine == code, 1.0, 0.0).astype(BF)
    sums = mm(member, rows_ref[...])
    tags = mm(seat_ref[...].astype(BF), member, NT)
    rounds = jnp.floor((most_ref[0:1, :] + (SEATS - 1.0)) / float(SEATS))
    line = iota((SEAT - SEATS, SEAT), 0)
    for d in range(chunk // SEAT):
        low = d * SEAT
        out_ref[low : low + SEATS, :] = sums[low : low + SEATS].astype(BF)
        origin = jnp.where(line == 0, tags[2:3, low : low + SEAT], jnp.where(line == 1, rounds, 0.0))
        place = jnp.where(line == 0, tags[3:4, low : low + SEAT], 0.0)
        out_ref[low + SEATS : low + SEAT, :] = jnp.concatenate([origin, place], axis=1).astype(BF)


def sum_runs(step, seats, most, rows, devices):
    count, width = rows.shape
    total = devices * SEAT
    chunk = 512
    fixed = lambda i: (0, 0)
    return pl.pallas_call(
        sum_kernel,
        grid=(total // chunk,),
        out_shape=jax.ShapeDtypeStruct((total, width), BF),
        in_specs=[
            SMEM,
            pl.BlockSpec((8, count), fixed),
            pl.BlockSpec((8, 128), fixed),
            pl.BlockSpec((count, width), fixed),
        ],
        out_specs=pl.BlockSpec((chunk, width), lambda i: (i, 0)),
        compiler_params=ROOM,
        cost_estimate=cost(2 * total * count * width, 4 * count * width),
    )(step, seats, most, rows)


def fold_kernel(per_owner, pieces_ref, before_ref, out_ref, target):
    step = pl.program_id(0)
    parents = out_ref.shape[0]
    chunk = pieces_ref.shape[0]

    @pl.when(step == 0)
    def _():
        out_ref[...] = before_ref[...]

    valid = iota((1, SEAT), 1) < SEATS
    for h in range(chunk // SEAT):
        tag = pieces_ref[h * SEAT + SEATS : (h + 1) * SEAT, :].astype(F32)[0:1]
        where = tag[:, :SEAT] * float(per_owner) + tag[:, SEAT:]
        target[0:1, h * SEAT : (h + 1) * SEAT] = jnp.where(valid, where, -1.0).astype(jnp.int32)
    member = jnp.where(iota((parents, 1), 0) == target[0:1, :], 1.0, 0.0).astype(BF)
    out_ref[...] += mm(member, pieces_ref[...])


def fold_pieces(pieces, before, per_owner):
    parents, width = before.shape
    chunk = min(2048, pieces.shape[0])
    fixed = lambda i: (0, 0)
    return pl.pallas_call(
        functools.partial(fold_kernel, per_owner),
        grid=(pieces.shape[0] // chunk,),
        out_shape=jax.ShapeDtypeStruct((parents, width), F32),
        in_specs=[
            pl.BlockSpec((chunk, width), lambda i: (i, 0)),
            pl.BlockSpec((parents, width), fixed),
        ],
        out_specs=pl.BlockSpec((parents, width), fixed),
        scratch_shapes=[pltpu.VMEM((8, chunk), jnp.int32)],
        compiler_params=ROOM,
        cost_estimate=cost(2 * parents * pieces.size, 4 * pieces.size),
    )(pieces, before)


def pool_kernel(
    in_ref, length_ref, w_ref, gain_ref, shift_ref, cot_ref, pooled_ref, back_ref, weight_ref, norm_ref, acc, sums
):
    step = pl.program_id(0)

    @pl.when(step == 0)
    def _():
        acc[...] = jnp.zeros_like(acc)
        sums[...] = jnp.zeros_like(sums)

    lengths = jnp.concatenate([length_ref[...]] * (in_ref.shape[1] // 128), axis=1)
    parent_in = (in_ref[...] / lengths).astype(BF)
    w_pool = w_ref[...]
    gain = gain_ref[...]
    projected = mm(parent_in, w_pool)
    centred = projected - jnp.mean(projected, axis=-1, keepdims=True)
    variance = jnp.mean(centred * centred, axis=-1, keepdims=True)
    inv_std = lax.rsqrt(variance + norm_eps)
    normed = centred * inv_std
    shifted = normed * gain + shift_ref[...]
    normal_cdf = 0.5 * (1.0 + lax.erf(shifted * inv_sqrt_two))
    pooled_ref[...] = (shifted * normal_cdf).astype(BF)
    grad_act = cot_ref[...].astype(F32) * (
        normal_cdf + shifted * jnp.exp(-0.5 * shifted * shifted) * inv_sqrt_tau
    )
    sums[0:1, :] += jnp.sum(grad_act * normed, axis=0, keepdims=True)
    sums[1:2, :] += jnp.sum(grad_act, axis=0, keepdims=True)
    scaled = grad_act * gain
    grad_proj = (
        (
            scaled
            - jnp.mean(scaled, axis=-1, keepdims=True)
            - normed * jnp.mean(scaled * normed, axis=-1, keepdims=True)
        )
        * inv_std
    ).astype(BF)
    acc[...] += mm(parent_in, grad_proj, TN)
    back_ref[...] = mm(grad_proj, w_pool, NT).astype(BF)

    @pl.when(step == pl.num_programs(0) - 1)
    def _():
        weight_ref[...] = acc[...].astype(BF)
        norm_ref[...] = sums[...]


def pool(parent_sum, length, w_pool, gain, shift, cotangent):
    parents, width = parent_sum.shape
    wide = w_pool.shape[1]
    chunk = 256
    fixed = lambda i: (0, 0)
    along = lambda i: (i, 0)
    return pl.pallas_call(
        pool_kernel,
        grid=(parents // chunk,),
        out_shape=(
            jax.ShapeDtypeStruct((parents, wide), BF),
            jax.ShapeDtypeStruct((parents, width), BF),
            jax.ShapeDtypeStruct((width, wide), BF),
            jax.ShapeDtypeStruct((8, wide), F32),
        ),
        in_specs=[
            pl.BlockSpec((chunk, width), along),
            pl.BlockSpec((chunk, 128), along),
            pl.BlockSpec((width, wide), fixed),
            pl.BlockSpec((1, wide), fixed),
            pl.BlockSpec((1, wide), fixed),
            pl.BlockSpec((chunk, wide), along),
        ],
        out_specs=(
            pl.BlockSpec((chunk, wide), along),
            pl.BlockSpec((chunk, width), along),
            pl.BlockSpec((width, wide), fixed),
            pl.BlockSpec((8, wide), fixed),
        ),
        scratch_shapes=[pltpu.VMEM((width, wide), F32), pltpu.VMEM((8, wide), F32)],
        compiler_params=ROOM,
        cost_estimate=cost(6 * parents * width * wide, 8 * parents * wide, 2 * parents * wide),
    )(parent_sum, length, w_pool, gain, shift, cotangent)


def spread_kernel(span_ref, grad_ref, out_ref, share):
    step = pl.program_id(0)
    chunk = out_ref.shape[0]
    parents, width = share.shape

    @pl.when(step == 0)
    def _():
        pick = jnp.where(iota((8, width), 0) == 2, 1.0, 0.0).astype(BF)
        lengths = mm(jnp.minimum(span_ref[...], 64).astype(F32).astype(BF), pick, TN)
        share[...] = (grad_ref[...].astype(F32) / lengths).astype(BF)

    row = iota((chunk, parents), 0) + step * chunk
    inside = (row >= span_ref[0:1, :]) & (row < span_ref[1:2, :])
    out_ref[...] = mm(jnp.where(inside, 1.0, 0.0).astype(BF), share[...]).astype(BF)


def spread_grads(span, grad_back, rows):
    parents, width = grad_back.shape
    chunk = 512
    fixed = lambda i: (0, 0)
    return pl.pallas_call(
        spread_kernel,
        grid=(rows // chunk,),
        out_shape=jax.ShapeDtypeStruct((rows, width), BF),
        in_specs=[
            pl.BlockSpec((8, parents), fixed),
            pl.BlockSpec((parents, width), fixed),
        ],
        out_specs=pl.BlockSpec((chunk, width), lambda i: (i, 0)),
        scratch_shapes=[pltpu.VMEM((parents, width), BF)],
        compiler_params=ROOM,
        cost_estimate=cost(2 * rows * parents * width, 4 * rows * width),
    )(span, grad_back)


def swap(parts):
    return lax.all_to_all(parts, "pts", split_axis=0, concat_axis=0, tiled=True)


def exchange(rows, devices):
    return swap(rows.reshape(devices, rows.shape[0] // devices, rows.shape[1])).reshape(rows.shape)


def received_index(codes, blocks, capacity):
    devices = codes.shape[0]
    mine = codes // blocks == lax.axis_index("pts")
    slots = codes % blocks
    lane = jnp.arange(blocks)
    rank = jnp.sum(mine[:, None, :] & (lane[None, :] < lane[:, None])[None], axis=2)
    index = jnp.arange(devices)[:, None] * capacity + rank
    both = index * blocks + lane[None, :]
    hit = mine[:, :, None] & (slots[:, :, None] == lane[None, None, :])
    both = jnp.sum(jnp.where(hit, both[:, :, None], 0), axis=(0, 1)).astype(jnp.int32)
    return both // blocks, both % blocks


def key_windows(patch_ids):
    tiles, span = patch_ids.shape
    patch = jnp.arange(PATCHES + 1)
    starts = jnp.sum(patch_ids[:, None, :] < patch[None, :, None], axis=2)
    by_block = patch_ids.reshape(tiles, span // ROWS, ROWS)
    first, last = by_block[:, :, 0], by_block[:, :, -1]
    pick = lambda which: jnp.sum(
        jnp.where(which[:, :, None] == patch[None, None, :], starts[:, None, :], 0), axis=2
    )
    low = pick(first) // ROWS * ROWS
    count = (pick(last + 1) - low + WINDOW - 1) // WINDOW
    low = jnp.minimum(low, span - count * WINDOW)
    return low.reshape(-1).astype(jnp.int32), count.reshape(-1).astype(jnp.int32)


def local(
    points,
    hil_dest,
    hil_slot,
    patch_ids,
    child_counts,
    parent_order,
    w_qkv,
    w_out,
    w_pool,
    norm_gain,
    norm_shift,
    cotangent,
):
    devices = lax.axis_size("pts")
    blocks = hil_dest.shape[0]
    rows, width = points.shape
    wide = w_pool.shape[1]
    parents = child_counts.shape[1]
    per_owner = parents // devices
    capacity = (blocks + devices - 1) // devices

    info, span = order_tables(child_counts, parent_order, hil_dest, hil_slot, devices)
    info = swap(info)
    payload = pack_blocks(hil_dest, points, devices, capacity)
    received = exchange(payload, devices)
    index, block = received_index(info[:, parents // 128, :blocks], blocks, capacity)
    seats, most = seat_rows(
        index // capacity, block, info.reshape(devices * INFO, 128), per_owner
    )
    low, count = key_windows(patch_ids)
    lengths = lax.dynamic_slice_in_dim(
        info[:, : parents // 128].reshape(devices, parents),
        lax.axis_index("pts") * per_owner,
        per_owner,
        axis=1,
    ).reshape(parents, 1) % 16
    lengths = jnp.broadcast_to(lengths.astype(F32), (parents, 128))
    index, low, count, seats, most, lengths = lax.optimization_barrier(
        (index, low, count, seats, most, lengths)
    )
    mixed = attend(index, low, count, patch_ids, w_qkv, w_out, received)

    def turn(step, before):
        sent = sum_runs(step.reshape(1), seats, most, mixed, devices)
        pieces = exchange(sent, devices)
        needed = jnp.max(pieces.reshape(devices, SEAT, width)[:, SEATS + 1, 0].astype(F32))
        return needed.astype(jnp.int32), fold_pieces(pieces, before, per_owner)

    rounds, parent_sum = turn(jnp.int32(0), jnp.zeros((parents, width), F32))
    _, parent_sum = lax.while_loop(
        lambda carry: carry[0] < rounds,
        lambda carry: (carry[0] + 1, turn(carry[0], carry[1])[1]),
        (jnp.int32(1), parent_sum),
    )
    pooled, back, weight, norm = pool(
        parent_sum, lengths, w_pool, norm_gain[None], norm_shift[None], cotangent
    )
    norm_high = norm.astype(BF)
    norm_low = (norm - norm_high.astype(F32)).astype(BF)
    norm_parts = jnp.concatenate([norm_high[:2], norm_low[:2]], axis=0).reshape(1, -1, width)
    outgoing = jnp.concatenate(
        [
            back.reshape(devices, -1, width),
            weight.reshape(devices, -1, width),
            jnp.broadcast_to(norm_parts, (devices,) + norm_parts.shape[1:]),
        ],
        axis=1,
    )
    arrived = swap(outgoing)
    weight_rows = width * wide // width // devices
    grad_back = arrived[:, :per_owner].reshape(parents, width)
    weight_sum = jnp.sum(arrived[:, per_owner : per_owner + weight_rows].astype(F32), axis=0)
    norm_sum = jnp.sum(arrived[:, per_owner + weight_rows :].astype(F32), axis=0)
    norm_sum = norm_sum.reshape(4, wide)
    grad_norm = norm_sum[:2] + norm_sum[2:]
    shared = jnp.broadcast_to(weight_sum.astype(BF)[None], (devices,) + weight_sum.shape)
    grad_weight = swap(shared).reshape(width, wide).astype(F32)
    grad_points = spread_grads(span, grad_back, rows)
    return (pooled, grad_points, grad_weight, grad_norm)


def solution(mesh):
    in_specs = (
        P(("grp", "pts"), None),
        P(("grp", "pts")),
        P(("grp", "pts")),
        P(("grp", "pts"), None),
        P(("grp", "pts"), None),
        P(("grp", "pts"), None),
        P(),
        P(),
        P(),
        P(),
        P(),
        P(("grp", "pts"), None),
    )
    out_specs = (P(("grp", "pts"), None), P(("grp", "pts"), None), P("grp", None), P("grp", None))
    return jax.shard_map(local, mesh=mesh, in_specs=in_specs, out_specs=out_specs, check_vma=False)
```

time: 350 us -> 269 us (0.77)
  Pallas kernels: 216 us -> 142 us
  blocking collectives: 94.3 us -> 28.1 us
  waiting for transfers between devices: 3.78 us -> 57.5 us
  starting transfers between devices: 21.5 us -> 26.6 us
    pallas_call x6, Pallas kernels: 201 us -> 130 us  [the longest x1 102 us: attend(): pl.pallas_call(attend_kernel, out_shape=jax.ShapeDtypeStruct((tiles * spa...]
    all_to_all x4, waiting for transfers between devices: 3.78 us -> 57.5 us  [swap(): return lax.all_to_all(parts, 'pts', split_axis=0, concat_axis=0, tiled=True)]
    unnamed x1 -> x0, blocking collectives: 47.9 us -> none
    all_to_all x2 -> x1, blocking collectives: 46.4 us -> 28.1 us  [swap(): return lax.all_to_all(parts, 'pts', split_axis=0, concat_axis=0, tiled=True)]
    all_to_all x4, starting transfers between devices: 21.5 us -> 26.6 us  [swap(): return lax.all_to_all(parts, 'pts', split_axis=0, concat_axis=0, tiled=True)]
    unnamed x41 -> x33, local copies, waits for them, and re-layouts: 7.57 us -> 7.33 us
  transfers between devices with their start and end apart: 4 -> 4, of which waited for: 2 -> 4; matrix products, arithmetic and copies ran while one was open for 1% -> 1% of each run, Pallas kernels for 32% -> 7%
where the time goes in v2:
time: 269 us; the launch traced here: 268 us
  Pallas kernels  142 us (53%)
  waiting for transfers between devices  57.5 us (21%)
  blocking collectives  28.1 us (10%)
  starting transfers between devices  26.6 us (10%)
  local copies, waits for them, and re-layouts  10.3 us (4%)
    pallas_call x1, Pallas kernels, attend(): pl.pallas_call(attend_kernel, out_shape=jax.ShapeDtypeStruct((tiles * spa...  102 us
    all_to_all x4, waiting for transfers between devices, swap(): return lax.all_to_all(parts, 'pts', split_axis=0, concat_axis=0, tiled=True)  57.5 us
    all_to_all x1, blocking collectives, swap(): return lax.all_to_all(parts, 'pts', split_axis=0, concat_axis=0, tiled=True)  28.1 us
    all_to_all x4, starting transfers between devices, swap(): return lax.all_to_all(parts, 'pts', split_axis=0, concat_axis=0, tiled=True)  26.6 us
    pallas_call x1, Pallas kernels, seat_rows(): pl.pallas_call(functools.partial(seat_kernel, per_owner), out_shape=(jax....  12.2 us
    pallas_call x1, Pallas kernels, sum_runs(): pl.pallas_call(sum_kernel, grid=(total // chunk,), out_shape=jax.ShapeDty...  10.2 us
    unnamed x33, local copies, waits for them, and re-layouts  7.33 us
    pallas_call x1, Pallas kernels, pool(): pl.pallas_call(pool_kernel, grid=(parents // chunk,), out_shape=(jax.Shap...  6.82 us
  transfers between devices with their start and end apart: 4, of which 4 were waited for; matrix products, arithmetic and copies ran while one was open for 1% of the time, Pallas kernels for 7%

profile of v2, /device:TPU:0, one launch (start us, length us, event | category | flops | bytes accessed | tf_op | source)
XLA Modules:
  0.0 267.9 jit_solution(4919809321760718346)
XLA Ops:
  0.6 0.0 copy-start.2
  0.6 0.6 copy-done.2
  1.3 0.7 copy-done.8
  2.0 0.7 copy-done.9
  2.7 0.7 copy-done.12
  3.3 1.3 shard_map.147
  4.6 7.4 %all-to-all-start.1 = ((s32[16,16,128]{2,1,0:T(8,128)}), s32[16,16,128]{2,1,0:T(8,128)S(1)}, u32[]{:S(2)}, u32[]{:S(2)}) async-start(s32[16,16,128]{2,1,0:T(8,128)} %get-tuple-element.51), calls=%async_computation.1 | async-start | bytes 262144 | tf_op jit(solution)/shard_map/all_to_all | solution.py:503
  12.0 1.6 copy-done
  13.6 0.7 copy-done.3
  14.3 1.9 shard_map.149
  16.2 3.7 %all-to-all-done.1 = s32[16,16,128]{2,1,0:T(8,128)S(1)} async-done(((s32[16,16,128]{2,1,0:T(8,128)}), s32[16,16,128]{2,1,0:T(8,128)S(1)}, u32[]{:S(2)}, u32[]{:S(2)}) %all-to-all-start.1) | async-done | bytes 131104 | tf_op jit(solution)/shard_map/all_to_all | solution.py:503
  20.0 3.9 %all-to-all-start.2 = ((bf16[16,256,256]{2,1,0:T(8,128)(2,1)}), bf16[16,256,256]{2,1,0:T(8,128)(2,1)S(1)}, u32[]{:S(2)}, u32[]{:S(2)}) async-start(bf16[16,256,256]{2,1,0:T(8,128)(2,1)} %bitcast.9), calls=%async_computation.2 | async-start | bytes 4194304 | tf_op jit(solution)/shard_map/all_to_all | solution.py:503
  23.8 0.1 fusion.9
  23.9 0.1 copy.23
  24.0 0.1 copy.27
  24.1 0.2 convert_reduce_fusion.2
  24.3 0.1 select_reduce_fusion.1
  24.4 0.1 reduce_sum.74
  24.5 0.1 reduce_sum.76
  24.6 0.1 fusion.2
  24.7 0.1 constant_dynamic-slice_fusion
  24.8 0.1 reshape.192
  24.9 0.3 convert_reduce_fusion
  25.2 0.1 add_select_fusion
  25.3 0.3 select_reduce_fusion
  25.6 12.2 %shard_map.148 = (f32[8,4096]{1,0:T(8,128)S(1)}, f32[8,128]{1,0:T(8,128)S(1)}) custom-call(s32[32]{0:T(128)S(1)} %get-tuple-element.80.source_ref, s32[32]{0:T(128)S(1)} %get-tuple-element.86.block_ref, s32[256,128]{1,0:T(8,128)S(1)} %bitcast.39), custom_call_target="tpu_custom_call" | custom-call | flops 167772160 | bytes 32768 | tf_op jit(solution)/shard_map/pallas_call | solution.py:180
  37.8 0.2 broadcast_in_dim.84.length_ref
  38.0 26.9 %all-to-all-done.2 = bf16[16,256,256]{2,1,0:T(8,128)(2,1)S(1)} async-done(((bf16[16,256,256]{2,1,0:T(8,128)(2,1)}), bf16[16,256,256]{2,1,0:T(8,128)(2,1)S(1)}, u32[]{:S(2)}, u32[]{:S(2)}) %all-to-all-start.2) | async-done | bytes 2097184 | tf_op jit(solution)/shard_map/all_to_all | solution.py:503
  64.9 101.8 %shard_map.150.rows_ref = bf16[4096,256]{1,0:T(8,128)(2,1)S(1)} custom-call(s32[32]{0:T(128)S(1)} %get-tuple-element.56.index_ref, s32[32]{0:T(128)S(1)} %get-tuple-element.57.low_ref, s32[32]{0:T(128)S(1)} %get-tuple-element.58.count_ref, s32[4,1024]{1,0:T(4,128)S(1)} %copy-done.1, bf16[256,768]{1,0:T(8,128)(2,1)S(1)} %copy-done.5, ...), custom_call_target="tpu_custom_call" | custom-call | flops 34359738368 | bytes 4194304 | tf_op jit(solution)/shard_map/pallas_call | solution.py:290
  166.7 0.0 copy-start.13
  166.7 10.2 %shard_map.151 = bf16[2048,256]{1,0:T(8,128)(2,1)} custom-call(s32[1]{0:T(128)} %constant.104.clone.1.round_ref, f32[8,4096]{1,0:T(8,128)S(1)} %get-tuple-element.130.seat_ref, f32[8,128]{1,0:T(8,128)S(1)} %get-tuple-element.131.most_ref, bf16[4096,256]{1,0:T(8,128)(2,1)S(1)} %shard_map.150.rows_ref), custom_call_target="tpu_custom_call" | custom-call | flops 4294967296 | bytes 4194304 | tf_op jit(solution)/shard_map/pallas_call | solution.py:334
  177.0 11.2 %all-to-all-start.3 = ((bf16[16,128,256]{2,1,0:T(8,128)(2,1)}), bf16[16,128,256]{2,1,0:T(8,128)(2,1)S(1)}, u32[]{:S(2)}, u32[]{:S(2)}) async-start(bf16[16,128,256]{2,1,0:T(8,128)(2,1)} %bitcast.11), calls=%async_computation.3 | async-start | bytes 2097152 | tf_op jit(solution)/shard_map/all_to_all | solution.py:503
  188.2 22.9 %all-to-all-done.3 = bf16[16,128,256]{2,1,0:T(8,128)(2,1)S(1)} async-done(((bf16[16,128,256]{2,1,0:T(8,128)(2,1)}), bf16[16,128,256]{2,1,0:T(8,128)(2,1)S(1)}, u32[]{:S(2)}, u32[]{:S(2)}) %all-to-all-start.3) | async-done | bytes 1048608 | tf_op jit(solution)/shard_map/all_to_all | solution.py:503
  211.1 0.6 slice_reduce_fusion.1
  212.4 0.1 broadcast_in_dim.85.before_ref
  212.5 2.2 shard_map.152
  214.7 0.9 copy-done.6
  215.6 1.2 copy-done.4
  216.9 6.8 %shard_map.153 = (bf16[1024,512]{1,0:T(8,128)(2,1)}, bf16[1024,256]{1,0:T(8,128)(2,1)S(1)}, bf16[256,512]{1,0:T(8,128)(2,1)S(1)}, f32[8,512]{1,0:T(8,128)S(1)}) custom-call(f32[1024,256]{1,0:T(8,128)} %get-tuple-element.59.in_ref, f32[1024,128]{1,0:T(8,128)S(1)} %broadcast_in_dim.84.length_ref, bf16[256,512]{1,0:T(8,128)(2,1)S(1)} %copy-done.6, ...), custom_call_target="tpu_custom_call" | custom-call | flops 805306368 | bytes 4194304 | tf_op jit(solution)/shard_map/pallas_call | solution.py:438
  223.7 0.1 reshape.198
  223.9 0.1 pad_maximum_fusion
  223.9 28.1 %all_to_all.31 = bf16[16,104,256]{2,1,0:T(8,128)(2,1)S(1)} all-to-all(bf16[16,104,256]{2,1,0:T(8,128)(2,1)S(1)} %pad_maximum_fusion), channel_id=1, replica_groups=mesh['grp'=2,'pts'=16] {'pts'}, dimensions={0} | all-to-all | bytes 1703936 | tf_op jit(solution)/shard_map/all_to_all | solution.py:503
  252.0 0.7 broadcast_in_dim.90
  252.8 4.2 %all-to-all-start.5 = ((bf16[16,32,256]{2,1,0:T(8,128)(2,1)}), bf16[16,32,256]{2,1,0:T(8,128)(2,1)S(1)}, u32[]{:S(2)}, u32[]{:S(2)}) async-start(bf16[16,32,256]{2,1,0:T(8,128)(2,1)} %broadcast_in_dim.90), calls=%async_computation.5 | async-start | bytes 524288 | tf_op jit(solution)/shard_map/all_to_all | solution.py:503
  257.0 0.6 add.99
  257.7 5.4 %shard_map.154 = bf16[4096,256]{1,0:T(8,128)(2,1)} custom-call(s32[8,1024]{1,0:T(8,128)S(1)} %get-tuple-element.62.span_ref, bf16[1024,256]{1,0:T(8,128)(2,1)S(1)} %bitcast.38), custom_call_target="tpu_custom_call" | custom-call | flops 2147483648 | bytes 4194304 | tf_op jit(solution)/shard_map/pallas_call | solution.py:487
  263.1 3.9 %all-to-all-done.5 = bf16[16,32,256]{2,1,0:T(8,128)(2,1)S(1)} async-done(((bf16[16,32,256]{2,1,0:T(8,128)(2,1)}), bf16[16,32,256]{2,1,0:T(8,128)(2,1)S(1)}, u32[]{:S(2)}, u32[]{:S(2)}) %all-to-all-start.5) | async-done | bytes 262176 | tf_op jit(solution)/shard_map/all_to_all | solution.py:503
  267.0 0.9 reshape.200
  (40 shorter events, 0.3 us)
Async XLA Ops:
  0.6 0.7 copy-start.2
  1.3 0.7 copy-start.8
  2.0 0.7 copy-start.9
  2.7 0.7 copy-start.12
  4.6 15.3 %all-to-all-start.1 = ((s32[16,16,128]{2,1,0:T(8,128)}), s32[16,16,128]{2,1,0:T(8,128)S(1)}, u32[]{:S(2)}, u32[]{:S(2)}) async-start(s32[16,16,128]{2,1,0:T(8,128)} %get-tuple-element.51), calls=%async_computation.1 | async-start | bytes 262144 | tf_op jit(solution)/shard_map/all_to_all | solution.py:503
  12.0 1.6 copy-start
  13.6 0.7 copy-start.3
  20.0 3.9 %copy-start.1 = (s32[4,1024]{1,0:T(4,128)S(1)}, s32[4,1024]{1,0:T(4,128)}, u32[]{:S(2)}) copy-start(s32[4,1024]{1,0:T(4,128)} %ids_ref.1) | copy-start | bytes 49156
  20.0 44.9 %copy-start.5 = (bf16[256,768]{1,0:T(8,128)(2,1)S(1)}, bf16[256,768]{1,0:T(8,128)(2,1)}, u32[]{:S(2)}) copy-start(bf16[256,768]{1,0:T(8,128)(2,1)} %w_ref.2) | copy-start | bytes 1179652
  20.0 44.9 %copy-start.7 = (bf16[256,256]{1,0:T(8,128)(2,1)S(1)}, bf16[256,256]{1,0:T(8,128)(2,1)}, u32[]{:S(2)}) copy-start(bf16[256,256]{1,0:T(8,128)(2,1)} %wo_ref.1) | copy-start | bytes 393220
  20.0 44.9 %all-to-all-start.2 = ((bf16[16,256,256]{2,1,0:T(8,128)(2,1)}), bf16[16,256,256]{2,1,0:T(8,128)(2,1)S(1)}, u32[]{:S(2)}, u32[]{:S(2)}) async-start(bf16[16,256,256]{2,1,0:T(8,128)(2,1)} %bitcast.9), calls=%async_computation.2 | async-start | bytes 4194304 | tf_op jit(solution)/shard_map/all_to_all | solution.py:503
  166.7 10.3 %copy-start.13 = (bf16[4096,256]{1,0:T(8,128)(2,1)}, bf16[4096,256]{1,0:T(8,128)(2,1)S(1)}, u32[]{:S(2)}) copy-start(bf16[4096,256]{1,0:T(8,128)(2,1)S(1)} %shard_map.150.rows_ref) | copy-start | bytes 6291460
  177.0 34.1 %all-to-all-start.3 = ((bf16[16,128,256]{2,1,0:T(8,128)(2,1)}), bf16[16,128,256]{2,1,0:T(8,128)(2,1)S(1)}, u32[]{:S(2)}, u32[]{:S(2)}) async-start(bf16[16,128,256]{2,1,0:T(8,128)(2,1)} %bitcast.11), calls=%async_computation.3 | async-start | bytes 2097152 | tf_op jit(solution)/shard_map/all_to_all | solution.py:503
  214.7 0.9 copy-start.6
  214.7 1.0 copy-start.10
  214.7 1.0 copy-start.11
  215.6 1.2 copy-start.4
  252.8 14.3 %all-to-all-start.5 = ((bf16[16,32,256]{2,1,0:T(8,128)(2,1)}), bf16[16,32,256]{2,1,0:T(8,128)(2,1)S(1)}, u32[]{:S(2)}, u32[]{:S(2)}) async-start(bf16[16,32,256]{2,1,0:T(8,128)(2,1)} %broadcast_in_dim.90), calls=%async_computation.5 | async-start | bytes 524288 | tf_op jit(solution)/shard_map/all_to_all | solution.py:503

commit v3 on v2

--- a/solution.py
+++ b/solution.py
@@ -14,6 +14,9 @@
 SEAT = 128
 SEATS = 112
 INFO = 16
+ALIGN = 16
+CHUNK = 512
+FIELDS = 6
 WINDOW = 256
 PATCHES = 4
 FAR = 2.0**100
@@ -33,6 +36,7 @@
 SMEM = pl.BlockSpec(memory_space=pltpu.SMEM)
 ANY = pl.BlockSpec(memory_space=pl.ANY)
 ROOM = pltpu.CompilerParams(vmem_limit_bytes=48 << 20)
+FULL = pltpu.CompilerParams(vmem_limit_bytes=60 << 20)
 
 
 def iota(shape, dim):
@@ -49,7 +53,20 @@
     )
 
 
-def pack_kernel(capacity, dest_ref, points_ref, payload_ref, used, sem):
+def front_kernel(
+    capacity,
+    dest_ref,
+    counts_ref,
+    order_ref,
+    dest_row_ref,
+    slot_row_ref,
+    points_ref,
+    payload_ref,
+    info_ref,
+    span_ref,
+    used,
+    sem,
+):
     blocks = dest_ref.shape[0]
 
     def clear(d, _):
@@ -70,25 +87,8 @@
         return 0
 
     lax.fori_loop(0, blocks, send, 0)
-    whole = pl.ds(0, blocks * ROWS)
-    pltpu.make_async_copy(points_ref.at[whole], payload_ref.at[whole], sem).wait()
-
-
-def pack_blocks(hil_dest, points, devices, capacity):
-    return pl.pallas_call(
-        functools.partial(pack_kernel, capacity),
-        out_shape=jax.ShapeDtypeStruct((devices * capacity * ROWS, points.shape[1]), BF),
-        in_specs=[SMEM, HBM],
-        out_specs=HBM,
-        scratch_shapes=[pltpu.SMEM((devices,), jnp.int32), pltpu.SemaphoreType.DMA],
-        compiler_params=ROOM,
-        cost_estimate=cost(0, 4 * points.size),
-    )(hil_dest, points)
-
-
-def order_kernel(counts_ref, order_ref, dest_ref, slot_ref, info_ref, span_ref, code):
+
     parents = counts_ref.shape[1]
-    blocks = dest_ref.shape[1]
     counts = jnp.broadcast_to(counts_ref[...], (8, parents)).astype(F32)
     upper = jnp.where(iota((parents, parents), 0) <= iota((parents, parents), 1), 1.0, 0.0)
     starts = mm(counts.astype(BF), upper.astype(BF)) - counts
@@ -101,32 +101,48 @@
     length = ordered[2:3]
     span_ref[...] = jnp.where(which == 0, first, jnp.where(which == 1, first + length, length))
     both = 16 * first + length
-    code[...] = jnp.zeros_like(code)
-    code[0:1, :blocks] = dest_ref[...] * blocks + slot_ref[...]
-    tile = jnp.concatenate(
-        [both[:, i * 128 : (i + 1) * 128] for i in range(parents // 128)] + [code[...]], axis=0
-    )
-    for d in range(info_ref.shape[0]):
-        info_ref[d] = tile
-
-
-def order_tables(child_counts, parent_order, hil_dest, hil_slot, devices):
+    lines = parents // 128
+    for i in range(lines):
+        info_ref[i : i + 1, :] = both[:, i * 128 : (i + 1) * 128]
+    info_ref[lines:, :] = jnp.zeros((INFO - lines, 128), jnp.int32)
+    info_ref[lines : lines + 1, :blocks] = dest_row_ref[...] * blocks + slot_row_ref[...]
+
+    whole = pl.ds(0, blocks * ROWS)
+    pltpu.make_async_copy(points_ref.at[whole], payload_ref.at[whole], sem).wait()
+
+
+def front(child_counts, parent_order, hil_dest, hil_slot, points, devices, capacity):
     parents = child_counts.shape[1]
     return pl.pallas_call(
-        order_kernel,
+        functools.partial(front_kernel, capacity),
         out_shape=(
-            jax.ShapeDtypeStruct((devices, INFO, 128), jnp.int32),
+            jax.ShapeDtypeStruct((devices * capacity * ROWS, points.shape[1]), BF),
+            jax.ShapeDtypeStruct((INFO, 128), jnp.int32),
             jax.ShapeDtypeStruct((8, parents), jnp.int32),
         ),
-        in_specs=[VMEM] * 4,
-        out_specs=(VMEM, VMEM),
-        scratch_shapes=[pltpu.VMEM((INFO - parents // 128, 128), jnp.int32)],
-        compiler_params=ROOM,
-        cost_estimate=cost(32 * parents * parents, 8 * parents),
-    )(child_counts, parent_order, hil_dest[None], hil_slot[None])
-
-
-def seat_kernel(per_owner, source_ref, block_ref, info_ref, seat_ref, most_ref, owner, place, origin):
+        in_specs=[SMEM, VMEM, VMEM, VMEM, VMEM, HBM],
+        out_specs=(HBM, VMEM, VMEM),
+        scratch_shapes=[pltpu.SMEM((devices,), jnp.int32), pltpu.SemaphoreType.DMA],
+        compiler_params=FULL,
+        cost_estimate=cost(32 * parents * parents, 4 * points.size),
+    )(hil_dest, child_counts, parent_order, hil_dest[None], hil_slot[None], points)
+
+
+def seat_kernel(
+    per_owner,
+    source_ref,
+    entry_ref,
+    block_ref,
+    info_ref,
+    table_ref,
+    local_ref,
+    base_ref,
+    most_ref,
+    owner,
+    place,
+    origin,
+    seats,
+):
     blocks = owner.shape[0]
     parents = 128 * 8
     devices = info_ref.shape[0] // INFO
@@ -136,8 +152,8 @@
     fields = fields.astype(F32).astype(BF)
 
     def one(v, _):
-        source = source_ref[v]
-        packed = info_ref[pl.ds(pl.multiple_of(source * INFO, INFO), 8), :]
+        entry = entry_ref[v]
+        packed = info_ref[pl.ds(pl.multiple_of(entry * INFO, INFO), 8), :]
         line = jnp.concatenate([packed[i : i + 1] for i in range(8)], axis=1)
         first = line // 16
         row = block_ref[v] * ROWS + iota((ROWS, parents), 0)
@@ -145,18 +161,18 @@
         found = mm(fields, jnp.where(inside, 1.0, 0.0).astype(BF), NT)
         owner[pl.ds(v, 1), :] = found[0:1]
         place[pl.ds(v, 1), :] = found[1:2]
-        origin[pl.ds(v, 1), :] = jnp.full((1, ROWS), source, jnp.int32).astype(F32)
+        origin[pl.ds(v, 1), :] = jnp.full((1, ROWS), source_ref[v], jnp.int32).astype(F32)
         return 0
 
     lax.fori_loop(0, blocks, one, 0)
     own = owner[...]
-    own_place = place[...]
-    run = own * per_owner + own_place
+    run = own * per_owner + place[...]
     opens = (iota((blocks, ROWS), 1) == 0) | (run != pltpu.roll(run, 1, 1))
     opened = jnp.where(opens, 1.0, 0.0)
     upper = jnp.where(iota((ROWS, ROWS), 0) <= iota((ROWS, ROWS), 1), 1.0, 0.0).astype(BF)
     every = jnp.ones((ROWS, ROWS), BF)
     before = jnp.where(iota((blocks, blocks), 1) < iota((blocks, blocks), 0), 1.0, 0.0).astype(BF)
+    local_ref[...] = (mm(opened.astype(BF), upper) - 1.0).astype(jnp.int32)
 
     def count(e, carry):
         seat, most = carry
@@ -167,29 +183,115 @@
 
     zero = jnp.zeros((blocks, ROWS), F32)
     seat, most = lax.fori_loop(0, devices, count, (zero, zero))
-    seat_ref[...] = jnp.zeros_like(seat_ref)
-    for i, value in enumerate((own, seat, opened * origin[...], opened * own_place)):
-        for v in range(blocks):
-            seat_ref[i : i + 1, v * ROWS : (v + 1) * ROWS] = value[v : v + 1]
+    seats[...] = seat
     most_ref[...] = jnp.full((8, 128), jnp.max(most), F32)
-
-
-def seat_rows(source, block, info, per_owner):
+    table_ref[...] = jnp.zeros_like(table_ref)
+    field = iota((ROWS, ROWS), 0)
+
+    def lay(v, base):
+        base = pl.multiple_of(base, ALIGN)
+        base_ref[v] = base
+        at = pl.ds(v, 1)
+        local = local_ref[at, :]
+        seat = seats[at, :]
+        coarse = jnp.floor(seat * (1.0 / 64.0))
+        lines = (owner[at, :], coarse, seat - 64.0 * coarse, origin[at, :], place[at, :])
+        values = jnp.ones((ROWS, ROWS), F32)
+        for i, line in enumerate(lines):
+            values = jnp.where(field == i, line, values)
+        previous = jnp.where(iota((1, ROWS), 1) == 0, -1, pltpu.roll(local, 1, 1))
+        begins = (field == local) & (local != previous)
+        found = mm(jnp.where(begins, 1.0, 0.0).astype(BF), values.astype(BF), NT)
+        table_ref[pl.ds(base, ROWS), :] = found.astype(BF)
+        return base + (jnp.max(local) + ALIGN) // ALIGN * ALIGN
+
+    base_ref[blocks] = lax.fori_loop(0, blocks, lay, 0)
+
+
+def seat_rows(source, entry, block, info, per_owner):
     blocks = source.shape[0]
     rows = blocks * ROWS
     return pl.pallas_call(
         functools.partial(seat_kernel, per_owner),
-        out_shape=(jax.ShapeDtypeStruct((8, rows), F32), jax.ShapeDtypeStruct((8, 128), F32)),
-        in_specs=[SMEM, SMEM, VMEM],
-        out_specs=(VMEM, VMEM),
-        scratch_shapes=[pltpu.VMEM((blocks, ROWS), F32)] * 3,
+        out_shape=(
+            jax.ShapeDtypeStruct((rows + CHUNK, 128), BF),
+            jax.ShapeDtypeStruct((blocks, ROWS), jnp.int32),
+            jax.ShapeDtypeStruct((blocks + 1,), jnp.int32),
+            jax.ShapeDtypeStruct((8, 128), F32),
+        ),
+        in_specs=[SMEM, SMEM, SMEM, VMEM],
+        out_specs=(VMEM, VMEM, SMEM, VMEM),
+        scratch_shapes=[pltpu.VMEM((blocks, ROWS), F32)] * 4,
         compiler_params=ROOM,
         cost_estimate=cost(40 * rows * 1024, 8 * rows),
-    )(source, block, info)
+    )(source, entry, block, info)
+
+
+def plan_kernel(round_ref, base_ref, most_ref, table_ref, code_ref, tags_ref, found):
+    first = (SEATS * round_ref[0]).astype(F32)
+    chunks = (base_ref[base_ref.shape[0] - 1] + CHUNK - 1) // CHUNK
+    total = tags_ref.shape[1]
+    pick = jnp.where(iota((16, 128), 0) == iota((16, 128), 1), 1.0, 0.0).astype(BF)
+    base = pl.program_id(0) * total
+    found[...] = jnp.zeros_like(found)
+
+    def step(c, _):
+        at = pl.ds(pl.multiple_of(c * CHUNK, CHUNK), CHUNK)
+        lines = mm(pick, table_ref[at, :], NT)
+        seat = 64.0 * lines[1:2] + lines[2:3] - first
+        seated = (lines[5:6] > 0.5) & (seat >= 0.0) & (seat < float(SEATS))
+        code = jnp.where(seated, lines[0:1] * float(SEAT) + seat, -1.0).astype(jnp.int32)
+        code_ref[:, at] = jnp.broadcast_to(code, (8, CHUNK))
+        member = jnp.where(iota((total, 1), 0) + base == code, 1.0, 0.0).astype(BF)
+        found[...] += mm(lines.astype(BF), member, NT)
+        return 0
+
+    lax.fori_loop(0, chunks, step, 0)
+    rounds = jnp.floor((jnp.max(most_ref[...]) + (SEATS - 1.0)) * (1.0 / SEATS) + 1e-3)
+    line = iota((8, total), 0)
+    tags_ref[...] = jnp.where(
+        line == 0, found[3:4, :], jnp.where(line == 1, found[4:5, :], rounds)
+    )
+
+
+def plan_seats(step, base, most, table, devices):
+    total = devices * SEAT
+    part = min(2048, total)
+    return pl.pallas_call(
+        plan_kernel,
+        grid=(total // part,),
+        out_shape=(
+            jax.ShapeDtypeStruct((8, table.shape[0]), jnp.int32),
+            jax.ShapeDtypeStruct((8, total), F32),
+        ),
+        in_specs=[SMEM, SMEM, VMEM, VMEM],
+        out_specs=(
+            pl.BlockSpec((8, table.shape[0]), lambda i: (0, 0)),
+            pl.BlockSpec((8, part), lambda i: (0, i)),
+        ),
+        scratch_shapes=[pltpu.VMEM((16, part), F32)],
+        compiler_params=ROOM,
+        cost_estimate=cost(64 * total * table.shape[0], 4 * table.size),
+    )(step, base, most, table)
 
 
 def attend_kernel(
-    index_ref, low_ref, count_ref, ids_ref, w_ref, wo_ref, rows_ref, out_ref, x, qx, kx, vx, att, sems
+    index_ref,
+    low_ref,
+    count_ref,
+    base_ref,
+    local_ref,
+    ids_ref,
+    w_ref,
+    wo_ref,
+    rows_ref,
+    out_ref,
+    x,
+    qx,
+    kx,
+    vx,
+    att,
+    sems,
 ):
     tiles, span = ids_ref.shape
     width = w_ref.shape[0]
@@ -207,6 +309,7 @@
                 sems.at[t],
             ).start()
 
+    out_ref[...] = jnp.zeros_like(out_ref)
     lane = iota((ROWS, 2 * cols), 1)
     of_head = [(lane // HDIM == h) | (lane >= cols) for h in range(HEAD_GROUP)]
     lane_out = lane % cols // HDIM
@@ -275,13 +378,18 @@
             return 0
 
         lax.fori_loop(0, per_tile, block, 0)
-        out_ref[at, :] = (tile_rows.astype(F32) + mm(att[...], wo_ref[...])).astype(BF)
+        mixed = (tile_rows.astype(F32) + mm(att[...], wo_ref[...])).astype(BF)
+        for b in range(per_tile):
+            s = t * per_tile + b
+            run = jnp.where(iota((ROWS, ROWS), 0) == local_ref[pl.ds(s, 1), :], 1.0, 0.0)
+            sums = mm(run.astype(BF), mixed[b * ROWS : (b + 1) * ROWS])
+            out_ref[pl.ds(pl.multiple_of(base_ref[s], ALIGN), ROWS), :] = sums.astype(BF)
         return 0
 
     lax.fori_loop(0, tiles, tile, 0)
 
 
-def attend(index, low, count, ids, w_qkv, w_out, rows):
+def attend(index, low, count, base, local, ids, w_qkv, w_out, rows):
     tiles, span = ids.shape
     width = rows.shape[1]
     cols = HEAD_GROUP * HDIM
@@ -289,8 +397,8 @@
     pairs = tiles * span * span * HEAD_GROUP
     return pl.pallas_call(
         attend_kernel,
-        out_shape=jax.ShapeDtypeStruct((tiles * span, width), BF),
-        in_specs=[SMEM, SMEM, SMEM, VMEM, VMEM, VMEM, HBM],
+        out_shape=jax.ShapeDtypeStruct((tiles * span + CHUNK, width), BF),
+        in_specs=[SMEM, SMEM, SMEM, SMEM, VMEM, VMEM, VMEM, VMEM, HBM],
         out_specs=VMEM,
         scratch_shapes=[
             pltpu.VMEM((tiles * span, width), BF),
@@ -302,49 +410,61 @@
         ],
         compiler_params=ROOM,
         cost_estimate=cost(pairs * 1024, 4 * rows.size, pairs),
-    )(index, low, count, ids, w_qkv, w_out, rows)
-
-
-def sum_kernel(round_ref, seat_ref, most_ref, rows_ref, out_ref):
-    chunk = out_ref.shape[0]
-    first = SEATS * round_ref[0].astype(F32)
-    owner = seat_ref[0:1, :]
-    seat = seat_ref[1:2, :] - first
-    seated = (seat >= 0.0) & (seat < float(SEATS))
-    code = jnp.where(seated, owner * float(SEAT) + seat, -1.0).astype(jnp.int32)
-    mine = iota((chunk, 1), 0) + pl.program_id(0) * chunk
-    member = jnp.where(mine == code, 1.0, 0.0).astype(BF)
-    sums = mm(member, rows_ref[...])
-    tags = mm(seat_ref[...].astype(BF), member, NT)
-    rounds = jnp.floor((most_ref[0:1, :] + (SEATS - 1.0)) / float(SEATS))
+    )(index, low, count, base, local, ids, w_qkv, w_out, rows)
+
+
+def route_kernel(base_ref, code_ref, tags_ref, sums_ref, out_ref, acc):
+    total = out_ref.shape[0]
+    chunks = (base_ref[base_ref.shape[0] - 1] + CHUNK - 1) // CHUNK
+    seat = iota((total, 1), 0) + pl.program_id(0) * total
+    acc[...] = jnp.zeros_like(acc)
+
+    def step(c, _):
+        at = pl.ds(pl.multiple_of(c * CHUNK, CHUNK), CHUNK)
+        member = jnp.where(seat == code_ref[0:1, at], 1.0, 0.0).astype(BF)
+        acc[...] += mm(member, sums_ref[at, :])
+        return 0
+
+    lax.fori_loop(0, chunks, step, 0)
     line = iota((SEAT - SEATS, SEAT), 0)
-    for d in range(chunk // SEAT):
+    for d in range(total // SEAT):
         low = d * SEAT
-        out_ref[low : low + SEATS, :] = sums[low : low + SEATS].astype(BF)
-        origin = jnp.where(line == 0, tags[2:3, low : low + SEAT], jnp.where(line == 1, rounds, 0.0))
-        place = jnp.where(line == 0, tags[3:4, low : low + SEAT], 0.0)
+        here = slice(low, low + SEAT)
+        out_ref[low : low + SEATS, :] = acc[low : low + SEATS, :].astype(BF)
+        origin = jnp.where(
+            line == 0, tags_ref[0:1, here], jnp.where(line == 1, tags_ref[2:3, here], 0.0)
+        )
+        place = jnp.where(line == 0, tags_ref[1:2, here], 0.0)
         out_ref[low + SEATS : low + SEAT, :] = jnp.concatenate([origin, place], axis=1).astype(BF)
 
 
-def sum_runs(step, seats, most, rows, devices):
-    count, width = rows.shape
-    total = devices * SEAT
-    chunk = 512
-    fixed = lambda i: (0, 0)
+def route_sums(base, code, tags, sums):
+    count, width = sums.shape
+    total = tags.shape[1]
+    part = min(2048, total)
     return pl.pallas_call(
-        sum_kernel,
-        grid=(total // chunk,),
+        route_kernel,
+        grid=(total // part,),
         out_shape=jax.ShapeDtypeStruct((total, width), BF),
         in_specs=[
             SMEM,
-            pl.BlockSpec((8, count), fixed),
-            pl.BlockSpec((8, 128), fixed),
-            pl.BlockSpec((count, width), fixed),
+            VMEM,
+            pl.BlockSpec((8, part), lambda i: (0, i)),
+            VMEM,
         ],
-        out_specs=pl.BlockSpec((chunk, width), lambda i: (i, 0)),
+        out_specs=pl.BlockSpec((part, width), lambda i: (i, 0)),
+        scratch_shapes=[pltpu.VMEM((part, width), F32)],
         compiler_params=ROOM,
-        cost_estimate=cost(2 * total * count * width, 4 * count * width),
-    )(step, seats, most, rows)
+        cost_estimate=cost(total * count * width, 4 * count * width),
+    )(base, code, tags, sums)
+
+
+def seat_targets(per_owner, pieces_ref, target):
+    valid = iota((1, SEAT), 1) < SEATS
+    for h in range(pieces_ref.shape[0] // SEAT):
+        tag = pieces_ref[h * SEAT + SEATS : (h + 1) * SEAT, :].astype(F32)[0:1]
+        where = tag[:, :SEAT] * float(per_owner) + tag[:, SEAT:]
+        target[0:1, h * SEAT : (h + 1) * SEAT] = jnp.where(valid, where, -1.0).astype(jnp.int32)
 
 
 def fold_kernel(per_owner, pieces_ref, before_ref, out_ref, target):
@@ -356,11 +476,7 @@
     def _():
         out_ref[...] = before_ref[...]
 
-    valid = iota((1, SEAT), 1) < SEATS
-    for h in range(chunk // SEAT):
-        tag = pieces_ref[h * SEAT + SEATS : (h + 1) * SEAT, :].astype(F32)[0:1]
-        where = tag[:, :SEAT] * float(per_owner) + tag[:, SEAT:]
-        target[0:1, h * SEAT : (h + 1) * SEAT] = jnp.where(valid, where, -1.0).astype(jnp.int32)
+    seat_targets(per_owner, pieces_ref, target)
     member = jnp.where(iota((parents, 1), 0) == target[0:1, :], 1.0, 0.0).astype(BF)
     out_ref[...] += mm(member, pieces_ref[...])
 
@@ -385,7 +501,21 @@
 
 
 def pool_kernel(
-    in_ref, length_ref, w_ref, gain_ref, shift_ref, cot_ref, pooled_ref, back_ref, weight_ref, norm_ref, acc, sums
+    per_owner,
+    pieces_ref,
+    more_ref,
+    length_ref,
+    w_ref,
+    gain_ref,
+    shift_ref,
+    cot_ref,
+    pooled_ref,
+    back_ref,
+    weight_ref,
+    norm_ref,
+    acc,
+    sums,
+    target,
 ):
     step = pl.program_id(0)
 
@@ -393,9 +523,17 @@
     def _():
         acc[...] = jnp.zeros_like(acc)
         sums[...] = jnp.zeros_like(sums)
-
-    lengths = jnp.concatenate([length_ref[...]] * (in_ref.shape[1] // 128), axis=1)
-    parent_in = (in_ref[...] / lengths).astype(BF)
+        seat_targets(per_owner, pieces_ref, target)
+
+    chunk, width = more_ref.shape
+    total = more_ref[...]
+    parent = iota((chunk, 1), 0) + step * chunk
+    part = min(2048, pieces_ref.shape[0])
+    for low in range(0, pieces_ref.shape[0], part):
+        member = jnp.where(parent == target[0:1, low : low + part], 1.0, 0.0).astype(BF)
+        total = total + mm(member, pieces_ref[low : low + part, :])
+    lengths = jnp.concatenate([length_ref[...]] * (width // 128), axis=1)
+    parent_in = (total / lengths).astype(BF)
     w_pool = w_ref[...]
     gain = gain_ref[...]
     projected = mm(parent_in, w_pool)
@@ -429,14 +567,14 @@
         norm_ref[...] = sums[...]
 
 
-def pool(parent_sum, length, w_pool, gain, shift, cotangent):
-    parents, width = parent_sum.shape
+def pool(pieces, more, length, w_pool, gain, shift, cotangent):
+    parents, width = more.shape
     wide = w_pool.shape[1]
     chunk = 256
     fixed = lambda i: (0, 0)
     along = lambda i: (i, 0)
     return pl.pallas_call(
-        pool_kernel,
+        functools.partial(pool_kernel, parents * SEAT // pieces.shape[0]),
         grid=(parents // chunk,),
         out_shape=(
             jax.ShapeDtypeStruct((parents, wide), BF),
@@ -445,6 +583,7 @@
             jax.ShapeDtypeStruct((8, wide), F32),
         ),
         in_specs=[
+            pl.BlockSpec(pieces.shape, fixed),
             pl.BlockSpec((chunk, width), along),
             pl.BlockSpec((chunk, 128), along),
             pl.BlockSpec((width, wide), fixed),
@@ -458,10 +597,14 @@
             pl.BlockSpec((width, wide), fixed),
             pl.BlockSpec((8, wide), fixed),
         ),
-        scratch_shapes=[pltpu.VMEM((width, wide), F32), pltpu.VMEM((8, wide), F32)],
-        compiler_params=ROOM,
+        scratch_shapes=[
+            pltpu.VMEM((width, wide), F32),
+            pltpu.VMEM((8, wide), F32),
+            pltpu.VMEM((8, pieces.shape[0]), jnp.int32),
+        ],
+        compiler_params=FULL,
         cost_estimate=cost(6 * parents * width * wide, 8 * parents * wide, 2 * parents * wide),
-    )(parent_sum, length, w_pool, gain, shift, cotangent)
+    )(pieces, more, length, w_pool, gain, shift, cotangent)
 
 
 def spread_kernel(span_ref, grad_ref, out_ref, share):
@@ -507,13 +650,24 @@
     return swap(rows.reshape(devices, rows.shape[0] // devices, rows.shape[1])).reshape(rows.shape)
 
 
+def gather_info(info, devices):
+    known = info[None]
+    bit = 1
+    while bit < devices:
+        pairs = [(d, d ^ bit) for d in range(devices)]
+        known = jnp.concatenate([known, lax.ppermute(known, "pts", pairs)], axis=0)
+        bit *= 2
+    return known
+
+
 def received_index(codes, blocks, capacity):
     devices = codes.shape[0]
-    mine = codes // blocks == lax.axis_index("pts")
+    me = lax.axis_index("pts")
+    mine = codes // blocks == me
     slots = codes % blocks
     lane = jnp.arange(blocks)
     rank = jnp.sum(mine[:, None, :] & (lane[None, :] < lane[:, None])[None], axis=2)
-    index = jnp.arange(devices)[:, None] * capacity + rank
+    index = (jnp.arange(devices) ^ me)[:, None] * capacity + rank
     both = index * blocks + lane[None, :]
     hit = mine[:, :, None] & (slots[:, :, None] == lane[None, None, :])
     both = jnp.sum(jnp.where(hit, both[:, :, None], 0), axis=(0, 1)).astype(jnp.int32)
@@ -557,41 +711,43 @@
     per_owner = parents // devices
     capacity = (blocks + devices - 1) // devices
 
-    info, span = order_tables(child_counts, parent_order, hil_dest, hil_slot, devices)
-    info = swap(info)
-    payload = pack_blocks(hil_dest, points, devices, capacity)
+    me = lax.axis_index("pts")
+    payload, info, span = front(
+        child_counts, parent_order, hil_dest, hil_slot, points, devices, capacity
+    )
     received = exchange(payload, devices)
+    info = gather_info(info, devices)
     index, block = received_index(info[:, parents // 128, :blocks], blocks, capacity)
-    seats, most = seat_rows(
-        index // capacity, block, info.reshape(devices * INFO, 128), per_owner
-    )
+    source = index // capacity
+    table, local_run, base, most = seat_rows(
+        source, source ^ me, block, info.reshape(devices * INFO, 128), per_owner
+    )
+    code, tags = plan_seats(jnp.zeros((1,), jnp.int32), base, most, table, devices)
     low, count = key_windows(patch_ids)
     lengths = lax.dynamic_slice_in_dim(
-        info[:, : parents // 128].reshape(devices, parents),
-        lax.axis_index("pts") * per_owner,
-        per_owner,
-        axis=1,
-    ).reshape(parents, 1) % 16
+        info[:, : parents // 128].reshape(devices, parents), me * per_owner, per_owner, axis=1
+    )
+    lengths = lengths[jnp.arange(devices) ^ me].reshape(parents, 1) % 16
     lengths = jnp.broadcast_to(lengths.astype(F32), (parents, 128))
-    index, low, count, seats, most, lengths = lax.optimization_barrier(
-        (index, low, count, seats, most, lengths)
-    )
-    mixed = attend(index, low, count, patch_ids, w_qkv, w_out, received)
-
-    def turn(step, before):
-        sent = sum_runs(step.reshape(1), seats, most, mixed, devices)
-        pieces = exchange(sent, devices)
-        needed = jnp.max(pieces.reshape(devices, SEAT, width)[:, SEATS + 1, 0].astype(F32))
-        return needed.astype(jnp.int32), fold_pieces(pieces, before, per_owner)
-
-    rounds, parent_sum = turn(jnp.int32(0), jnp.zeros((parents, width), F32))
-    _, parent_sum = lax.while_loop(
-        lambda carry: carry[0] < rounds,
-        lambda carry: (carry[0] + 1, turn(carry[0], carry[1])[1]),
-        (jnp.int32(1), parent_sum),
+    more = jnp.zeros((parents, width), F32)
+    index, low, count, base, local_run, code, tags, lengths = lax.optimization_barrier(
+        (index, low, count, base, local_run, code, tags, lengths)
+    )
+    sums = attend(index, low, count, base, local_run, patch_ids, w_qkv, w_out, received)
+    pieces = exchange(route_sums(base, code, tags, sums), devices)
+    rounds = jnp.max(pieces.reshape(devices, SEAT, width)[:, SEATS + 1, 0].astype(F32))
+
+    def turn(carry):
+        step, before = carry
+        code, tags = plan_seats(step.reshape(1), base, most, table, devices)
+        late = exchange(route_sums(base, code, tags, sums), devices)
+        return step + 1, fold_pieces(late, before, per_owner)
+
+    _, more = lax.while_loop(
+        lambda carry: carry[0] < rounds.astype(jnp.int32), turn, (jnp.int32(1), more)
     )
     pooled, back, weight, norm = pool(
-        parent_sum, lengths, w_pool, norm_gain[None], norm_shift[None], cotangent
+        pieces, more, lengths, w_pool, norm_gain[None], norm_shift[None], cotangent
     )
     norm_high = norm.astype(BF)
     norm_low = (norm - norm_high.astype(F32)).astype(BF)

time: 269 us -> 347 us (1.29)
  Pallas kernels: 142 us -> 213 us
  waiting for transfers between devices: 57.5 us -> 70.8 us
  local copies, waits for them, and re-layouts: 10.3 us -> 5.53 us
  starting transfers between devices: 26.6 us -> 22.4 us
    pallas_call x5 -> x4, Pallas kernels: 22.5 us -> 84 us  [the longest x1 66.2 us: front(): pl.pallas_call(functools.partial(front_kernel, capacity), out_shape=(jax....]
    ppermute x0 -> x4, waiting for transfers between devices: none -> 43.9 us  [gather_info(): known = jnp.concatenate([known, lax.ppermute(known, 'pts', pairs)], axis=0)]
    all_to_all x4 -> x3, waiting for transfers between devices: 57.5 us -> 26.9 us  [swap(): return lax.all_to_all(parts, 'pts', split_axis=0, concat_axis=0, tiled=True)]
    all_to_all x4 -> x3, starting transfers between devices: 26.6 us -> 15.3 us  [swap(): return lax.all_to_all(parts, 'pts', split_axis=0, concat_axis=0, tiled=True)]
    pallas_call x1, Pallas kernels: 12.2 us -> 20.3 us  [seat_rows(): pl.pallas_call(functools.partial(seat_kernel, per_owner), out_shape=(jax....]
    ppermute x0 -> x4, starting transfers between devices: none -> 7.14 us  [gather_info(): known = jnp.concatenate([known, lax.ppermute(known, 'pts', pairs)], axis=0)]
    unnamed x33 -> x23, local copies, waits for them, and re-layouts: 7.33 us -> 0.26 us
  transfers between devices with their start and end apart: 4 -> 7, of which waited for: 4 -> 5; matrix products, arithmetic and copies ran while one was open for 1% -> 1% of each run, Pallas kernels for 7% -> 9%
where the time goes in v3:
time: 347 us; the launch traced here: 346 us
  Pallas kernels  213 us (61%)
  waiting for transfers between devices  70.8 us (20%)
  blocking collectives  28.1 us (8%)
  starting transfers between devices  22.4 us (6%)
  local copies, waits for them, and re-layouts  5.53 us (2%)
  other arithmetic  4.55 us (1%)
    pallas_call x1, Pallas kernels, attend(): pl.pallas_call(attend_kernel, out_shape=jax.ShapeDtypeStruct((tiles * spa...  103 us
    pallas_call x1, Pallas kernels, front(): pl.pallas_call(functools.partial(front_kernel, capacity), out_shape=(jax....  66.2 us
    ppermute x4, waiting for transfers between devices, gather_info(): known = jnp.concatenate([known, lax.ppermute(known, 'pts', pairs)], axis=0)  43.9 us
    all_to_all x1, blocking collectives, swap(): return lax.all_to_all(parts, 'pts', split_axis=0, concat_axis=0, tiled=True)  28.1 us
    all_to_all x3, waiting for transfers between devices, swap(): return lax.all_to_all(parts, 'pts', split_axis=0, concat_axis=0, tiled=True)  26.9 us
    pallas_call x1, Pallas kernels, seat_rows(): pl.pallas_call(functools.partial(seat_kernel, per_owner), out_shape=(jax....  20.3 us
    all_to_all x3, starting transfers between devices, swap(): return lax.all_to_all(parts, 'pts', split_axis=0, concat_axis=0, tiled=True)  15.3 us
    pallas_call x1, Pallas kernels, pool(): pl.pallas_call(functools.partial(pool_kernel, parents * SEAT // pieces.sh...  9.88 us
  transfers between devices with their start and end apart: 7, of which 5 were waited for; matrix products, arithmetic and copies ran while one was open for 1% of the time, Pallas kernels for 9%

profile of v3, /device:TPU:0, one launch (start us, length us, event | category | flops | bytes accessed | tf_op | source)
XLA Modules:
  0.0 346.1 jit_solution(3466912462846936960)
XLA Ops:
  0.6 66.2 %shard_map.147 = (bf16[4096,256]{1,0:T(8,128)(2,1)}, s32[16,128]{1,0:T(8,128)}, s32[8,1024]{1,0:T(8,128)}) custom-call(s32[32]{0:T(128)} %dest_ref.1, s32[1,1024]{1,0:T(1,128)} %counts_ref.1, s32[1,1024]{1,0:T(1,128)} %order_ref.1, s32[1,32]{1,0:T(1,128)} %bitcast.60, s32[1,32]{1,0:T(1,128)} %bitcast.61, bf16[4096,256]{1,0:T(8,128)(2,1)} %points_ref.1), custom_call_target="tpu_custom_call" | custom-call | flops 33554432 | bytes 4194304 | tf_op jit(solution)/shard_map/pallas_call | solution.py:116
  66.8 0.0 copy-start.5
  66.8 0.0 copy-start
  66.8 7.4 %all-to-all-start.1 = ((bf16[16,256,256]{2,1,0:T(8,128)(2,1)}), bf16[16,256,256]{2,1,0:T(8,128)(2,1)S(1)}, u32[]{:S(2)}, u32[]{:S(2)}) async-start(bf16[16,256,256]{2,1,0:T(8,128)(2,1)} %bitcast.44), calls=%async_computation.1 | async-start | bytes 4194304 | tf_op jit(solution)/shard_map/all_to_all | solution.py:646
  74.2 0.5 collective-permute-start
  74.7 0.1 fusion.10
  74.8 0.1 copy.23
  74.9 0.1 copy.27
  75.0 0.2 convert_reduce_fusion.2
  75.2 0.1 select_reduce_fusion.1
  75.3 0.1 reduce_sum.76
  75.3 0.1 reduce_sum.74
  75.5 0.0 collective-permute-done
  75.5 1.9 collective-permute-start.1
  77.4 9.8 %collective-permute-done.1 = s32[2,16,128]{2,1,0:T(8,128)S(1)} collective-permute-done((s32[2,16,128]{2,1,0:T(8,128)S(1)}, s32[2,16,128]{2,1,0:T(8,128)S(1)}, u32[]{:S(2)}, u32[]{:S(2)}) %collective-permute-start.1) | collective-permute-done | bytes 16416 | tf_op jit(solution)/shard_map/ppermute | solution.py:658
  87.2 0.4 collective-permute-start.2
  87.6 22.3 %collective-permute-done.2 = s32[4,16,128]{2,1,0:T(8,128)S(1)} collective-permute-done((s32[4,16,128]{2,1,0:T(8,128)S(1)}, s32[4,16,128]{2,1,0:T(8,128)S(1)}, u32[]{:S(2)}, u32[]{:S(2)}) %collective-permute-start.2) | collective-permute-done | bytes 32800 | tf_op jit(solution)/shard_map/ppermute | solution.py:658
  109.9 4.4 %collective-permute-start.3 = (s32[8,16,128]{2,1,0:T(8,128)S(1)}, s32[8,16,128]{2,1,0:T(8,128)S(1)}, u32[]{:S(2)}, u32[]{:S(2)}) collective-permute-start(s32[8,16,128]{2,1,0:T(8,128)S(1)} %pad_add_fusion), channel_id=1, source_target_pairs={{0,8},{1,9},{2,10},{3,11},{4,12},{5,13},{6,14},{7,15},{8,0},{9,1},... | collective-permute-start | bytes 196616 | tf_op jit(solution)/shard_map/ppermute | solution.py:658
  114.3 11.8 %collective-permute-done.3 = s32[8,16,128]{2,1,0:T(8,128)S(1)} collective-permute-done((s32[8,16,128]{2,1,0:T(8,128)S(1)}, s32[8,16,128]{2,1,0:T(8,128)S(1)}, u32[]{:S(2)}, u32[]{:S(2)}) %collective-permute-start.3) | collective-permute-done | bytes 65568 | tf_op jit(solution)/shard_map/ppermute | solution.py:658
  126.1 0.1 fusion.2
  126.2 0.1 constant_dynamic-slice_fusion
  126.3 0.6 gather_fusion
  126.9 0.1 reshape.207
  126.9 0.3 convert_reduce_fusion
  127.3 0.1 add_select_fusion
  127.4 0.3 select_reduce_fusion
  127.7 20.3 %shard_map.148 = (bf16[4608,128]{1,0:T(8,128)(2,1)}, s32[32,128]{1,0:T(8,128)S(1)}, s32[33]{0:T(128)S(1)}, f32[8,128]{1,0:T(8,128)S(1)}) custom-call(s32[32]{0:T(128)S(1)} %get-tuple-element.104.source_ref, s32[32]{0:T(128)S(1)} %get-tuple-element.103.entry_ref, s32[32]{0:T(128)S(1)} %get-tuple-element.110.block_ref, s32[256,128]{1,0:T(8,128)S(1)} %bitcast.42), custom_call_target="tpu_custom_call" | custom-call | flops 167772160 | bytes 32768 | tf_op jit(solution)/shard_map/pallas_call | solution.py:214
  148.0 4.1 %shard_map.149 = (s32[8,4608]{1,0:T(8,128)S(1)}, f32[8,2048]{1,0:T(8,128)S(1)}) custom-call(s32[1]{0:T(128)} %constant.120.clone.1.round_ref, s32[33]{0:T(128)S(1)} %get-tuple-element.164.base_ref, f32[8,128]{1,0:T(8,128)S(1)} %get-tuple-element.165.most_ref, bf16[4608,128]{1,0:T(8,128)(2,1)} %get-tuple-element.166.table_ref), custom_call_target="tpu_custom_call" | custom-call | flops 603979776 | bytes 2359296 | tf_op jit(solution)/shard_map/pallas_call | solution.py:260
  152.2 1.0 broadcast_in_dim.89.length_ref
  153.2 103.1 %shard_map.150.sums_ref = bf16[4608,256]{1,0:T(8,128)(2,1)S(1)} custom-call(s32[32]{0:T(128)S(1)} %get-tuple-element.75.index_ref, s32[32]{0:T(128)S(1)} %get-tuple-element.76.low_ref, s32[32]{0:T(128)S(1)} %get-tuple-element.77.count_ref, s32[33]{0:T(128)S(1)} %get-tuple-element.164.base_ref, s32[32,128]{1,0:T(8,128)S(1)} %get-tuple-element.78.local_ref, ...), custom_call_target="tpu_custom_call" | custom-call | flops 34359738368 | bytes 4194304 | tf_op jit(solution)/shard_map/pallas_call | solution.py:398
  256.3 3.9 %shard_map.151 = bf16[2048,256]{1,0:T(8,128)(2,1)} custom-call(s32[33]{0:T(128)S(1)} %get-tuple-element.164.base_ref, s32[8,4608]{1,0:T(8,128)S(1)} %get-tuple-element.73.code_ref, f32[8,2048]{1,0:T(8,128)S(1)} %get-tuple-element.74.tags_ref, bf16[4608,256]{1,0:T(8,128)(2,1)S(1)} %shard_map.150.sums_ref), custom_call_target="tpu_custom_call" | custom-call | flops 2415919104 | bytes 4718592 | tf_op jit(solution)/shard_map/pallas_call | solution.py:445
  260.2 3.7 %all-to-all-start.2 = ((bf16[16,128,256]{2,1,0:T(8,128)(2,1)}), bf16[16,128,256]{2,1,0:T(8,128)(2,1)S(1)}, u32[]{:S(2)}, u32[]{:S(2)}) async-start(bf16[16,128,256]{2,1,0:T(8,128)(2,1)} %bitcast.13), calls=%async_computation.2 | async-start | bytes 2097152 | tf_op jit(solution)/shard_map/all_to_all | solution.py:646
  263.9 22.9 %all-to-all-done.2 = bf16[16,128,256]{2,1,0:T(8,128)(2,1)S(1)} async-done(((bf16[16,128,256]{2,1,0:T(8,128)(2,1)}), bf16[16,128,256]{2,1,0:T(8,128)(2,1)S(1)}, u32[]{:S(2)}, u32[]{:S(2)}) %all-to-all-start.2) | async-done | bytes 1048608 | tf_op jit(solution)/shard_map/all_to_all | solution.py:646
  286.9 0.7 slice_reduce_fusion.1
  288.2 0.1 broadcast_in_dim.90
  288.3 0.2 while.10
  288.6 9.9 %shard_map.152 = (bf16[1024,512]{1,0:T(8,128)(2,1)}, bf16[1024,256]{1,0:T(8,128)(2,1)}, bf16[256,512]{1,0:T(8,128)(2,1)}, f32[8,512]{1,0:T(8,128)}) custom-call(bf16[2048,256]{1,0:T(8,128)(2,1)} %bitcast.43, f32[1024,256]{1,0:T(8,128)S(1)} %get-tuple-element.80.more_ref, f32[1024,128]{1,0:T(8,128)} %broadcast_in_dim.89.length_ref, bf16[256,512]{1,0:T(8,128)(2,1)} %w_ref.3, ...), custom_call_target="tpu_custom_call" | custom-call | flops 805306368 | bytes 4194304 | tf_op jit(solution)/shard_map/pallas_call | solution.py:576
  298.5 0.7 convert_element_type.41
  299.2 0.7 fusion.7
  299.9 1.0 reshape.213
  301.0 1.1 pad_maximum_fusion
  302.1 28.1 %all_to_all.26 = bf16[16,104,256]{2,1,0:T(8,128)(2,1)S(1)} all-to-all(bf16[16,104,256]{2,1,0:T(8,128)(2,1)S(1)} %pad_maximum_fusion), channel_id=1, replica_groups=mesh['grp'=2,'pts'=16] {'pts'}, dimensions={0} | all-to-all | bytes 1703936 | tf_op jit(solution)/shard_map/all_to_all | solution.py:646
  330.2 0.7 broadcast_in_dim.95
  331.0 4.2 %all-to-all-start.4 = ((bf16[16,32,256]{2,1,0:T(8,128)(2,1)}), bf16[16,32,256]{2,1,0:T(8,128)(2,1)S(1)}, u32[]{:S(2)}, u32[]{:S(2)}) async-start(bf16[16,32,256]{2,1,0:T(8,128)(2,1)} %broadcast_in_dim.95), calls=%async_computation.4 | async-start | bytes 524288 | tf_op jit(solution)/shard_map/all_to_all | solution.py:646
  335.2 0.6 add.110
  335.9 5.4 %shard_map.153 = bf16[4096,256]{1,0:T(8,128)(2,1)} custom-call(s32[8,1024]{1,0:T(8,128)S(1)} %copy-done.3, bf16[1024,256]{1,0:T(8,128)(2,1)S(1)} %bitcast.40), custom_call_target="tpu_custom_call" | custom-call | flops 2147483648 | bytes 4194304 | tf_op jit(solution)/shard_map/pallas_call | solution.py:630
  341.3 3.9 %all-to-all-done.4 = bf16[16,32,256]{2,1,0:T(8,128)(2,1)S(1)} async-done(((bf16[16,32,256]{2,1,0:T(8,128)(2,1)}), bf16[16,32,256]{2,1,0:T(8,128)(2,1)S(1)}, u32[]{:S(2)}, u32[]{:S(2)}) %all-to-all-start.4) | async-done | bytes 262176 | tf_op jit(solution)/shard_map/all_to_all | solution.py:646
  345.2 0.9 reshape.215
  (42 shorter events, 0.3 us)
Async XLA Ops:
  66.8 7.4 %copy-start.5 = (s32[16,128]{1,0:T(8,128)S(1)}, s32[16,128]{1,0:T(8,128)}, u32[]{:S(2)}) copy-start(s32[16,128]{1,0:T(8,128)} %get-tuple-element.65) | copy-start | bytes 24580
  66.8 7.9 %copy-start = (s32[4,1024]{1,0:T(4,128)S(1)}, s32[4,1024]{1,0:T(4,128)}, u32[]{:S(2)}) copy-start(s32[4,1024]{1,0:T(4,128)} %ids_ref.1) | copy-start | bytes 49156
  66.8 86.3 %all-to-all-start.1 = ((bf16[16,256,256]{2,1,0:T(8,128)(2,1)}), bf16[16,256,256]{2,1,0:T(8,128)(2,1)S(1)}, u32[]{:S(2)}, u32[]{:S(2)}) async-start(bf16[16,256,256]{2,1,0:T(8,128)(2,1)} %bitcast.44), calls=%async_computation.1 | async-start | bytes 4194304 | tf_op jit(solution)/shard_map/all_to_all | solution.py:646
  74.2 1.3 collective-permute-start
  75.5 11.6 %collective-permute-start.1 = (s32[2,16,128]{2,1,0:T(8,128)S(1)}, s32[2,16,128]{2,1,0:T(8,128)S(1)}, u32[]{:S(2)}, u32[]{:S(2)}) collective-permute-start(s32[2,16,128]{2,1,0:T(8,128)S(1)} %pad_add_fusion.2), channel_id=1, source_target_pairs={{0,2},{1,3},{2,0},{3,1},{4,6},{5,7},{6,4},{7,5},{8,10},{9,11},{10,... | collective-permute-start | bytes 49160 | tf_op jit(solution)/shard_map/ppermute | solution.py:658
  87.2 22.7 %collective-permute-start.2 = (s32[4,16,128]{2,1,0:T(8,128)S(1)}, s32[4,16,128]{2,1,0:T(8,128)S(1)}, u32[]{:S(2)}, u32[]{:S(2)}) collective-permute-start(s32[4,16,128]{2,1,0:T(8,128)S(1)} %pad_add_fusion.1), channel_id=1, source_target_pairs={{0,4},{1,5},{2,6},{3,7},{4,0},{5,1},{6,2},{7,3},{8,12},{9,13},{10,... | collective-permute-start | bytes 98312 | tf_op jit(solution)/shard_map/ppermute | solution.py:658
  109.9 16.2 %collective-permute-start.3 = (s32[8,16,128]{2,1,0:T(8,128)S(1)}, s32[8,16,128]{2,1,0:T(8,128)S(1)}, u32[]{:S(2)}, u32[]{:S(2)}) collective-permute-start(s32[8,16,128]{2,1,0:T(8,128)S(1)} %pad_add_fusion), channel_id=1, source_target_pairs={{0,8},{1,9},{2,10},{3,11},{4,12},{5,13},{6,14},{7,15},{8,0},{9,1},... | collective-permute-start | bytes 196616 | tf_op jit(solution)/shard_map/ppermute | solution.py:658
  127.7 25.5 %copy-start.1 = (bf16[256,768]{1,0:T(8,128)(2,1)S(1)}, bf16[256,768]{1,0:T(8,128)(2,1)}, u32[]{:S(2)}) copy-start(bf16[256,768]{1,0:T(8,128)(2,1)} %w_ref.2) | copy-start | bytes 1179652
  127.7 25.5 %copy-start.2 = (bf16[256,256]{1,0:T(8,128)(2,1)S(1)}, bf16[256,256]{1,0:T(8,128)(2,1)}, u32[]{:S(2)}) copy-start(bf16[256,256]{1,0:T(8,128)(2,1)} %wo_ref.1) | copy-start | bytes 393220
  256.3 3.9 %copy-start.6 = (bf16[4608,256]{1,0:T(8,128)(2,1)}, bf16[4608,256]{1,0:T(8,128)(2,1)S(1)}, u32[]{:S(2)}) copy-start(bf16[4608,256]{1,0:T(8,128)(2,1)S(1)} %shard_map.150.sums_ref) | copy-start | bytes 7077892
  260.2 26.6 %all-to-all-start.2 = ((bf16[16,128,256]{2,1,0:T(8,128)(2,1)}), bf16[16,128,256]{2,1,0:T(8,128)(2,1)S(1)}, u32[]{:S(2)}, u32[]{:S(2)}) async-start(bf16[16,128,256]{2,1,0:T(8,128)(2,1)} %bitcast.13), calls=%async_computation.2 | async-start | bytes 2097152 | tf_op jit(solution)/shard_map/all_to_all | solution.py:646
  286.9 1.5 copy-start.4
  302.1 33.8 %copy-start.3 = (s32[8,1024]{1,0:T(8,128)S(1)}, s32[8,1024]{1,0:T(8,128)}, u32[]{:S(2)}) copy-start(s32[8,1024]{1,0:T(8,128)} %get-tuple-element.83.span_ref) | copy-start | bytes 98308
  331.0 14.3 %all-to-all-start.4 = ((bf16[16,32,256]{2,1,0:T(8,128)(2,1)}), bf16[16,32,256]{2,1,0:T(8,128)(2,1)S(1)}, u32[]{:S(2)}, u32[]{:S(2)}) async-start(bf16[16,32,256]{2,1,0:T(8,128)(2,1)} %broadcast_in_dim.95), calls=%async_computation.4 | async-start | bytes 524288 | tf_op jit(solution)/shard_map/all_to_all | solution.py:646

commit v4 on v3

--- a/solution.py
+++ b/solution.py
@@ -53,42 +53,9 @@
     )
 
 
-def front_kernel(
-    capacity,
-    dest_ref,
-    counts_ref,
-    order_ref,
-    dest_row_ref,
-    slot_row_ref,
-    points_ref,
-    payload_ref,
-    info_ref,
-    span_ref,
-    used,
-    sem,
-):
-    blocks = dest_ref.shape[0]
-
-    def clear(d, _):
-        used[d] = 0
-        return 0
-
-    lax.fori_loop(0, used.shape[0], clear, 0)
-
-    def send(b, _):
-        d = dest_ref[b]
-        place = d * capacity + used[d]
-        used[d] = used[d] + 1
-        pltpu.make_async_copy(
-            points_ref.at[pl.ds(pl.multiple_of(b * ROWS, ROWS), ROWS)],
-            payload_ref.at[pl.ds(pl.multiple_of(place * ROWS, ROWS), ROWS)],
-            sem,
-        ).start()
-        return 0
-
-    lax.fori_loop(0, blocks, send, 0)
-
+def order_kernel(counts_ref, order_ref, dest_ref, slot_ref, info_ref, span_ref):
     parents = counts_ref.shape[1]
+    blocks = dest_ref.shape[1]
     counts = jnp.broadcast_to(counts_ref[...], (8, parents)).astype(F32)
     upper = jnp.where(iota((parents, parents), 0) <= iota((parents, parents), 1), 1.0, 0.0)
     starts = mm(counts.astype(BF), upper.astype(BF)) - counts
@@ -102,36 +69,70 @@
     span_ref[...] = jnp.where(which == 0, first, jnp.where(which == 1, first + length, length))
     both = 16 * first + length
     lines = parents // 128
+    info_ref[0, lines:, :] = jnp.zeros((INFO - lines, 128), jnp.int32)
+    info_ref[0, lines : lines + 1, :blocks] = dest_ref[...] * blocks + slot_ref[...]
     for i in range(lines):
-        info_ref[i : i + 1, :] = both[:, i * 128 : (i + 1) * 128]
-    info_ref[lines:, :] = jnp.zeros((INFO - lines, 128), jnp.int32)
-    info_ref[lines : lines + 1, :blocks] = dest_row_ref[...] * blocks + slot_row_ref[...]
-
+        info_ref[0, i : i + 1, :] = both[:, i * 128 : (i + 1) * 128]
+    tile = info_ref[0]
+    for d in range(1, info_ref.shape[0]):
+        info_ref[d] = tile
+
+
+def order_tables(child_counts, parent_order, hil_dest, hil_slot, devices):
+    parents = child_counts.shape[1]
+    return pl.pallas_call(
+        order_kernel,
+        out_shape=(
+            jax.ShapeDtypeStruct((devices, INFO, 128), jnp.int32),
+            jax.ShapeDtypeStruct((8, parents), jnp.int32),
+        ),
+        in_specs=[VMEM] * 4,
+        out_specs=(VMEM, VMEM),
+        compiler_params=FULL,
+        cost_estimate=cost(32 * parents * parents, 8 * parents),
+    )(child_counts, parent_order, hil_dest[None], hil_slot[None])
+
+
+def pack_kernel(capacity, dest_ref, points_ref, payload_ref, used, sem):
+    blocks = dest_ref.shape[0]
+
+    def clear(d, _):
+        used[d] = 0
+        return 0
+
+    lax.fori_loop(0, used.shape[0], clear, 0)
+
+    def send(b, _):
+        d = dest_ref[b]
+        place = d * capacity + used[d]
+        used[d] = used[d] + 1
+        pltpu.make_async_copy(
+            points_ref.at[pl.ds(pl.multiple_of(b * ROWS, ROWS), ROWS)],
+            payload_ref.at[pl.ds(pl.multiple_of(place * ROWS, ROWS), ROWS)],
+            sem,
+        ).start()
+        return 0
+
+    lax.fori_loop(0, blocks, send, 0)
     whole = pl.ds(0, blocks * ROWS)
     pltpu.make_async_copy(points_ref.at[whole], payload_ref.at[whole], sem).wait()
 
 
-def front(child_counts, parent_order, hil_dest, hil_slot, points, devices, capacity):
-    parents = child_counts.shape[1]
-    return pl.pallas_call(
-        functools.partial(front_kernel, capacity),
-        out_shape=(
-            jax.ShapeDtypeStruct((devices * capacity * ROWS, points.shape[1]), BF),
-            jax.ShapeDtypeStruct((INFO, 128), jnp.int32),
-            jax.ShapeDtypeStruct((8, parents), jnp.int32),
-        ),
-        in_specs=[SMEM, VMEM, VMEM, VMEM, VMEM, HBM],
-        out_specs=(HBM, VMEM, VMEM),
+def pack_blocks(hil_dest, points, devices, capacity):
+    return pl.pallas_call(
+        functools.partial(pack_kernel, capacity),
+        out_shape=jax.ShapeDtypeStruct((devices * capacity * ROWS, points.shape[1]), BF),
+        in_specs=[SMEM, HBM],
+        out_specs=VMEM,
         scratch_shapes=[pltpu.SMEM((devices,), jnp.int32), pltpu.SemaphoreType.DMA],
         compiler_params=FULL,
-        cost_estimate=cost(32 * parents * parents, 4 * points.size),
-    )(hil_dest, child_counts, parent_order, hil_dest[None], hil_slot[None], points)
+        cost_estimate=cost(0, 4 * points.size),
+    )(hil_dest, points)
 
 
 def seat_kernel(
     per_owner,
     source_ref,
-    entry_ref,
     block_ref,
     info_ref,
     table_ref,
@@ -152,8 +153,8 @@
     fields = fields.astype(F32).astype(BF)
 
     def one(v, _):
-        entry = entry_ref[v]
-        packed = info_ref[pl.ds(pl.multiple_of(entry * INFO, INFO), 8), :]
+        source = source_ref[v]
+        packed = info_ref[pl.ds(pl.multiple_of(source * INFO, INFO), 8), :]
         line = jnp.concatenate([packed[i : i + 1] for i in range(8)], axis=1)
         first = line // 16
         row = block_ref[v] * ROWS + iota((ROWS, parents), 0)
@@ -161,7 +162,7 @@
         found = mm(fields, jnp.where(inside, 1.0, 0.0).astype(BF), NT)
         owner[pl.ds(v, 1), :] = found[0:1]
         place[pl.ds(v, 1), :] = found[1:2]
-        origin[pl.ds(v, 1), :] = jnp.full((1, ROWS), source_ref[v], jnp.int32).astype(F32)
+        origin[pl.ds(v, 1), :] = jnp.full((1, ROWS), source, jnp.int32).astype(F32)
         return 0
 
     lax.fori_loop(0, blocks, one, 0)
@@ -208,7 +209,7 @@
     base_ref[blocks] = lax.fori_loop(0, blocks, lay, 0)
 
 
-def seat_rows(source, entry, block, info, per_owner):
+def seat_rows(source, block, info, per_owner):
     blocks = source.shape[0]
     rows = blocks * ROWS
     return pl.pallas_call(
@@ -219,12 +220,12 @@
             jax.ShapeDtypeStruct((blocks + 1,), jnp.int32),
             jax.ShapeDtypeStruct((8, 128), F32),
         ),
-        in_specs=[SMEM, SMEM, SMEM, VMEM],
+        in_specs=[SMEM, SMEM, VMEM],
         out_specs=(VMEM, VMEM, SMEM, VMEM),
         scratch_shapes=[pltpu.VMEM((blocks, ROWS), F32)] * 4,
         compiler_params=ROOM,
         cost_estimate=cost(40 * rows * 1024, 8 * rows),
-    )(source, entry, block, info)
+    )(source, block, info)
 
 
 def plan_kernel(round_ref, base_ref, most_ref, table_ref, code_ref, tags_ref, found):
@@ -500,6 +501,17 @@
     )(pieces, before)
 
 
+def whole_tiles(rows):
+    return (rows + 15) // 16 * 16
+
+
+def pad_rows(value):
+    spare = whole_tiles(value.shape[0]) - value.shape[0]
+    if spare == 0:
+        return value
+    return jnp.concatenate([value, jnp.zeros((spare, value.shape[1]), value.dtype)], axis=0)
+
+
 def pool_kernel(
     per_owner,
     pieces_ref,
@@ -510,9 +522,7 @@
     shift_ref,
     cot_ref,
     pooled_ref,
-    back_ref,
-    weight_ref,
-    norm_ref,
+    sent_ref,
     acc,
     sums,
     target,
@@ -559,18 +569,41 @@
         * inv_std
     ).astype(BF)
     acc[...] += mm(parent_in, grad_proj, TN)
-    back_ref[...] = mm(grad_proj, w_pool, NT).astype(BF)
+    back = mm(grad_proj, w_pool, NT)
+    devices, _, width = sent_ref.shape
+    fits = chunk // per_owner
+    for d in range(fits):
+        part = back[d * per_owner : (d + 1) * per_owner]
+        sent_ref[step * fits + d, : whole_tiles(per_owner), :] = pad_rows(part).astype(BF)
 
     @pl.when(step == pl.num_programs(0) - 1)
     def _():
-        weight_ref[...] = acc[...].astype(BF)
-        norm_ref[...] = sums[...]
+        each = acc.shape[0] // devices
+        tall = whole_tiles(each)
+        exact = sums[0:2, :]
+        high = exact.astype(BF).astype(F32)
+        parts = []
+        for value in (high, exact - high):
+            for row in range(2):
+                for low in range(0, acc.shape[1], width):
+                    parts.append(value[row : row + 1, low : low + width])
+        norm = pad_rows(jnp.concatenate(parts, axis=0)).astype(BF)
+        for d in range(devices):
+            low = whole_tiles(per_owner)
+            for side in range(0, acc.shape[1], width):
+                part = acc[d * each : (d + 1) * each, side : side + width]
+                sent_ref[d, low : low + tall, :] = pad_rows(part).astype(BF)
+                low += tall
+            sent_ref[d, low:, :] = norm
 
 
 def pool(pieces, more, length, w_pool, gain, shift, cotangent):
     parents, width = more.shape
     wide = w_pool.shape[1]
     chunk = 256
+    devices = pieces.shape[0] // SEAT
+    tall = whole_tiles(parents // devices) + wide // width * whole_tiles(width // devices)
+    tall += whole_tiles(4 * wide // width)
     fixed = lambda i: (0, 0)
     along = lambda i: (i, 0)
     return pl.pallas_call(
@@ -578,9 +611,7 @@
         grid=(parents // chunk,),
         out_shape=(
             jax.ShapeDtypeStruct((parents, wide), BF),
-            jax.ShapeDtypeStruct((parents, width), BF),
-            jax.ShapeDtypeStruct((width, wide), BF),
-            jax.ShapeDtypeStruct((8, wide), F32),
+            jax.ShapeDtypeStruct((devices, tall, width), BF),
         ),
         in_specs=[
             pl.BlockSpec(pieces.shape, fixed),
@@ -593,9 +624,7 @@
         ],
         out_specs=(
             pl.BlockSpec((chunk, wide), along),
-            pl.BlockSpec((chunk, width), along),
-            pl.BlockSpec((width, wide), fixed),
-            pl.BlockSpec((8, wide), fixed),
+            pl.BlockSpec((devices, tall, width), lambda i: (0, 0, 0)),
         ),
         scratch_shapes=[
             pltpu.VMEM((width, wide), F32),
@@ -616,15 +645,18 @@
     def _():
         pick = jnp.where(iota((8, width), 0) == 2, 1.0, 0.0).astype(BF)
         lengths = mm(jnp.minimum(span_ref[...], 64).astype(F32).astype(BF), pick, TN)
-        share[...] = (grad_ref[...].astype(F32) / lengths).astype(BF)
+        per_owner = parents // grad_ref.shape[0]
+        grads = [grad_ref[d, :per_owner, :].astype(F32) for d in range(grad_ref.shape[0])]
+        share[...] = (jnp.concatenate(grads, axis=0) / lengths).astype(BF)
 
     row = iota((chunk, parents), 0) + step * chunk
     inside = (row >= span_ref[0:1, :]) & (row < span_ref[1:2, :])
     out_ref[...] = mm(jnp.where(inside, 1.0, 0.0).astype(BF), share[...]).astype(BF)
 
 
-def spread_grads(span, grad_back, rows):
-    parents, width = grad_back.shape
+def spread_grads(span, arrived, rows):
+    parents = span.shape[1]
+    width = arrived.shape[2]
     chunk = 512
     fixed = lambda i: (0, 0)
     return pl.pallas_call(
@@ -633,13 +665,47 @@
         out_shape=jax.ShapeDtypeStruct((rows, width), BF),
         in_specs=[
             pl.BlockSpec((8, parents), fixed),
-            pl.BlockSpec((parents, width), fixed),
+            pl.BlockSpec(arrived.shape, lambda i: (0, 0, 0)),
         ],
         out_specs=pl.BlockSpec((chunk, width), lambda i: (i, 0)),
         scratch_shapes=[pltpu.VMEM((parents, width), BF)],
         compiler_params=ROOM,
         cost_estimate=cost(2 * rows * parents * width, 4 * rows * width),
-    )(span, grad_back)
+    )(span, arrived)
+
+
+def settle_kernel(per_owner, arrived_ref, shared_ref, norm_ref):
+    devices, tall, width = arrived_ref.shape
+    low = whole_tiles(per_owner)
+    total = arrived_ref[0, low:, :].astype(F32)
+    for d in range(1, devices):
+        total = total + arrived_ref[d, low:, :].astype(F32)
+    weight_rows = shared_ref.shape[1]
+    weight = total[:weight_rows].astype(BF)
+    for d in range(devices):
+        shared_ref[d] = weight
+    norm = total[weight_rows : weight_rows + 8]
+    sides = norm_ref.shape[1] // width
+    for row in range(2):
+        for side in range(sides):
+            i = row * sides + side
+            value = norm[i : i + 1] + norm[2 * sides + i : 2 * sides + i + 1]
+            norm_ref[row : row + 1, side * width : (side + 1) * width] = value
+
+
+def settle(arrived, per_owner, weight_rows, wide):
+    devices, tall, width = arrived.shape
+    return pl.pallas_call(
+        functools.partial(settle_kernel, per_owner),
+        out_shape=(
+            jax.ShapeDtypeStruct((devices, weight_rows, width), BF),
+            jax.ShapeDtypeStruct((2, wide), F32),
+        ),
+        in_specs=[VMEM],
+        out_specs=(VMEM, VMEM),
+        compiler_params=ROOM,
+        cost_estimate=cost(arrived.size, 2 * arrived.size),
+    )(arrived)
 
 
 def swap(parts):
@@ -648,16 +714,6 @@
 
 def exchange(rows, devices):
     return swap(rows.reshape(devices, rows.shape[0] // devices, rows.shape[1])).reshape(rows.shape)
-
-
-def gather_info(info, devices):
-    known = info[None]
-    bit = 1
-    while bit < devices:
-        pairs = [(d, d ^ bit) for d in range(devices)]
-        known = jnp.concatenate([known, lax.ppermute(known, "pts", pairs)], axis=0)
-        bit *= 2
-    return known
 
 
 def received_index(codes, blocks, capacity):
@@ -667,7 +723,7 @@
     slots = codes % blocks
     lane = jnp.arange(blocks)
     rank = jnp.sum(mine[:, None, :] & (lane[None, :] < lane[:, None])[None], axis=2)
-    index = (jnp.arange(devices) ^ me)[:, None] * capacity + rank
+    index = jnp.arange(devices)[:, None] * capacity + rank
     both = index * blocks + lane[None, :]
     hit = mine[:, :, None] & (slots[:, :, None] == lane[None, None, :])
     both = jnp.sum(jnp.where(hit, both[:, :, None], 0), axis=(0, 1)).astype(jnp.int32)
@@ -712,22 +768,21 @@
     capacity = (blocks + devices - 1) // devices
 
     me = lax.axis_index("pts")
-    payload, info, span = front(
-        child_counts, parent_order, hil_dest, hil_slot, points, devices, capacity
-    )
+    info, span = order_tables(child_counts, parent_order, hil_dest, hil_slot, devices)
+    info = swap(info)
+    payload = pack_blocks(hil_dest, points, devices, capacity)
     received = exchange(payload, devices)
-    info = gather_info(info, devices)
     index, block = received_index(info[:, parents // 128, :blocks], blocks, capacity)
     source = index // capacity
     table, local_run, base, most = seat_rows(
-        source, source ^ me, block, info.reshape(devices * INFO, 128), per_owner
+        source, block, info.reshape(devices * INFO, 128), per_owner
     )
     code, tags = plan_seats(jnp.zeros((1,), jnp.int32), base, most, table, devices)
     low, count = key_windows(patch_ids)
     lengths = lax.dynamic_slice_in_dim(
         info[:, : parents // 128].reshape(devices, parents), me * per_owner, per_owner, axis=1
     )
-    lengths = lengths[jnp.arange(devices) ^ me].reshape(parents, 1) % 16
+    lengths = lengths.reshape(parents, 1) % 16
     lengths = jnp.broadcast_to(lengths.astype(F32), (parents, 128))
     more = jnp.zeros((parents, width), F32)
     index, low, count, base, local_run, code, tags, lengths = lax.optimization_barrier(
@@ -746,30 +801,20 @@
     _, more = lax.while_loop(
         lambda carry: carry[0] < rounds.astype(jnp.int32), turn, (jnp.int32(1), more)
     )
-    pooled, back, weight, norm = pool(
+    pooled, outgoing = pool(
         pieces, more, lengths, w_pool, norm_gain[None], norm_shift[None], cotangent
     )
-    norm_high = norm.astype(BF)
-    norm_low = (norm - norm_high.astype(F32)).astype(BF)
-    norm_parts = jnp.concatenate([norm_high[:2], norm_low[:2]], axis=0).reshape(1, -1, width)
-    outgoing = jnp.concatenate(
-        [
-            back.reshape(devices, -1, width),
-            weight.reshape(devices, -1, width),
-            jnp.broadcast_to(norm_parts, (devices,) + norm_parts.shape[1:]),
-        ],
-        axis=1,
-    )
     arrived = swap(outgoing)
-    weight_rows = width * wide // width // devices
-    grad_back = arrived[:, :per_owner].reshape(parents, width)
-    weight_sum = jnp.sum(arrived[:, per_owner : per_owner + weight_rows].astype(F32), axis=0)
-    norm_sum = jnp.sum(arrived[:, per_owner + weight_rows :].astype(F32), axis=0)
-    norm_sum = norm_sum.reshape(4, wide)
-    grad_norm = norm_sum[:2] + norm_sum[2:]
-    shared = jnp.broadcast_to(weight_sum.astype(BF)[None], (devices,) + weight_sum.shape)
-    grad_weight = swap(shared).reshape(width, wide).astype(F32)
-    grad_points = spread_grads(span, grad_back, rows)
+    each = width // devices
+    tall = whole_tiles(each)
+    sides = wide // width
+    shared, grad_norm = settle(arrived, per_owner, sides * tall, wide)
+    shared = swap(shared)
+    grad_weight = jnp.concatenate(
+        [shared[:, side * tall : side * tall + each] for side in range(sides)], axis=2
+    )
+    grad_weight = grad_weight.reshape(width, wide).astype(F32)
+    grad_points = spread_grads(span, arrived, rows)
     return (pooled, grad_points, grad_weight, grad_norm)
 
 

time: 347 us -> 265 us (0.76)
  Pallas kernels: 213 us -> 156 us
  waiting for transfers between devices: 70.8 us -> 45.5 us
  starting transfers between devices: 22.4 us -> 26.9 us
  local copies, waits for them, and re-layouts: 5.53 us -> 1.9 us
    pallas_call x1 -> x3, Pallas kernels: 66.2 us -> 6.48 us  [the longest x1 3.7 us: pack_blocks(): pl.pallas_call(functools.partial(pack_kernel, capacity), out_shape=jax.Sh...]
    ppermute x4 -> x0, waiting for transfers between devices: 43.9 us -> none  [gather_info(): known = jnp.concatenate([known, lax.ppermute(known, 'pts', pairs)], axis=0)]
    all_to_all x3 -> x4, waiting for transfers between devices: 26.9 us -> 45.5 us  [swap(): return lax.all_to_all(parts, 'pts', split_axis=0, concat_axis=0, tiled=True)]
    all_to_all x3 -> x4, starting transfers between devices: 15.3 us -> 26.9 us  [swap(): return lax.all_to_all(parts, 'pts', split_axis=0, concat_axis=0, tiled=True)]
    ppermute x4 -> x0, starting transfers between devices: 7.14 us -> none  [gather_info(): known = jnp.concatenate([known, lax.ppermute(known, 'pts', pairs)], axis=0)]
  transfers between devices with their start and end apart: 7 -> 4, of which waited for: 5 -> 4; matrix products, arithmetic and copies ran while one was open for 1% -> 1% of each run, Pallas kernels for 9% -> 13%
where the time goes in v4:
time: 265 us; the launch traced here: 264 us
  Pallas kernels  156 us (59%)
  waiting for transfers between devices  45.5 us (17%)
  blocking collectives  29.4 us (11%)
  starting transfers between devices  26.9 us (10%)
  other arithmetic  2.8 us (1%)
    pallas_call x1, Pallas kernels, attend(): pl.pallas_call(attend_kernel, out_shape=jax.ShapeDtypeStruct((tiles * spa...  105 us
    all_to_all x4, waiting for transfers between devices, swap(): return lax.all_to_all(parts, 'pts', split_axis=0, concat_axis=0, tiled=True)  45.5 us
    all_to_all x1, blocking collectives, swap(): return lax.all_to_all(parts, 'pts', split_axis=0, concat_axis=0, tiled=True)  29.4 us
    all_to_all x4, starting transfers between devices, swap(): return lax.all_to_all(parts, 'pts', split_axis=0, concat_axis=0, tiled=True)  26.9 us
    pallas_call x1, Pallas kernels, seat_rows(): pl.pallas_call(functools.partial(seat_kernel, per_owner), out_shape=(jax....  20.4 us
    pallas_call x1, Pallas kernels, pool(): pl.pallas_call(functools.partial(pool_kernel, parents * SEAT // pieces.sh...  10.1 us
    pallas_call x1, Pallas kernels, spread_grads(): pl.pallas_call(spread_kernel, grid=(rows // chunk,), out_shape=jax.ShapeD...  5.42 us
  transfers between devices with their start and end apart: 4, of which 4 were waited for; matrix products, arithmetic and copies ran while one was open for 1% of the time, Pallas kernels for 13%

profile of v4, /device:TPU:0, one launch (start us, length us, event | category | flops | bytes accessed | tf_op | source)
XLA Modules:
  0.0 264.2 jit_solution(17366019995241504938)
XLA Ops:
  0.6 2.0 shard_map.147
  2.7 7.4 %all-to-all-start.1 = ((s32[16,16,128]{2,1,0:T(8,128)}), s32[16,16,128]{2,1,0:T(8,128)S(1)}, u32[]{:S(2)}, u32[]{:S(2)}) async-start(s32[16,16,128]{2,1,0:T(8,128)} %get-tuple-element.64), calls=%async_computation.1 | async-start | bytes 262144 | tf_op jit(solution)/shard_map/all_to_all | solution.py:712
  10.0 3.7 %shard_map.150 = bf16[4096,256]{1,0:T(8,128)(2,1)} custom-call(s32[32]{0:T(128)} %dest_ref.1, bf16[4096,256]{1,0:T(8,128)(2,1)} %points_ref.1), custom_call_target="tpu_custom_call" | custom-call | bytes 4194304 | tf_op jit(solution)/shard_map/pallas_call | solution.py:122
  13.8 4.2 %all-to-all-done.1 = s32[16,16,128]{2,1,0:T(8,128)S(1)} async-done(((s32[16,16,128]{2,1,0:T(8,128)}), s32[16,16,128]{2,1,0:T(8,128)S(1)}, u32[]{:S(2)}, u32[]{:S(2)}) %all-to-all-start.1) | async-done | bytes 131104 | tf_op jit(solution)/shard_map/all_to_all | solution.py:712
  18.0 0.0 copy-start
  18.0 3.9 %all-to-all-start.2 = ((bf16[16,256,256]{2,1,0:T(8,128)(2,1)}), bf16[16,256,256]{2,1,0:T(8,128)(2,1)S(1)}, u32[]{:S(2)}, u32[]{:S(2)}) async-start(bf16[16,256,256]{2,1,0:T(8,128)(2,1)} %bitcast.39), calls=%async_computation.2 | async-start | bytes 4194304 | tf_op jit(solution)/shard_map/all_to_all | solution.py:712
  21.8 0.0 copy-start.1
  21.9 0.0 copy-start.2
  21.9 0.0 copy-done
  21.9 0.1 fusion.9
  22.0 0.1 copy.23
  22.1 0.1 copy.27
  22.2 0.2 convert_reduce_fusion.1
  22.4 0.1 select_reduce_fusion.1
  22.4 0.1 reduce_sum.55
  22.5 0.1 reduce_sum.53
  22.6 0.1 fusion.2
  22.8 0.1 constant_dynamic-slice_fusion
  22.8 0.1 reshape.176
  22.9 0.3 convert_reduce_fusion
  23.3 0.1 add_select_fusion
  23.4 0.3 select_reduce_fusion
  23.7 20.4 %shard_map.148 = (bf16[4608,128]{1,0:T(8,128)(2,1)}, s32[32,128]{1,0:T(8,128)S(1)}, s32[33]{0:T(128)S(1)}, f32[8,128]{1,0:T(8,128)S(1)}) custom-call(s32[32]{0:T(128)S(1)} %get-tuple-element.101.source_ref, s32[32]{0:T(128)S(1)} %get-tuple-element.109.block_ref, s32[256,128]{1,0:T(8,128)S(1)} %bitcast.37), custom_call_target="tpu_custom_call" | custom-call | flops 167772160 | bytes 32768 | tf_op jit(solution)/shard_map/pallas_call | solution.py:215
  44.1 4.1 %shard_map.149 = (s32[8,4608]{1,0:T(8,128)S(1)}, f32[8,2048]{1,0:T(8,128)S(1)}) custom-call(s32[1]{0:T(128)} %constant.116.clone.1.round_ref, s32[33]{0:T(128)S(1)} %get-tuple-element.163.base_ref, f32[8,128]{1,0:T(8,128)S(1)} %get-tuple-element.164.most_ref, bf16[4608,128]{1,0:T(8,128)(2,1)} %get-tuple-element.165.table_ref), custom_call_target="tpu_custom_call" | custom-call | flops 603979776 | bytes 2359296 | tf_op jit(solution)/shard_map/pallas_call | solution.py:261
  48.2 1.0 broadcast_in_dim.71.length_ref
  49.2 13.7 %all-to-all-done.2 = bf16[16,256,256]{2,1,0:T(8,128)(2,1)S(1)} async-done(((bf16[16,256,256]{2,1,0:T(8,128)(2,1)}), bf16[16,256,256]{2,1,0:T(8,128)(2,1)S(1)}, u32[]{:S(2)}, u32[]{:S(2)}) %all-to-all-start.2) | async-done | bytes 2097184 | tf_op jit(solution)/shard_map/all_to_all | solution.py:712
  62.9 0.0 copy-done.1
  62.9 0.0 copy-done.2
  62.9 104.5 %shard_map.151.sums_ref = bf16[4608,256]{1,0:T(8,128)(2,1)} custom-call(s32[32]{0:T(128)S(1)} %get-tuple-element.74.index_ref, s32[32]{0:T(128)S(1)} %get-tuple-element.75.low_ref, s32[32]{0:T(128)S(1)} %get-tuple-element.76.count_ref, s32[33]{0:T(128)S(1)} %get-tuple-element.163.base_ref, s32[32,128]{1,0:T(8,128)S(1)} %get-tuple-element.77.local_ref, ...), custom_call_target="tpu_custom_call" | custom-call | flops 34359738368 | bytes 4194304 | tf_op jit(solution)/shard_map/pallas_call | solution.py:399
  167.4 5.0 %shard_map.152 = bf16[2048,256]{1,0:T(8,128)(2,1)} custom-call(s32[33]{0:T(128)S(1)} %get-tuple-element.163.base_ref, s32[8,4608]{1,0:T(8,128)S(1)} %get-tuple-element.72.code_ref, f32[8,2048]{1,0:T(8,128)S(1)} %get-tuple-element.73.tags_ref, bf16[4608,256]{1,0:T(8,128)(2,1)} %shard_map.151.sums_ref), custom_call_target="tpu_custom_call" | custom-call | flops 2415919104 | bytes 4718592 | tf_op jit(solution)/shard_map/pallas_call | solution.py:446
  172.4 11.2 %all-to-all-start.3 = ((bf16[16,128,256]{2,1,0:T(8,128)(2,1)}), bf16[16,128,256]{2,1,0:T(8,128)(2,1)S(1)}, u32[]{:S(2)}, u32[]{:S(2)}) async-start(bf16[16,128,256]{2,1,0:T(8,128)(2,1)} %bitcast.11), calls=%async_computation.3 | async-start | bytes 2097152 | tf_op jit(solution)/shard_map/all_to_all | solution.py:712
  183.6 22.9 %all-to-all-done.3 = bf16[16,128,256]{2,1,0:T(8,128)(2,1)S(1)} async-done(((bf16[16,128,256]{2,1,0:T(8,128)(2,1)}), bf16[16,128,256]{2,1,0:T(8,128)(2,1)S(1)}, u32[]{:S(2)}, u32[]{:S(2)}) %all-to-all-start.3) | async-done | bytes 1048608 | tf_op jit(solution)/shard_map/all_to_all | solution.py:712
  206.6 0.0 copy-start.4
  206.6 0.7 slice_reduce_fusion
  207.3 0.3 copy-done.4
  208.2 0.1 broadcast_in_dim.72
  208.3 0.2 while.10
  208.5 10.1 %shard_map.153 = (bf16[1024,512]{1,0:T(8,128)(2,1)}, bf16[16,112,256]{2,1,0:T(8,128)(2,1)}) custom-call(bf16[2048,256]{1,0:T(8,128)(2,1)} %bitcast.40, f32[1024,256]{1,0:T(8,128)S(1)} %get-tuple-element.78.more_ref, f32[1024,128]{1,0:T(8,128)} %broadcast_in_dim.71.length_ref, bf16[256,512]{1,0:T(8,128)(2,1)} %w_ref.3, f32[1,512]{1,0:T(1,128)} %bitcast.49, ...), custom_call_target="tpu_custom_call" | custom-call | flops 805306368 | bytes 4194304 | tf_op jit(solution)/shard_map/pallas_call | solution.py:609
  218.6 0.0 copy-start.3
  218.6 29.4 %all_to_all.31.grad_ref.arrived_ref = bf16[16,112,256]{2,1,0:T(8,128)(2,1)S(1)} all-to-all(bf16[16,112,256]{2,1,0:T(8,128)(2,1)} %get-tuple-element.82), channel_id=1, replica_groups=mesh['grp'=2,'pts'=16] {'pts'}, dimensions={0} | all-to-all | bytes 1835008 | tf_op jit(solution)/shard_map/all_to_all | solution.py:712
  248.0 0.8 shard_map.155
  248.8 4.5 %all-to-all-start.5 = ((bf16[16,32,256]{2,1,0:T(8,128)(2,1)}), bf16[16,32,256]{2,1,0:T(8,128)(2,1)S(1)}, u32[]{:S(2)}, u32[]{:S(2)}) async-start(bf16[16,32,256]{2,1,0:T(8,128)(2,1)} %get-tuple-element.83), calls=%async_computation.5 | async-start | bytes 524288 | tf_op jit(solution)/shard_map/all_to_all | solution.py:712
  253.3 0.0 copy-done.3
  253.3 5.4 %shard_map.154 = bf16[4096,256]{1,0:T(8,128)(2,1)} custom-call(s32[8,1024]{1,0:T(8,128)S(1)} %copy-done.3, bf16[16,112,256]{2,1,0:T(8,128)(2,1)S(1)} %all_to_all.31.grad_ref.arrived_ref), custom_call_target="tpu_custom_call" | custom-call | flops 2147483648 | bytes 4194304 | tf_op jit(solution)/shard_map/pallas_call | solution.py:662
  258.7 4.6 %all-to-all-done.5 = bf16[16,32,256]{2,1,0:T(8,128)(2,1)S(1)} async-done(((bf16[16,32,256]{2,1,0:T(8,128)(2,1)}), bf16[16,32,256]{2,1,0:T(8,128)(2,1)S(1)}, u32[]{:S(2)}, u32[]{:S(2)}) %all-to-all-start.5) | async-done | bytes 262176 | tf_op jit(solution)/shard_map/all_to_all | solution.py:712
  263.4 0.9 bitcast_convert_fusion
  (13 shorter events, 0.2 us)
Async XLA Ops:
  2.7 15.3 %all-to-all-start.1 = ((s32[16,16,128]{2,1,0:T(8,128)}), s32[16,16,128]{2,1,0:T(8,128)S(1)}, u32[]{:S(2)}, u32[]{:S(2)}) async-start(s32[16,16,128]{2,1,0:T(8,128)} %get-tuple-element.64), calls=%async_computation.1 | async-start | bytes 262144 | tf_op jit(solution)/shard_map/all_to_all | solution.py:712
  18.0 3.9 %copy-start = (s32[4,1024]{1,0:T(4,128)S(1)}, s32[4,1024]{1,0:T(4,128)}, u32[]{:S(2)}) copy-start(s32[4,1024]{1,0:T(4,128)} %ids_ref.1) | copy-start | bytes 49156
  18.0 44.9 %all-to-all-start.2 = ((bf16[16,256,256]{2,1,0:T(8,128)(2,1)}), bf16[16,256,256]{2,1,0:T(8,128)(2,1)S(1)}, u32[]{:S(2)}, u32[]{:S(2)}) async-start(bf16[16,256,256]{2,1,0:T(8,128)(2,1)} %bitcast.39), calls=%async_computation.2 | async-start | bytes 4194304 | tf_op jit(solution)/shard_map/all_to_all | solution.py:712
  21.8 41.0 %copy-start.1 = (bf16[256,768]{1,0:T(8,128)(2,1)S(1)}, bf16[256,768]{1,0:T(8,128)(2,1)}, u32[]{:S(2)}) copy-start(bf16[256,768]{1,0:T(8,128)(2,1)} %w_ref.2) | copy-start | bytes 1179652
  21.9 41.0 %copy-start.2 = (bf16[256,256]{1,0:T(8,128)(2,1)S(1)}, bf16[256,256]{1,0:T(8,128)(2,1)}, u32[]{:S(2)}) copy-start(bf16[256,256]{1,0:T(8,128)(2,1)} %wo_ref.1) | copy-start | bytes 393220
  172.4 34.1 %all-to-all-start.3 = ((bf16[16,128,256]{2,1,0:T(8,128)(2,1)}), bf16[16,128,256]{2,1,0:T(8,128)(2,1)S(1)}, u32[]{:S(2)}, u32[]{:S(2)}) async-start(bf16[16,128,256]{2,1,0:T(8,128)(2,1)} %bitcast.11), calls=%async_computation.3 | async-start | bytes 2097152 | tf_op jit(solution)/shard_map/all_to_all | solution.py:712
  206.6 1.0 copy-start.4
  218.6 34.7 %copy-start.3 = (s32[8,1024]{1,0:T(8,128)S(1)}, s32[8,1024]{1,0:T(8,128)}, u32[]{:S(2)}) copy-start(s32[8,1024]{1,0:T(8,128)} %get-tuple-element.81.span_ref) | copy-start | bytes 98308
  248.8 14.5 %all-to-all-start.5 = ((bf16[16,32,256]{2,1,0:T(8,128)(2,1)}), bf16[16,32,256]{2,1,0:T(8,128)(2,1)S(1)}, u32[]{:S(2)}, u32[]{:S(2)}) async-start(bf16[16,32,256]{2,1,0:T(8,128)(2,1)} %get-tuple-element.83), calls=%async_computation.5 | async-start | bytes 524288 | tf_op jit(solution)/shard_map/all_to_all | solution.py:712

commit v5 on v4

--- a/solution.py
+++ b/solution.py
@@ -276,11 +276,22 @@
     )(step, base, most, table)
 
 
+def rotate_rows(doubled, turn, span):
+    coarse = pl.multiple_of(turn // 8 * 8, 8)
+    fine = turn % 8
+    width = doubled.shape[1]
+    rows = doubled[pl.ds(coarse, span + 8), :].reshape(span // 8 + 1, 8, width)
+    rolled = pltpu.roll(rows, (8 - fine) % 8, 1)
+    kept = iota((span // 8, 8, width), 1) < 8 - fine
+    return jnp.where(kept, rolled[:-1], rolled[1:]).reshape(span, width)
+
+
 def attend_kernel(
     index_ref,
     low_ref,
     count_ref,
     base_ref,
+    turn_ref,
     local_ref,
     ids_ref,
     w_ref,
@@ -292,6 +303,9 @@
     kx,
     vx,
     att,
+    doubled,
+    wrapped,
+    code,
     sems,
 ):
     tiles, span = ids_ref.shape
@@ -301,30 +315,39 @@
     heads = width // HDIM
     per_tile = span // ROWS
 
-    for t in range(tiles):
-        for b in range(per_tile):
-            s = t * per_tile + b
+    def fetch(t):
+        for s in range(t * per_tile, (t + 1) * per_tile):
             pltpu.make_async_copy(
                 rows_ref.at[pl.ds(pl.multiple_of(index_ref[s] * ROWS, ROWS), ROWS)],
                 x.at[pl.ds(s * ROWS, ROWS)],
                 sems.at[t],
             ).start()
 
+    fetch(0)
     out_ref[...] = jnp.zeros_like(out_ref)
     lane = iota((ROWS, 2 * cols), 1)
     of_head = [(lane // HDIM == h) | (lane >= cols) for h in range(HEAD_GROUP)]
     lane_out = lane % cols // HDIM
     for g in range(groups):
-        vx[g, :, cols:] = jnp.ones((span, cols), BF)
+        vx[g, :, cols:] = jnp.ones((tiles * span, cols), BF)
     r_i = iota((cols, cols), 0)
     c_i = iota((cols, cols), 1)
     far = jnp.where((r_i != c_i) & (c_i < PATCHES), -FAR, 0.0).astype(BF)
-
-    def tile(t, _):
-        at = pl.ds(pl.multiple_of(t * span, span), span)
-        pltpu.make_async_copy(rows_ref.at[pl.ds(0, span)], x.at[at], sems.at[t]).wait()
-        tile_rows = x[at, :]
-        same = ids_ref[pl.ds(t, 1), :] == iota((cols, span), 0)
+    bounds = []
+
+    for t in range(tiles):
+        at = slice(t * span, (t + 1) * span)
+        if t + 1 < tiles:
+            fetch(t + 1)
+        pltpu.make_async_copy(
+            rows_ref.at[pl.ds(0, span)], x.at[pl.ds(t * span, span)], sems.at[t]
+        ).wait()
+        whole = x[at, :].astype(F32)
+        doubled[:span, :] = whole
+        doubled[span:, :] = whole
+        tile_rows = rotate_rows(doubled, turn_ref[t], span).astype(BF)
+        x[at, :] = tile_rows
+        same = ids_ref[t : t + 1, :] == iota((cols, span), 0)
         patch_hot = jnp.where(same, 1.0, 0.0).astype(BF)
         query = mm(tile_rows, w_ref[:, :width])
         keys = mm(w_ref[:, width : 2 * width], tile_rows, (((0,), (1,)), ((), ())))
@@ -332,65 +355,78 @@
         patch_far = mm(patch_hot, far, TN).astype(BF)
         for g in range(groups):
             some = slice(g * cols, (g + 1) * cols)
-            qx[g, :, :cols] = query[:, some].astype(BF)
-            qx[g, :, cols:] = patch_far
-            kx[g, :cols, :] = keys[some].astype(BF)
-            kx[g, cols:, :] = patch_hot
-            vx[g, :, :cols] = value[:, some]
+            qx[g, at, :cols] = query[:, some].astype(BF)
+            qx[g, at, cols:] = patch_far
+            kx[g, :cols, at] = keys[some].astype(BF)
+            kx[g, cols:, at] = patch_hot
+            vx[g, at, :cols] = value[:, some]
         query_most = jnp.max(jnp.abs(query), axis=0, keepdims=True)
         key_most = jnp.max(jnp.abs(keys), axis=1, keepdims=True)
         by_head = jnp.where(
             iota((heads, width), 1) // HDIM == iota((heads, width), 0), query_most, 0.0
         )
-        bound = jnp.max(mm(by_head.astype(BF), jnp.broadcast_to(key_most, (width, 128)).astype(BF)))
-        safe = bound * SCORE_SCALE < SCORE_SAFE
-
-        def block(b, _):
-            low = pl.multiple_of(low_ref[t * per_tile + b], ROWS)
-            steps = count_ref[t * per_tile + b]
-            here = pl.ds(pl.multiple_of(b * ROWS, ROWS), ROWS)
-
-            def run(start, length, exact):
-                scores = []
-                for g in range(groups):
-                    q = qx[g, here, :]
-                    stacked = jnp.concatenate(
-                        [jnp.where(of_head[h], q, jnp.zeros_like(q)) for h in range(HEAD_GROUP)],
-                        axis=0,
-                    )
-                    scores.append(mm(stacked, kx[g, :, pl.ds(start, length)]))
-                for g in range(groups):
-                    level = scores[g] * SCORE_SCALE
-                    if exact:
-                        level = level - jnp.max(level, axis=1, keepdims=True)
-                    weights = jnp.exp2(level).astype(BF)
-                    mixed = mm(weights, vx[g, pl.ds(start, length), :])
-                    mixed = mixed.reshape(HEAD_GROUP, ROWS, 2 * cols)
-                    own = mixed[0]
-                    for h in range(1, HEAD_GROUP):
-                        own = jnp.where(lane_out == h, mixed[h], own)
-                    att[here, g * cols : (g + 1) * cols] = (own[:, :cols] / own[:, cols:]).astype(BF)
-
-            for i in range(span // WINDOW):
-                pl.when(safe & (steps == i + 1))(
-                    functools.partial(run, low, (i + 1) * WINDOW, False)
+        bounds.append(mm(by_head.astype(BF), jnp.broadcast_to(key_most, (width, 128)).astype(BF)))
+    bound = bounds[0]
+    for other in bounds[1:]:
+        bound = jnp.maximum(bound, other)
+    safe = jnp.max(bound) * SCORE_SCALE < SCORE_SAFE
+
+    def block(s, _):
+        start = pl.multiple_of(s // per_tile * span, span)
+        steps = count_ref[s]
+        here = pl.ds(pl.multiple_of(s * ROWS, ROWS), ROWS)
+
+        def run(first, length, exact):
+            at = pl.ds(pl.multiple_of(start + first, ROWS), length)
+            scores = []
+            for g in range(groups):
+                q = qx[g, here, :]
+                stacked = jnp.concatenate(
+                    [jnp.where(of_head[h], q, jnp.zeros_like(q)) for h in range(HEAD_GROUP)],
+                    axis=0,
                 )
-            pl.when(jnp.logical_not(safe))(functools.partial(run, 0, span, True))
-            return 0
-
-        lax.fori_loop(0, per_tile, block, 0)
-        mixed = (tile_rows.astype(F32) + mm(att[...], wo_ref[...])).astype(BF)
+                scores.append(mm(stacked, kx[g, :, at]))
+            for g in range(groups):
+                level = scores[g] * SCORE_SCALE
+                if exact:
+                    level = level - jnp.max(level, axis=1, keepdims=True)
+                weights = jnp.exp2(level).astype(BF)
+                mixed = mm(weights, vx[g, at, :])
+                mixed = mixed.reshape(HEAD_GROUP, ROWS, 2 * cols)
+                own = mixed[0]
+                for h in range(1, HEAD_GROUP):
+                    own = jnp.where(lane_out == h, mixed[h], own)
+                att[here, g * cols : (g + 1) * cols] = (own[:, :cols] / own[:, cols:]).astype(BF)
+
+        for i in range(span // WINDOW):
+            pl.when(safe & (steps == i + 1))(
+                functools.partial(run, low_ref[s], (i + 1) * WINDOW, False)
+            )
+        pl.when(jnp.logical_not(safe))(functools.partial(run, 0, span, True))
+        return 0
+
+    lax.fori_loop(0, tiles * per_tile, block, 0)
+
+    for t in range(tiles):
+        at = slice(t * span, (t + 1) * span)
+        turn = turn_ref[t]
+        mixed = (x[at, :].astype(F32) + mm(att[at, :], wo_ref[...])).astype(BF)
+        wrapped[t, :span, :] = mixed
+        wrapped[t, span:, :] = mixed[:ROWS]
+        runs = local_ref[t : t + 1, :] + iota((1, span), 1) // ROWS * ROWS
+        runs = pltpu.roll(jnp.broadcast_to(runs, (8, span)), lax.rem(span - turn, span), 1)
+        code[t, :, :span] = runs
+        code[t, :, span:] = runs[:, :ROWS]
         for b in range(per_tile):
-            s = t * per_tile + b
-            run = jnp.where(iota((ROWS, ROWS), 0) == local_ref[pl.ds(s, 1), :], 1.0, 0.0)
-            sums = mm(run.astype(BF), mixed[b * ROWS : (b + 1) * ROWS])
-            out_ref[pl.ds(pl.multiple_of(base_ref[s], ALIGN), ROWS), :] = sums.astype(BF)
-        return 0
-
-    lax.fori_loop(0, tiles, tile, 0)
-
-
-def attend(index, low, count, base, local, ids, w_qkv, w_out, rows):
+            first = lax.rem(b * ROWS + span - turn, span) // ROWS * ROWS
+            window = pl.ds(pl.multiple_of(first, ROWS), 2 * ROWS)
+            run = iota((ROWS, 2 * ROWS), 0) + b * ROWS == code[t, 0:1, window]
+            sums = mm(jnp.where(run, 1.0, 0.0).astype(BF), wrapped[t, window, :])
+            put = pl.multiple_of(base_ref[t * per_tile + b], ALIGN)
+            out_ref[pl.ds(put, ROWS), :] = sums.astype(BF)
+
+
+def attend(index, low, count, base, turn, local, ids, w_qkv, w_out, rows):
     tiles, span = ids.shape
     width = rows.shape[1]
     cols = HEAD_GROUP * HDIM
@@ -399,19 +435,22 @@
     return pl.pallas_call(
         attend_kernel,
         out_shape=jax.ShapeDtypeStruct((tiles * span + CHUNK, width), BF),
-        in_specs=[SMEM, SMEM, SMEM, SMEM, VMEM, VMEM, VMEM, VMEM, HBM],
+        in_specs=[SMEM, SMEM, SMEM, SMEM, SMEM, VMEM, VMEM, VMEM, VMEM, HBM],
         out_specs=VMEM,
         scratch_shapes=[
             pltpu.VMEM((tiles * span, width), BF),
-            pltpu.VMEM((groups, span, 2 * cols), BF),
-            pltpu.VMEM((groups, 2 * cols, span), BF),
-            pltpu.VMEM((groups, span, 2 * cols), BF),
-            pltpu.VMEM((span, width), BF),
+            pltpu.VMEM((groups, tiles * span, 2 * cols), BF),
+            pltpu.VMEM((groups, 2 * cols, tiles * span), BF),
+            pltpu.VMEM((groups, tiles * span, 2 * cols), BF),
+            pltpu.VMEM((tiles * span, width), BF),
+            pltpu.VMEM((2 * span, width), F32),
+            pltpu.VMEM((tiles, span + ROWS, width), BF),
+            pltpu.VMEM((tiles, 8, span + ROWS), jnp.int32),
             pltpu.SemaphoreType.DMA((tiles,)),
         ],
         compiler_params=ROOM,
         cost_estimate=cost(pairs * 1024, 4 * rows.size, pairs),
-    )(index, low, count, base, local, ids, w_qkv, w_out, rows)
+    )(index, low, count, base, turn, local, ids, w_qkv, w_out, rows)
 
 
 def route_kernel(base_ref, code_ref, tags_ref, sums_ref, out_ref, acc):
@@ -732,17 +771,25 @@
 
 def key_windows(patch_ids):
     tiles, span = patch_ids.shape
-    patch = jnp.arange(PATCHES + 1)
-    starts = jnp.sum(patch_ids[:, None, :] < patch[None, :, None], axis=2)
-    by_block = patch_ids.reshape(tiles, span // ROWS, ROWS)
-    first, last = by_block[:, :, 0], by_block[:, :, -1]
-    pick = lambda which: jnp.sum(
-        jnp.where(which[:, :, None] == patch[None, None, :], starts[:, None, :], 0), axis=2
-    )
-    low = pick(first) // ROWS * ROWS
-    count = (pick(last + 1) - low + WINDOW - 1) // WINDOW
+    patch = jnp.arange(PATCHES)
+    sizes = jnp.sum(patch_ids[:, None, :] == patch[None, :, None], axis=2)
+    starts = jnp.sum(jnp.where(patch[None, :] < patch[:, None], sizes[:, None, :], 0), axis=2)
+    longest = sizes == jnp.max(sizes, axis=1, keepdims=True)
+    turn = jnp.min(jnp.where(longest, starts, span), axis=1)
+    firsts = (starts - turn[:, None]) % span
+    row = jnp.arange(span)[None, :, None]
+    inside = (row >= firsts[:, None, :]) & (row < (firsts + sizes)[:, None, :])
+    turned = jnp.sum(jnp.where(inside, patch, 0), axis=2)
+    block = jnp.arange(0, span, ROWS)[None, :, None]
+    starts_in = (block >= firsts[:, None, :]) & (block < (firsts + sizes)[:, None, :])
+    ending = block + ROWS - 1
+    ends_in = (ending >= firsts[:, None, :]) & (ending < (firsts + sizes)[:, None, :])
+    low = jnp.sum(jnp.where(starts_in, firsts[:, None, :], 0), axis=2) // ROWS * ROWS
+    high = jnp.sum(jnp.where(ends_in, (firsts + sizes)[:, None, :], 0), axis=2)
+    count = (high - low + WINDOW - 1) // WINDOW
     low = jnp.minimum(low, span - count * WINDOW)
-    return low.reshape(-1).astype(jnp.int32), count.reshape(-1).astype(jnp.int32)
+    as_int = lambda value: value.astype(jnp.int32)
+    return as_int(low.reshape(-1)), as_int(count.reshape(-1)), as_int(turn), as_int(turned)
 
 
 def local(
@@ -778,17 +825,20 @@
         source, block, info.reshape(devices * INFO, 128), per_owner
     )
     code, tags = plan_seats(jnp.zeros((1,), jnp.int32), base, most, table, devices)
-    low, count = key_windows(patch_ids)
+    low, count, turn, turned = key_windows(patch_ids)
     lengths = lax.dynamic_slice_in_dim(
         info[:, : parents // 128].reshape(devices, parents), me * per_owner, per_owner, axis=1
     )
     lengths = lengths.reshape(parents, 1) % 16
     lengths = jnp.broadcast_to(lengths.astype(F32), (parents, 128))
     more = jnp.zeros((parents, width), F32)
-    index, low, count, base, local_run, code, tags, lengths = lax.optimization_barrier(
-        (index, low, count, base, local_run, code, tags, lengths)
-    )
-    sums = attend(index, low, count, base, local_run, patch_ids, w_qkv, w_out, received)
+    index, low, count, turn, turned, base, local_run, code, tags, lengths = (
+        lax.optimization_barrier(
+            (index, low, count, turn, turned, base, local_run, code, tags, lengths)
+        )
+    )
+    local_run = local_run.reshape(patch_ids.shape)
+    sums = attend(index, low, count, base, turn, local_run, turned, w_qkv, w_out, received)
     pieces = exchange(route_sums(base, code, tags, sums), devices)
     rounds = jnp.max(pieces.reshape(devices, SEAT, width)[:, SEATS + 1, 0].astype(F32))
 

time: 265 us -> 265 us (level)
  no operation moved by 1% of the time
where the time goes in v5:
time: 265 us; the launch traced here: 264 us
  Pallas kernels  156 us (59%)
  waiting for transfers between devices  45.1 us (17%)
  blocking collectives  29.4 us (11%)
  starting transfers between devices  26.9 us (10%)
  other arithmetic  3.38 us (1%)
    pallas_call x1, Pallas kernels, attend(): pl.pallas_call(attend_kernel, out_shape=jax.ShapeDtypeStruct((tiles * spa...  105 us
    all_to_all x4, waiting for transfers between devices, swap(): return lax.all_to_all(parts, 'pts', split_axis=0, concat_axis=0, tiled=True)  45.1 us
    all_to_all x1, blocking collectives, swap(): return lax.all_to_all(parts, 'pts', split_axis=0, concat_axis=0, tiled=True)  29.4 us
    all_to_all x4, starting transfers between devices, swap(): return lax.all_to_all(parts, 'pts', split_axis=0, concat_axis=0, tiled=True)  26.9 us
    pallas_call x1, Pallas kernels, seat_rows(): pl.pallas_call(functools.partial(seat_kernel, per_owner), out_shape=(jax....  20.4 us
    pallas_call x1, Pallas kernels, pool(): pl.pallas_call(functools.partial(pool_kernel, parents * SEAT // pieces.sh...  10.1 us
    pallas_call x1, Pallas kernels, spread_grads(): pl.pallas_call(spread_kernel, grid=(rows // chunk,), out_shape=jax.ShapeD...  5.41 us
  transfers between devices with their start and end apart: 4, of which 4 were waited for; matrix products, arithmetic and copies ran while one was open for 1% of the time, Pallas kernels for 13%

profile of v5, /device:TPU:0, one launch (start us, length us, event | category | flops | bytes accessed | tf_op | source)
XLA Modules:
  0.0 264.4 jit_solution(6557294798192776787)
XLA Ops:
  0.6 2.0 shard_map.147
  2.7 7.4 %all-to-all-start.1 = ((s32[16,16,128]{2,1,0:T(8,128)}), s32[16,16,128]{2,1,0:T(8,128)S(1)}, u32[]{:S(2)}, u32[]{:S(2)}) async-start(s32[16,16,128]{2,1,0:T(8,128)} %get-tuple-element.66), calls=%async_computation.1 | async-start | bytes 262144 | tf_op jit(solution)/shard_map/all_to_all | solution.py:751
  10.0 3.7 %shard_map.150 = bf16[4096,256]{1,0:T(8,128)(2,1)} custom-call(s32[32]{0:T(128)} %dest_ref.1, bf16[4096,256]{1,0:T(8,128)(2,1)} %points_ref.1), custom_call_target="tpu_custom_call" | custom-call | bytes 4194304 | tf_op jit(solution)/shard_map/pallas_call | solution.py:122
  13.8 4.2 %all-to-all-done.1 = s32[16,16,128]{2,1,0:T(8,128)S(1)} async-done(((s32[16,16,128]{2,1,0:T(8,128)}), s32[16,16,128]{2,1,0:T(8,128)S(1)}, u32[]{:S(2)}, u32[]{:S(2)}) %all-to-all-start.1) | async-done | bytes 131104 | tf_op jit(solution)/shard_map/all_to_all | solution.py:751
  18.0 0.0 copy-start.4
  18.0 3.9 %all-to-all-start.2 = ((bf16[16,256,256]{2,1,0:T(8,128)(2,1)}), bf16[16,256,256]{2,1,0:T(8,128)(2,1)S(1)}, u32[]{:S(2)}, u32[]{:S(2)}) async-start(bf16[16,256,256]{2,1,0:T(8,128)(2,1)} %bitcast.32), calls=%async_computation.2 | async-start | bytes 4194304 | tf_op jit(solution)/shard_map/all_to_all | solution.py:751
  21.8 0.0 copy-start
  21.9 0.0 copy-start.1
  21.9 0.0 copy-done.4
  21.9 0.2 convert_reduce_fusion.1
  22.0 0.1 reduce_max.23
  22.2 0.1 select_reduce_fusion.4
  22.3 0.2 select_reduce_fusion.5.turn_ref
  22.5 0.1 fusion.10
  22.6 0.1 select_reduce_fusion.2
  22.7 0.1 reduce_sum.74
  22.8 0.1 reduce_sum.72
  22.9 0.1 select_reduce_fusion.1.ids_ref
  23.0 0.1 fusion.3
  23.2 0.1 constant_dynamic-slice_fusion
  23.2 0.1 reshape.224
  23.3 0.3 convert_reduce_fusion
  23.7 0.1 add_select_fusion
  23.8 0.3 select_reduce_fusion
  24.1 20.4 %shard_map.148 = (bf16[4608,128]{1,0:T(8,128)(2,1)}, s32[32,128]{1,0:T(8,128)S(1)}, s32[33]{0:T(128)S(1)}, f32[8,128]{1,0:T(8,128)S(1)}) custom-call(s32[32]{0:T(128)S(1)} %get-tuple-element.105.source_ref, s32[32]{0:T(128)S(1)} %get-tuple-element.113.block_ref, s32[256,128]{1,0:T(8,128)S(1)} %bitcast.31), custom_call_target="tpu_custom_call" | custom-call | flops 167772160 | bytes 32768 | tf_op jit(solution)/shard_map/pallas_call | solution.py:215
  44.5 4.0 %shard_map.149 = (s32[8,4608]{1,0:T(8,128)S(1)}, f32[8,2048]{1,0:T(8,128)S(1)}) custom-call(s32[1]{0:T(128)} %constant.137.clone.1.round_ref, s32[33]{0:T(128)S(1)} %get-tuple-element.169.base_ref, f32[8,128]{1,0:T(8,128)S(1)} %get-tuple-element.170.most_ref, bf16[4608,128]{1,0:T(8,128)(2,1)} %get-tuple-element.171.table_ref), custom_call_target="tpu_custom_call" | custom-call | flops 603979776 | bytes 2359296 | tf_op jit(solution)/shard_map/pallas_call | solution.py:261
  48.5 1.0 broadcast_in_dim.112.length_ref
  49.5 13.3 %all-to-all-done.2 = bf16[16,256,256]{2,1,0:T(8,128)(2,1)S(1)} async-done(((bf16[16,256,256]{2,1,0:T(8,128)(2,1)}), bf16[16,256,256]{2,1,0:T(8,128)(2,1)S(1)}, u32[]{:S(2)}, u32[]{:S(2)}) %all-to-all-start.2) | async-done | bytes 2097184 | tf_op jit(solution)/shard_map/all_to_all | solution.py:751
  62.9 0.0 copy-done
  62.9 0.0 copy-done.1
  62.9 104.7 %shard_map.151.sums_ref = bf16[4608,256]{1,0:T(8,128)(2,1)} custom-call(s32[32]{0:T(128)S(1)} %get-tuple-element.76.index_ref, s32[32]{0:T(128)S(1)} %get-tuple-element.77.low_ref, s32[32]{0:T(128)S(1)} %get-tuple-element.78.count_ref, s32[33]{0:T(128)S(1)} %get-tuple-element.169.base_ref, s32[4]{0:T(128)S(1)} %select_reduce_fusion.5.turn_ref, ...), custom_call_target="tpu_custom_call" | custom-call | flops 34359738368 | bytes 4194304 | tf_op jit(solution)/shard_map/pallas_call | solution.py:435
  167.6 5.0 %shard_map.152 = bf16[2048,256]{1,0:T(8,128)(2,1)} custom-call(s32[33]{0:T(128)S(1)} %get-tuple-element.169.base_ref, s32[8,4608]{1,0:T(8,128)S(1)} %get-tuple-element.74.code_ref, f32[8,2048]{1,0:T(8,128)S(1)} %get-tuple-element.75.tags_ref, bf16[4608,256]{1,0:T(8,128)(2,1)} %shard_map.151.sums_ref), custom_call_target="tpu_custom_call" | custom-call | flops 2415919104 | bytes 4718592 | tf_op jit(solution)/shard_map/pallas_call | solution.py:485
  172.6 11.2 %all-to-all-start.3 = ((bf16[16,128,256]{2,1,0:T(8,128)(2,1)}), bf16[16,128,256]{2,1,0:T(8,128)(2,1)S(1)}, u32[]{:S(2)}, u32[]{:S(2)}) async-start(bf16[16,128,256]{2,1,0:T(8,128)(2,1)} %bitcast.9), calls=%async_computation.3 | async-start | bytes 2097152 | tf_op jit(solution)/shard_map/all_to_all | solution.py:751
  183.8 22.9 %all-to-all-done.3 = bf16[16,128,256]{2,1,0:T(8,128)(2,1)S(1)} async-done(((bf16[16,128,256]{2,1,0:T(8,128)(2,1)}), bf16[16,128,256]{2,1,0:T(8,128)(2,1)S(1)}, u32[]{:S(2)}, u32[]{:S(2)}) %all-to-all-start.3) | async-done | bytes 1048608 | tf_op jit(solution)/shard_map/all_to_all | solution.py:751
  206.7 0.0 copy-start.3
  206.7 0.7 slice_reduce_fusion
  207.5 0.3 copy-done.3
  208.4 0.1 broadcast_in_dim.113
  208.5 0.2 while.10
  208.7 10.1 %shard_map.153 = (bf16[1024,512]{1,0:T(8,128)(2,1)}, bf16[16,112,256]{2,1,0:T(8,128)(2,1)}) custom-call(bf16[2048,256]{1,0:T(8,128)(2,1)} %bitcast.33, f32[1024,256]{1,0:T(8,128)S(1)} %get-tuple-element.82.more_ref, f32[1024,128]{1,0:T(8,128)} %broadcast_in_dim.112.length_ref, bf16[256,512]{1,0:T(8,128)(2,1)} %w_ref.3, f32[1,512]{1,0:T(1,128)} %bitcast.39, ...), custom_call_target="tpu_custom_call" | custom-call | flops 805306368 | bytes 4194304 | tf_op jit(solution)/shard_map/pallas_call | solution.py:648
  218.8 0.0 copy-start.2
  218.8 29.4 %all_to_all.31.grad_ref.arrived_ref = bf16[16,112,256]{2,1,0:T(8,128)(2,1)S(1)} all-to-all(bf16[16,112,256]{2,1,0:T(8,128)(2,1)} %get-tuple-element.86), channel_id=1, replica_groups=mesh['grp'=2,'pts'=16] {'pts'}, dimensions={0} | all-to-all | bytes 1835008 | tf_op jit(solution)/shard_map/all_to_all | solution.py:751
  248.2 0.8 shard_map.155
  249.0 4.5 %all-to-all-start.5 = ((bf16[16,32,256]{2,1,0:T(8,128)(2,1)}), bf16[16,32,256]{2,1,0:T(8,128)(2,1)S(1)}, u32[]{:S(2)}, u32[]{:S(2)}) async-start(bf16[16,32,256]{2,1,0:T(8,128)(2,1)} %get-tuple-element.87), calls=%async_computation.5 | async-start | bytes 524288 | tf_op jit(solution)/shard_map/all_to_all | solution.py:751
  253.4 0.0 copy-done.2
  253.4 5.4 %shard_map.154 = bf16[4096,256]{1,0:T(8,128)(2,1)} custom-call(s32[8,1024]{1,0:T(8,128)S(1)} %copy-done.2, bf16[16,112,256]{2,1,0:T(8,128)(2,1)S(1)} %all_to_all.31.grad_ref.arrived_ref), custom_call_target="tpu_custom_call" | custom-call | flops 2147483648 | bytes 4194304 | tf_op jit(solution)/shard_map/pallas_call | solution.py:701
  258.9 4.6 %all-to-all-done.5 = bf16[16,32,256]{2,1,0:T(8,128)(2,1)S(1)} async-done(((bf16[16,32,256]{2,1,0:T(8,128)(2,1)}), bf16[16,32,256]{2,1,0:T(8,128)(2,1)S(1)}, u32[]{:S(2)}, u32[]{:S(2)}) %all-to-all-start.5) | async-done | bytes 262176 | tf_op jit(solution)/shard_map/all_to_all | solution.py:751
  263.5 0.9 bitcast_convert_fusion
  (15 shorter events, 0.2 us)
Async XLA Ops:
  2.7 15.3 %all-to-all-start.1 = ((s32[16,16,128]{2,1,0:T(8,128)}), s32[16,16,128]{2,1,0:T(8,128)S(1)}, u32[]{:S(2)}, u32[]{:S(2)}) async-start(s32[16,16,128]{2,1,0:T(8,128)} %get-tuple-element.66), calls=%async_computation.1 | async-start | bytes 262144 | tf_op jit(solution)/shard_map/all_to_all | solution.py:751
  18.0 3.9 %copy-start.4 = (s32[4,1024]{1,0:T(4,128)S(1)}, s32[4,1024]{1,0:T(4,128)}, u32[]{:S(2)}) copy-start(s32[4,1024]{1,0:T(4,128)} %param.17) | copy-start | bytes 49156
  18.0 44.9 %all-to-all-start.2 = ((bf16[16,256,256]{2,1,0:T(8,128)(2,1)}), bf16[16,256,256]{2,1,0:T(8,128)(2,1)S(1)}, u32[]{:S(2)}, u32[]{:S(2)}) async-start(bf16[16,256,256]{2,1,0:T(8,128)(2,1)} %bitcast.32), calls=%async_computation.2 | async-start | bytes 4194304 | tf_op jit(solution)/shard_map/all_to_all | solution.py:751
  21.8 41.0 %copy-start = (bf16[256,768]{1,0:T(8,128)(2,1)S(1)}, bf16[256,768]{1,0:T(8,128)(2,1)}, u32[]{:S(2)}) copy-start(bf16[256,768]{1,0:T(8,128)(2,1)} %w_ref.2) | copy-start | bytes 1179652
  21.9 41.0 %copy-start.1 = (bf16[256,256]{1,0:T(8,128)(2,1)S(1)}, bf16[256,256]{1,0:T(8,128)(2,1)}, u32[]{:S(2)}) copy-start(bf16[256,256]{1,0:T(8,128)(2,1)} %wo_ref.1) | copy-start | bytes 393220
  172.6 34.1 %all-to-all-start.3 = ((bf16[16,128,256]{2,1,0:T(8,128)(2,1)}), bf16[16,128,256]{2,1,0:T(8,128)(2,1)S(1)}, u32[]{:S(2)}, u32[]{:S(2)}) async-start(bf16[16,128,256]{2,1,0:T(8,128)(2,1)} %bitcast.9), calls=%async_computation.3 | async-start | bytes 2097152 | tf_op jit(solution)/shard_map/all_to_all | solution.py:751
  206.7 1.0 copy-start.3
  218.8 34.7 %copy-start.2 = (s32[8,1024]{1,0:T(8,128)S(1)}, s32[8,1024]{1,0:T(8,128)}, u32[]{:S(2)}) copy-start(s32[8,1024]{1,0:T(8,128)} %get-tuple-element.85.span_ref) | copy-start | bytes 98308
  249.0 14.5 %all-to-all-start.5 = ((bf16[16,32,256]{2,1,0:T(8,128)(2,1)}), bf16[16,32,256]{2,1,0:T(8,128)(2,1)S(1)}, u32[]{:S(2)}, u32[]{:S(2)}) async-start(bf16[16,32,256]{2,1,0:T(8,128)(2,1)} %get-tuple-element.87), calls=%async_computation.5 | async-start | bytes 524288 | tf_op jit(solution)/shard_map/all_to_all | solution.py:751

commit v6 on v5

--- a/solution.py
+++ b/solution.py
@@ -11,12 +11,11 @@
 HDIM = 16
 HEAD_GROUP = 8
 ROWS = 128
-SEAT = 128
-SEATS = 112
+SEAT = 112
+TURN = 16 * SEAT
 INFO = 16
 ALIGN = 16
 CHUNK = 512
-FIELDS = 6
 WINDOW = 256
 PATCHES = 4
 FAR = 2.0**100
@@ -138,10 +137,8 @@
     table_ref,
     local_ref,
     base_ref,
-    most_ref,
     owner,
     place,
-    origin,
     seats,
 ):
     blocks = owner.shape[0]
@@ -162,7 +159,6 @@
         found = mm(fields, jnp.where(inside, 1.0, 0.0).astype(BF), NT)
         owner[pl.ds(v, 1), :] = found[0:1]
         place[pl.ds(v, 1), :] = found[1:2]
-        origin[pl.ds(v, 1), :] = jnp.full((1, ROWS), source, jnp.int32).astype(F32)
         return 0
 
     lax.fori_loop(0, blocks, one, 0)
@@ -175,17 +171,13 @@
     before = jnp.where(iota((blocks, blocks), 1) < iota((blocks, blocks), 0), 1.0, 0.0).astype(BF)
     local_ref[...] = (mm(opened.astype(BF), upper) - 1.0).astype(jnp.int32)
 
-    def count(e, carry):
-        seat, most = carry
+    def count(e, seat):
         here = own == e.astype(F32)
         marks = jnp.where(here, opened, 0.0).astype(BF)
         total = mm(marks, upper) + mm(before, mm(marks, every).astype(BF))
-        return jnp.where(here, total - 1.0, seat), jnp.maximum(most, total)
-
-    zero = jnp.zeros((blocks, ROWS), F32)
-    seat, most = lax.fori_loop(0, devices, count, (zero, zero))
-    seats[...] = seat
-    most_ref[...] = jnp.full((8, 128), jnp.max(most), F32)
+        return jnp.where(here, total - 1.0, seat)
+
+    seats[...] = lax.fori_loop(0, devices, count, jnp.zeros((blocks, ROWS), F32))
     table_ref[...] = jnp.zeros_like(table_ref)
     field = iota((ROWS, ROWS), 0)
 
@@ -196,7 +188,7 @@
         local = local_ref[at, :]
         seat = seats[at, :]
         coarse = jnp.floor(seat * (1.0 / 64.0))
-        lines = (owner[at, :], coarse, seat - 64.0 * coarse, origin[at, :], place[at, :])
+        lines = (owner[at, :], coarse, seat - 64.0 * coarse)
         values = jnp.ones((ROWS, ROWS), F32)
         for i, line in enumerate(lines):
             values = jnp.where(field == i, line, values)
@@ -218,62 +210,41 @@
             jax.ShapeDtypeStruct((rows + CHUNK, 128), BF),
             jax.ShapeDtypeStruct((blocks, ROWS), jnp.int32),
             jax.ShapeDtypeStruct((blocks + 1,), jnp.int32),
-            jax.ShapeDtypeStruct((8, 128), F32),
         ),
         in_specs=[SMEM, SMEM, VMEM],
-        out_specs=(VMEM, VMEM, SMEM, VMEM),
-        scratch_shapes=[pltpu.VMEM((blocks, ROWS), F32)] * 4,
+        out_specs=(VMEM, VMEM, SMEM),
+        scratch_shapes=[pltpu.VMEM((blocks, ROWS), F32)] * 3,
         compiler_params=ROOM,
         cost_estimate=cost(40 * rows * 1024, 8 * rows),
     )(source, block, info)
 
 
-def plan_kernel(round_ref, base_ref, most_ref, table_ref, code_ref, tags_ref, found):
-    first = (SEATS * round_ref[0]).astype(F32)
+def plan_kernel(round_ref, base_ref, table_ref, code_ref):
+    first = (SEAT * round_ref[0]).astype(F32)
     chunks = (base_ref[base_ref.shape[0] - 1] + CHUNK - 1) // CHUNK
-    total = tags_ref.shape[1]
     pick = jnp.where(iota((16, 128), 0) == iota((16, 128), 1), 1.0, 0.0).astype(BF)
-    base = pl.program_id(0) * total
-    found[...] = jnp.zeros_like(found)
 
     def step(c, _):
         at = pl.ds(pl.multiple_of(c * CHUNK, CHUNK), CHUNK)
         lines = mm(pick, table_ref[at, :], NT)
         seat = 64.0 * lines[1:2] + lines[2:3] - first
-        seated = (lines[5:6] > 0.5) & (seat >= 0.0) & (seat < float(SEATS))
+        seated = (lines[3:4] > 0.5) & (seat >= 0.0) & (seat < float(SEAT))
         code = jnp.where(seated, lines[0:1] * float(SEAT) + seat, -1.0).astype(jnp.int32)
         code_ref[:, at] = jnp.broadcast_to(code, (8, CHUNK))
-        member = jnp.where(iota((total, 1), 0) + base == code, 1.0, 0.0).astype(BF)
-        found[...] += mm(lines.astype(BF), member, NT)
         return 0
 
     lax.fori_loop(0, chunks, step, 0)
-    rounds = jnp.floor((jnp.max(most_ref[...]) + (SEATS - 1.0)) * (1.0 / SEATS) + 1e-3)
-    line = iota((8, total), 0)
-    tags_ref[...] = jnp.where(
-        line == 0, found[3:4, :], jnp.where(line == 1, found[4:5, :], rounds)
-    )
-
-
-def plan_seats(step, base, most, table, devices):
-    total = devices * SEAT
-    part = min(2048, total)
+
+
+def plan_seats(step, base, table):
     return pl.pallas_call(
         plan_kernel,
-        grid=(total // part,),
-        out_shape=(
-            jax.ShapeDtypeStruct((8, table.shape[0]), jnp.int32),
-            jax.ShapeDtypeStruct((8, total), F32),
-        ),
-        in_specs=[SMEM, SMEM, VMEM, VMEM],
-        out_specs=(
-            pl.BlockSpec((8, table.shape[0]), lambda i: (0, 0)),
-            pl.BlockSpec((8, part), lambda i: (0, i)),
-        ),
-        scratch_shapes=[pltpu.VMEM((16, part), F32)],
+        out_shape=jax.ShapeDtypeStruct((8, table.shape[0]), jnp.int32),
+        in_specs=[SMEM, SMEM, VMEM],
+        out_specs=VMEM,
         compiler_params=ROOM,
-        cost_estimate=cost(64 * total * table.shape[0], 4 * table.size),
-    )(step, base, most, table)
+        cost_estimate=cost(64 * table.size, 4 * table.size),
+    )(step, base, table)
 
 
 def rotate_rows(doubled, turn, span):
@@ -453,7 +424,7 @@
     )(index, low, count, base, turn, local, ids, w_qkv, w_out, rows)
 
 
-def route_kernel(base_ref, code_ref, tags_ref, sums_ref, out_ref, acc):
+def route_kernel(base_ref, code_ref, sums_ref, out_ref, acc):
     total = out_ref.shape[0]
     chunks = (base_ref[base_ref.shape[0] - 1] + CHUNK - 1) // CHUNK
     seat = iota((total, 1), 0) + pl.program_id(0) * total
@@ -466,78 +437,64 @@
         return 0
 
     lax.fori_loop(0, chunks, step, 0)
-    line = iota((SEAT - SEATS, SEAT), 0)
-    for d in range(total // SEAT):
-        low = d * SEAT
-        here = slice(low, low + SEAT)
-        out_ref[low : low + SEATS, :] = acc[low : low + SEATS, :].astype(BF)
-        origin = jnp.where(
-            line == 0, tags_ref[0:1, here], jnp.where(line == 1, tags_ref[2:3, here], 0.0)
-        )
-        place = jnp.where(line == 0, tags_ref[1:2, here], 0.0)
-        out_ref[low + SEATS : low + SEAT, :] = jnp.concatenate([origin, place], axis=1).astype(BF)
-
-
-def route_sums(base, code, tags, sums):
+    out_ref[...] = acc[...].astype(BF)
+
+
+def route_sums(base, code, sums, devices):
     count, width = sums.shape
-    total = tags.shape[1]
-    part = min(2048, total)
+    total = devices * SEAT
+    part = min(TURN, total)
     return pl.pallas_call(
         route_kernel,
         grid=(total // part,),
         out_shape=jax.ShapeDtypeStruct((total, width), BF),
-        in_specs=[
-            SMEM,
-            VMEM,
-            pl.BlockSpec((8, part), lambda i: (0, i)),
-            VMEM,
-        ],
+        in_specs=[SMEM, VMEM, VMEM],
         out_specs=pl.BlockSpec((part, width), lambda i: (i, 0)),
         scratch_shapes=[pltpu.VMEM((part, width), F32)],
         compiler_params=ROOM,
         cost_estimate=cost(total * count * width, 4 * count * width),
-    )(base, code, tags, sums)
-
-
-def seat_targets(per_owner, pieces_ref, target):
-    valid = iota((1, SEAT), 1) < SEATS
-    for h in range(pieces_ref.shape[0] // SEAT):
-        tag = pieces_ref[h * SEAT + SEATS : (h + 1) * SEAT, :].astype(F32)[0:1]
-        where = tag[:, :SEAT] * float(per_owner) + tag[:, SEAT:]
-        target[0:1, h * SEAT : (h + 1) * SEAT] = jnp.where(valid, where, -1.0).astype(jnp.int32)
-
-
-def fold_kernel(per_owner, pieces_ref, before_ref, out_ref, target):
-    step = pl.program_id(0)
-    parents = out_ref.shape[0]
-    chunk = pieces_ref.shape[0]
-
-    @pl.when(step == 0)
-    def _():
-        out_ref[...] = before_ref[...]
-
-    seat_targets(per_owner, pieces_ref, target)
-    member = jnp.where(iota((parents, 1), 0) == target[0:1, :], 1.0, 0.0).astype(BF)
-    out_ref[...] += mm(member, pieces_ref[...])
-
-
-def fold_pieces(pieces, before, per_owner):
+    )(base, code, sums)
+
+
+def fold_rows(step, pieces_ref, about):
+    total = 0.0
+    part = min(TURN, pieces_ref.shape[0])
+    first = step * SEAT
+    seats = []
+    for i in (1, 3):
+        seat = about[:, i + 1 : i + 2].astype(jnp.int32) - first
+        seated = (seat >= 0) & (seat < SEAT)
+        seats.append(jnp.where(seated, about[:, i : i + 1].astype(jnp.int32) * SEAT + seat, -1))
+    for low in range(0, pieces_ref.shape[0], part):
+        column = iota((1, part), 1) + low
+        member = (column == seats[0]) | (column == seats[1])
+        member = jnp.where(member, 1.0, 0.0).astype(BF)
+        total = total + mm(member, pieces_ref[low : low + part, :])
+    return total
+
+
+def fold_kernel(step_ref, pieces_ref, about_ref, before_ref, out_ref):
+    out_ref[...] = before_ref[...] + fold_rows(step_ref[0], pieces_ref, about_ref[...])
+
+
+def fold_pieces(step, pieces, about, before):
     parents, width = before.shape
-    chunk = min(2048, pieces.shape[0])
-    fixed = lambda i: (0, 0)
-    return pl.pallas_call(
-        functools.partial(fold_kernel, per_owner),
-        grid=(pieces.shape[0] // chunk,),
+    chunk = 256
+    along = lambda i: (i, 0)
+    return pl.pallas_call(
+        fold_kernel,
+        grid=(parents // chunk,),
         out_shape=jax.ShapeDtypeStruct((parents, width), F32),
         in_specs=[
-            pl.BlockSpec((chunk, width), lambda i: (i, 0)),
-            pl.BlockSpec((parents, width), fixed),
+            SMEM,
+            pl.BlockSpec(pieces.shape, lambda i: (0, 0)),
+            pl.BlockSpec((chunk, 128), along),
+            pl.BlockSpec((chunk, width), along),
         ],
-        out_specs=pl.BlockSpec((parents, width), fixed),
-        scratch_shapes=[pltpu.VMEM((8, chunk), jnp.int32)],
+        out_specs=pl.BlockSpec((chunk, width), along),
         compiler_params=ROOM,
         cost_estimate=cost(2 * parents * pieces.size, 4 * pieces.size),
-    )(pieces, before)
+    )(step, pieces, about, before)
 
 
 def whole_tiles(rows):
@@ -555,7 +512,7 @@
     per_owner,
     pieces_ref,
     more_ref,
-    length_ref,
+    about_ref,
     w_ref,
     gain_ref,
     shift_ref,
@@ -564,7 +521,6 @@
     sent_ref,
     acc,
     sums,
-    target,
 ):
     step = pl.program_id(0)
 
@@ -572,16 +528,11 @@
     def _():
         acc[...] = jnp.zeros_like(acc)
         sums[...] = jnp.zeros_like(sums)
-        seat_targets(per_owner, pieces_ref, target)
 
     chunk, width = more_ref.shape
-    total = more_ref[...]
-    parent = iota((chunk, 1), 0) + step * chunk
-    part = min(2048, pieces_ref.shape[0])
-    for low in range(0, pieces_ref.shape[0], part):
-        member = jnp.where(parent == target[0:1, low : low + part], 1.0, 0.0).astype(BF)
-        total = total + mm(member, pieces_ref[low : low + part, :])
-    lengths = jnp.concatenate([length_ref[...]] * (width // 128), axis=1)
+    about = about_ref[...]
+    total = more_ref[...] + fold_rows(0, pieces_ref, about)
+    lengths = about[:, 0:1]
     parent_in = (total / lengths).astype(BF)
     w_pool = w_ref[...]
     gain = gain_ref[...]
@@ -636,10 +587,10 @@
             sent_ref[d, low:, :] = norm
 
 
-def pool(pieces, more, length, w_pool, gain, shift, cotangent):
+def pool(pieces, more, about, w_pool, gain, shift, cotangent):
     parents, width = more.shape
     wide = w_pool.shape[1]
-    chunk = 256
+    chunk = 512
     devices = pieces.shape[0] // SEAT
     tall = whole_tiles(parents // devices) + wide // width * whole_tiles(width // devices)
     tall += whole_tiles(4 * wide // width)
@@ -668,11 +619,10 @@
         scratch_shapes=[
             pltpu.VMEM((width, wide), F32),
             pltpu.VMEM((8, wide), F32),
-            pltpu.VMEM((8, pieces.shape[0]), jnp.int32),
         ],
         compiler_params=FULL,
         cost_estimate=cost(6 * parents * width * wide, 8 * parents * wide, 2 * parents * wide),
-    )(pieces, more, length, w_pool, gain, shift, cotangent)
+    )(pieces, more, about, w_pool, gain, shift, cotangent)
 
 
 def spread_kernel(span_ref, grad_ref, out_ref, share):
@@ -745,6 +695,50 @@
         compiler_params=ROOM,
         cost_estimate=cost(arrived.size, 2 * arrived.size),
     )(arrived)
+
+
+def piece_seats(info, codes, blocks, per_owner):
+    devices = codes.shape[0]
+    parents = devices * per_owner
+    me = lax.axis_index("pts")
+    packed = info.reshape(devices, parents)
+    span = blocks * ROWS
+    lane = jnp.arange(blocks)
+
+    def at_block(block):
+        found = jnp.where(block[:, :, None] == lane, codes[:, None, :], 0)
+        return jnp.sum(found, axis=2)
+
+    first = packed // 16
+    end = first + packed % 16 - 1
+    near = at_block(first // ROWS)
+    far = at_block(end // ROWS)
+    split = first // ROWS != end // ROWS
+    holders = jnp.arange(devices)
+    by_owner = lambda value: value.reshape(devices, devices, per_owner, 1)
+    filled = (by_owner(near // blocks) == holders).astype(jnp.int32)
+    filled += (by_owner(jnp.where(split, far // blocks, -1)) == holders).astype(jnp.int32)
+    rounds = (jnp.max(jnp.sum(filled, axis=(0, 2))) + SEAT - 1) // SEAT
+
+    mine = lambda value: lax.dynamic_slice_in_dim(value, me * per_owner, per_owner, axis=1)
+    near, far, split, first, packed = map(mine, (near, far, split, first, packed))
+    near_key = near * ROWS + first % ROWS
+    far_key = jnp.where(split, far * ROWS, devices * span)
+    near_key, far_key = near_key.reshape(parents, 1), far_key.reshape(parents, 1)
+    every = jnp.concatenate([near_key, far_key], axis=0).reshape(1, 2 * parents)
+
+    def place(key):
+        holder = key // span
+        rank = jnp.sum((every < key) & (every >= holder * span), axis=1, keepdims=True)
+        return holder, jnp.where(holder < devices, rank, -1)
+
+    length = (packed % 16).reshape(parents, 1)
+    columns = (length,) + place(near_key) + place(far_key)
+    wide = iota((parents, 128), 1)
+    about = jnp.zeros((parents, 128), jnp.int32)
+    for i, column in enumerate(columns):
+        about = jnp.where(wide == i, column, about)
+    return about.astype(F32), rounds.astype(jnp.int32)
 
 
 def swap(parts):
@@ -816,43 +810,40 @@
 
     me = lax.axis_index("pts")
     info, span = order_tables(child_counts, parent_order, hil_dest, hil_slot, devices)
+    info, patch_ids = lax.optimization_barrier((info, patch_ids))
     info = swap(info)
     payload = pack_blocks(hil_dest, points, devices, capacity)
     received = exchange(payload, devices)
     index, block = received_index(info[:, parents // 128, :blocks], blocks, capacity)
     source = index // capacity
-    table, local_run, base, most = seat_rows(
+    table, local_run, base = seat_rows(
         source, block, info.reshape(devices * INFO, 128), per_owner
     )
-    code, tags = plan_seats(jnp.zeros((1,), jnp.int32), base, most, table, devices)
+    code = plan_seats(jnp.zeros((1,), jnp.int32), base, table)
     low, count, turn, turned = key_windows(patch_ids)
-    lengths = lax.dynamic_slice_in_dim(
-        info[:, : parents // 128].reshape(devices, parents), me * per_owner, per_owner, axis=1
-    )
-    lengths = lengths.reshape(parents, 1) % 16
-    lengths = jnp.broadcast_to(lengths.astype(F32), (parents, 128))
-    more = jnp.zeros((parents, width), F32)
-    index, low, count, turn, turned, base, local_run, code, tags, lengths = (
+    codes = info[:, parents // 128, :blocks]
+    about, rounds = piece_seats(info[:, : parents // 128], codes, blocks, per_owner)
+    more = jnp.broadcast_to(about[:, 127:], (parents, width))
+    index, low, count, turn, turned, base, local_run, code, about, rounds, more = (
         lax.optimization_barrier(
-            (index, low, count, turn, turned, base, local_run, code, tags, lengths)
+            (index, low, count, turn, turned, base, local_run, code, about, rounds, more)
         )
     )
     local_run = local_run.reshape(patch_ids.shape)
     sums = attend(index, low, count, base, turn, local_run, turned, w_qkv, w_out, received)
-    pieces = exchange(route_sums(base, code, tags, sums), devices)
-    rounds = jnp.max(pieces.reshape(devices, SEAT, width)[:, SEATS + 1, 0].astype(F32))
-
-    def turn(carry):
+    pieces = exchange(route_sums(base, code, sums, devices), devices)
+
+    def turn_again(carry):
         step, before = carry
-        code, tags = plan_seats(step.reshape(1), base, most, table, devices)
-        late = exchange(route_sums(base, code, tags, sums), devices)
-        return step + 1, fold_pieces(late, before, per_owner)
+        step = step.reshape(1)
+        late = exchange(route_sums(base, plan_seats(step, base, table), sums, devices), devices)
+        return step[0] + 1, fold_pieces(step, late, about, before)
 
     _, more = lax.while_loop(
-        lambda carry: carry[0] < rounds.astype(jnp.int32), turn, (jnp.int32(1), more)
+        lambda carry: carry[0] < rounds, turn_again, (jnp.int32(1), more)
     )
     pooled, outgoing = pool(
-        pieces, more, lengths, w_pool, norm_gain[None], norm_shift[None], cotangent
+        pieces, more, about, w_pool, norm_gain[None], norm_shift[None], cotangent
     )
     arrived = swap(outgoing)
     each = width // devices

time: 265 us -> 259 us (0.977)
  blocking collectives: 29.4 us -> 61 us
  waiting for transfers between devices: 45.1 us -> 16.8 us
  starting transfers between devices: 26.9 us -> 15.6 us
  other arithmetic: 3.38 us -> 10.6 us
  Pallas kernels: 156 us -> 150 us
    all_to_all x1 -> x2, blocking collectives: 29.4 us -> 61 us  [swap(): return lax.all_to_all(parts, 'pts', split_axis=0, concat_axis=0, tiled=True)]
    all_to_all x4 -> x3, waiting for transfers between devices: 45.1 us -> 16.8 us  [swap(): return lax.all_to_all(parts, 'pts', split_axis=0, concat_axis=0, tiled=True)]
    all_to_all x4 -> x3, starting transfers between devices: 26.9 us -> 15.6 us  [swap(): return lax.all_to_all(parts, 'pts', split_axis=0, concat_axis=0, tiled=True)]
    reduce_sum x0 -> x3, other arithmetic: none -> 5.07 us  [the longest x1 3.32 us: place(): jnp.sum((every < key) & (every >= holder * span), axis=1, keepdims=True)]
  transfers between devices with their start and end apart: 4 -> 3, of which waited for: 4 -> 3; matrix products, arithmetic and copies ran while one was open for 1% -> 4% of each run, Pallas kernels for 13% -> 12%
where the time goes in v6:
time: 259 us; the launch traced here: 258 us
  Pallas kernels  150 us (58%)
  blocking collectives  61 us (24%)
  waiting for transfers between devices  16.8 us (6%)
  starting transfers between devices  15.6 us (6%)
  other arithmetic  10.6 us (4%)
    pallas_call x1, Pallas kernels, attend(): pl.pallas_call(attend_kernel, out_shape=jax.ShapeDtypeStruct((tiles * spa...  104 us
    all_to_all x2, blocking collectives, swap(): return lax.all_to_all(parts, 'pts', split_axis=0, concat_axis=0, tiled=True)  61 us
    pallas_call x1, Pallas kernels, seat_rows(): pl.pallas_call(functools.partial(seat_kernel, per_owner), out_shape=(jax....  20.2 us
    all_to_all x3, waiting for transfers between devices, swap(): return lax.all_to_all(parts, 'pts', split_axis=0, concat_axis=0, tiled=True)  16.8 us
    all_to_all x3, starting transfers between devices, swap(): return lax.all_to_all(parts, 'pts', split_axis=0, concat_axis=0, tiled=True)  15.6 us
    pallas_call x1, Pallas kernels, pool(): pl.pallas_call(functools.partial(pool_kernel, parents * SEAT // pieces.sh...  9.37 us
    pallas_call x1, Pallas kernels, spread_grads(): pl.pallas_call(spread_kernel, grid=(rows // chunk,), out_shape=jax.ShapeD...  5.41 us
  transfers between devices with their start and end apart: 3, of which 3 were waited for; matrix products, arithmetic and copies ran while one was open for 4% of the time, Pallas kernels for 12%

profile of v6, /device:TPU:0, one launch (start us, length us, event | category | flops | bytes accessed | tf_op | source)
XLA Modules:
  0.0 258.3 jit_solution(4079146908535299219)
XLA Ops:
  0.7 2.0 shard_map.147
  2.7 0.9 convert_reduce_fusion.3
  3.6 0.1 select_reduce_fusion.6
  3.8 0.1 reduce_max.18
  3.9 0.2 select_reduce_fusion.7.turn_ref
  4.1 0.1 fusion.37
  4.1 0.1 select_reduce_fusion.3.ids_ref
  4.3 0.1 select_reduce_fusion.4
  4.4 7.4 %all-to-all-start.1 = ((s32[16,16,128]{2,1,0:T(8,128)}), s32[16,16,128]{2,1,0:T(8,128)S(1)}, u32[]{:S(2)}, u32[]{:S(2)}) async-start(s32[16,16,128]{2,1,0:T(8,128)} %get-tuple-element.65), calls=%async_computation.1 | async-start | bytes 262144 | tf_op jit(solution)/shard_map/all_to_all | solution.py:745
  11.8 0.1 reduce_sum.121
  11.9 0.1 reduce_sum.123
  12.0 3.7 %shard_map.150 = bf16[4096,256]{1,0:T(8,128)(2,1)} custom-call(s32[32]{0:T(128)} %dest_ref.1, bf16[4096,256]{1,0:T(8,128)(2,1)} %points_ref.1), custom_call_target="tpu_custom_call" | custom-call | bytes 4194304 | tf_op jit(solution)/shard_map/pallas_call | solution.py:121
  15.7 4.0 %all-to-all-done.1 = s32[16,16,128]{2,1,0:T(8,128)S(1)} async-done(((s32[16,16,128]{2,1,0:T(8,128)}), s32[16,16,128]{2,1,0:T(8,128)S(1)}, u32[]{:S(2)}, u32[]{:S(2)}) %all-to-all-start.1) | async-done | bytes 131104 | tf_op jit(solution)/shard_map/all_to_all | solution.py:745
  19.7 0.1 add_select_fusion.9
  19.9 3.7 %all-to-all-start.2 = ((bf16[16,256,256]{2,1,0:T(8,128)(2,1)}), bf16[16,256,256]{2,1,0:T(8,128)(2,1)S(1)}, u32[]{:S(2)}, u32[]{:S(2)}) async-start(bf16[16,256,256]{2,1,0:T(8,128)(2,1)} %bitcast.42), calls=%async_computation.2 | async-start | bytes 4194304 | tf_op jit(solution)/shard_map/all_to_all | solution.py:745
  23.6 1.0 select_reduce_fusion.1
  24.7 0.1 multiply_select_fusion
  24.8 0.1 reshape.634
  24.9 0.1 add_select_fusion.10
  25.0 0.1 reshape.633
  25.2 0.1 reduce_sum.129
  25.2 0.1 reduce_sum.130
  25.3 0.1 reshape.636
  25.4 0.4 add_select_fusion.5
  25.8 0.7 add_reduce_fusion
  26.6 0.6 reduce_max.19
  27.9 0.1 broadcast_in_dim.181
  28.0 0.3 convert_reduce_fusion.2
  28.4 0.1 add_select_fusion.12
  28.5 0.3 select_reduce_fusion.2
  28.8 20.2 %shard_map.148 = (bf16[4608,128]{1,0:T(8,128)(2,1)}, s32[32,128]{1,0:T(8,128)S(1)}, s32[33]{0:T(128)S(1)}) custom-call(s32[32]{0:T(128)S(1)} %get-tuple-element.107.source_ref, s32[32]{0:T(128)S(1)} %get-tuple-element.122.block_ref, s32[256,128]{1,0:T(8,128)S(1)} %bitcast.41), custom_call_target="tpu_custom_call" | custom-call | flops 167772160 | bytes 32768 | tf_op jit(solution)/shard_map/pallas_call | solution.py:207
  49.0 1.8 shard_map.149.code_ref
  50.9 3.3 %convert_reduce_fusion.1 = (s32[1024]{0:T(1024)S(1)}, s32[1024]{0:T(1024)S(1)}) fusion(s32[2048]{0:T(1024)S(1)} %bitcast.51, s32[1024]{0:T(1024)S(1)} %broadcast_multiply_fusion.1, s32[1024]{0:T(1024)S(1)} %reshape.632, s32[1024]{0:T(1024)S(1)} %broadcast_multiply_fusion, s32[1024]{0:T(1024)S(1)} %reshape.635), kind=kLoop, calls=%fused_computation.1 | loop fusion | flops 20969472 | bytes 32768 | tf_op jit(solution)/shard_map/reduce_sum | solution.py:732
  54.2 0.7 select_convert_fusion.about_ref
  55.0 0.4 slice_reduce_fusion
  55.4 1.2 broadcast_in_dim.184
  56.5 8.1 %all-to-all-done.2 = bf16[16,256,256]{2,1,0:T(8,128)(2,1)S(1)} async-done(((bf16[16,256,256]{2,1,0:T(8,128)(2,1)}), bf16[16,256,256]{2,1,0:T(8,128)(2,1)S(1)}, u32[]{:S(2)}, u32[]{:S(2)}) %all-to-all-start.2) | async-done | bytes 2097184 | tf_op jit(solution)/shard_map/all_to_all | solution.py:745
  64.7 104.2 %shard_map.151.sums_ref = bf16[4608,256]{1,0:T(8,128)(2,1)S(1)} custom-call(s32[32]{0:T(128)S(1)} %get-tuple-element.72.index_ref, s32[32]{0:T(128)S(1)} %get-tuple-element.73.low_ref, s32[32]{0:T(128)S(1)} %get-tuple-element.74.count_ref, s32[33]{0:T(128)S(1)} %get-tuple-element.182.base_ref, s32[4]{0:T(128)S(1)} %select_reduce_fusion.7.turn_ref, ...), custom_call_target="tpu_custom_call" | custom-call | flops 34359738368 | bytes 4194304 | tf_op jit(solution)/shard_map/pallas_call | solution.py:406
  168.9 2.7 %shard_map.152 = bf16[1792,256]{1,0:T(8,128)(2,1)S(1)} custom-call(s32[33]{0:T(128)S(1)} %get-tuple-element.182.base_ref, s32[8,4608]{1,0:T(8,128)S(1)} %shard_map.149.code_ref, bf16[4608,256]{1,0:T(8,128)(2,1)S(1)} %shard_map.151.sums_ref), custom_call_target="tpu_custom_call" | custom-call | flops 2113929216 | bytes 4718592 | tf_op jit(solution)/shard_map/pallas_call | solution.py:447
  171.5 0.2 while.10
  171.8 33.8 %all_to_all.31 = bf16[16,112,256]{2,1,0:T(8,128)(2,1)} all-to-all(bf16[16,112,256]{2,1,0:T(8,128)(2,1)S(1)} %bitcast.40), channel_id=1, replica_groups=mesh['grp'=2,'pts'=16] {'pts'}, dimensions={0} | all-to-all | bytes 1835008 | tf_op jit(solution)/shard_map/all_to_all | solution.py:745
  205.6 9.4 %shard_map.153 = (bf16[1024,512]{1,0:T(8,128)(2,1)}, bf16[16,112,256]{2,1,0:T(8,128)(2,1)}) custom-call(bf16[1792,256]{1,0:T(8,128)(2,1)} %bitcast.43, f32[1024,256]{1,0:T(8,128)S(1)} %copy-done.3, f32[1024,128]{1,0:T(8,128)S(1)} %get-tuple-element.206, bf16[256,512]{1,0:T(8,128)(2,1)} %w_ref.3, f32[1,512]{1,0:T(1,128)} %bitcast.52, f32[1,512]{1,0:T(1,128)} %bitcast.53, ...), custom_call_target="tpu_custom_call" | custom-call | flops 805306368 | bytes 4194304 | tf_op jit(solution)/shard_map/pallas_call | solution.py:599
  215.0 27.2 %all_to_all.32.grad_ref.arrived_ref = bf16[16,112,256]{2,1,0:T(8,128)(2,1)S(1)} all-to-all(bf16[16,112,256]{2,1,0:T(8,128)(2,1)} %get-tuple-element.84), channel_id=1, replica_groups=mesh['grp'=2,'pts'=16] {'pts'}, dimensions={0} | all-to-all | bytes 1835008 | tf_op jit(solution)/shard_map/all_to_all | solution.py:745
  242.1 0.8 shard_map.155
  242.9 4.5 %all-to-all-start.5 = ((bf16[16,32,256]{2,1,0:T(8,128)(2,1)}), bf16[16,32,256]{2,1,0:T(8,128)(2,1)S(1)}, u32[]{:S(2)}, u32[]{:S(2)}) async-start(bf16[16,32,256]{2,1,0:T(8,128)(2,1)} %get-tuple-element.85), calls=%async_computation.5 | async-start | bytes 524288 | tf_op jit(solution)/shard_map/all_to_all | solution.py:745
  247.4 5.4 %shard_map.154 = bf16[4096,256]{1,0:T(8,128)(2,1)} custom-call(s32[8,1024]{1,0:T(8,128)S(1)} %copy-done.2, bf16[16,112,256]{2,1,0:T(8,128)(2,1)S(1)} %all_to_all.32.grad_ref.arrived_ref), custom_call_target="tpu_custom_call" | custom-call | flops 2147483648 | bytes 4194304 | tf_op jit(solution)/shard_map/pallas_call | solution.py:651
  252.8 4.6 %all-to-all-done.5 = bf16[16,32,256]{2,1,0:T(8,128)(2,1)S(1)} async-done(((bf16[16,32,256]{2,1,0:T(8,128)(2,1)}), bf16[16,32,256]{2,1,0:T(8,128)(2,1)S(1)}, u32[]{:S(2)}, u32[]{:S(2)}) %all-to-all-start.5) | async-done | bytes 262176 | tf_op jit(solution)/shard_map/all_to_all | solution.py:745
  257.5 0.9 bitcast_convert_fusion
  (35 shorter events, 0.4 us)
Async XLA Ops:
  4.4 15.3 %all-to-all-start.1 = ((s32[16,16,128]{2,1,0:T(8,128)}), s32[16,16,128]{2,1,0:T(8,128)S(1)}, u32[]{:S(2)}, u32[]{:S(2)}) async-start(s32[16,16,128]{2,1,0:T(8,128)} %get-tuple-element.65), calls=%async_computation.1 | async-start | bytes 262144 | tf_op jit(solution)/shard_map/all_to_all | solution.py:745
  19.9 44.8 %all-to-all-start.2 = ((bf16[16,256,256]{2,1,0:T(8,128)(2,1)}), bf16[16,256,256]{2,1,0:T(8,128)(2,1)S(1)}, u32[]{:S(2)}, u32[]{:S(2)}) async-start(bf16[16,256,256]{2,1,0:T(8,128)(2,1)} %bitcast.42), calls=%async_computation.2 | async-start | bytes 4194304 | tf_op jit(solution)/shard_map/all_to_all | solution.py:745
  28.8 35.9 %copy-start = (bf16[256,768]{1,0:T(8,128)(2,1)S(1)}, bf16[256,768]{1,0:T(8,128)(2,1)}, u32[]{:S(2)}) copy-start(bf16[256,768]{1,0:T(8,128)(2,1)} %w_ref.2) | copy-start | bytes 1179652
  28.8 35.9 %copy-start.1 = (bf16[256,256]{1,0:T(8,128)(2,1)S(1)}, bf16[256,256]{1,0:T(8,128)(2,1)}, u32[]{:S(2)}) copy-start(bf16[256,256]{1,0:T(8,128)(2,1)} %wo_ref.1) | copy-start | bytes 393220
  168.8 2.7 %copy-start.4 = (bf16[4608,256]{1,0:T(8,128)(2,1)}, bf16[4608,256]{1,0:T(8,128)(2,1)S(1)}, u32[]{:S(2)}) copy-start(bf16[4608,256]{1,0:T(8,128)(2,1)S(1)} %shard_map.151.sums_ref) | copy-start | bytes 7077892
  171.8 33.8 %copy-start.3 = (f32[1024,256]{1,0:T(8,128)S(1)}, f32[1024,256]{1,0:T(8,128)}, u32[]{:S(2)}) copy-start(f32[1024,256]{1,0:T(8,128)} %get-tuple-element.81.more_ref) | copy-start | bytes 3145732
  215.0 32.4 %copy-start.2 = (s32[8,1024]{1,0:T(8,128)S(1)}, s32[8,1024]{1,0:T(8,128)}, u32[]{:S(2)}) copy-start(s32[8,1024]{1,0:T(8,128)} %get-tuple-element.83.span_ref) | copy-start | bytes 98308
  242.9 14.5 %all-to-all-start.5 = ((bf16[16,32,256]{2,1,0:T(8,128)(2,1)}), bf16[16,32,256]{2,1,0:T(8,128)(2,1)S(1)}, u32[]{:S(2)}, u32[]{:S(2)}) async-start(bf16[16,32,256]{2,1,0:T(8,128)(2,1)} %get-tuple-element.85), calls=%async_computation.5 | async-start | bytes 524288 | tf_op jit(solution)/shard_map/all_to_all | solution.py:745

commit v7 on v6

--- a/solution.py
+++ b/solution.py
@@ -11,9 +11,9 @@
 HDIM = 16
 HEAD_GROUP = 8
 ROWS = 128
-SEAT = 112
+SEAT = 104
 TURN = 16 * SEAT
-INFO = 16
+INFO = 8
 ALIGN = 16
 CHUNK = 512
 WINDOW = 256
@@ -67,7 +67,8 @@
     length = ordered[2:3]
     span_ref[...] = jnp.where(which == 0, first, jnp.where(which == 1, first + length, length))
     both = 16 * first + length
-    lines = parents // 128
+    both = both[:, : parents // 2] | (both[:, parents // 2 :] << 16)
+    lines = parents // 256
     info_ref[0, lines:, :] = jnp.zeros((INFO - lines, 128), jnp.int32)
     info_ref[0, lines : lines + 1, :blocks] = dest_ref[...] * blocks + slot_ref[...]
     for i in range(lines):
@@ -129,21 +130,60 @@
     )(hil_dest, points)
 
 
+def key_windows(ids_ref, low_ref, count_ref, turn_ref, turned_ref):
+    tiles, span = ids_ref.shape
+    lane = iota((1, span), 1)
+    for t in range(tiles):
+        ids = ids_ref[t : t + 1, :]
+        sizes = [
+            jnp.sum(jnp.where(ids == c, 1.0, 0.0)).astype(jnp.int32) for c in range(PATCHES)
+        ]
+        starts = [jnp.int32(0)]
+        for c in range(1, PATCHES):
+            starts.append(starts[-1] + sizes[c - 1])
+        most, turn = sizes[0], starts[0]
+        for c in range(1, PATCHES):
+            turn = jnp.where(sizes[c] > most, starts[c], turn)
+            most = jnp.maximum(most, sizes[c])
+        firsts = [lax.rem(start - turn + span, span) for start in starts]
+        ends = [first + size for first, size in zip(firsts, sizes)]
+        turned = jnp.zeros((1, span), jnp.int32)
+        for c in range(1, PATCHES):
+            turned = jnp.where((lane >= firsts[c]) & (lane < ends[c]), c, turned)
+        turned_ref[t : t + 1, :] = turned
+        turn_ref[t] = turn
+        for b in range(span // ROWS):
+            top, bottom = b * ROWS, (b + 1) * ROWS - 1
+            low, high = jnp.int32(0), jnp.int32(span)
+            for c in range(PATCHES):
+                low = jnp.where((firsts[c] <= top) & (top < ends[c]), firsts[c], low)
+                high = jnp.where((firsts[c] <= bottom) & (bottom < ends[c]), ends[c], high)
+            low = low // ROWS * ROWS
+            count = (high - low + WINDOW - 1) // WINDOW
+            low_ref[t * (span // ROWS) + b] = jnp.minimum(low, span - count * WINDOW)
+            count_ref[t * (span // ROWS) + b] = count
+
+
 def seat_kernel(
     per_owner,
     source_ref,
     block_ref,
     info_ref,
+    ids_ref,
     table_ref,
     local_ref,
     base_ref,
+    low_ref,
+    count_ref,
+    turn_ref,
+    turned_ref,
     owner,
     place,
     seats,
 ):
     blocks = owner.shape[0]
     parents = 128 * 8
-    devices = info_ref.shape[0] // INFO
+    devices = info_ref.shape[0] // 8
     which = iota((16, parents), 0)
     rank = iota((16, parents), 1)
     fields = jnp.where(which == 0, rank // per_owner, jnp.where(which == 1, rank % per_owner, 0))
@@ -151,7 +191,7 @@
 
     def one(v, _):
         source = source_ref[v]
-        packed = info_ref[pl.ds(pl.multiple_of(source * INFO, INFO), 8), :]
+        packed = info_ref[pl.ds(pl.multiple_of(source * 8, 8), 8), :]
         line = jnp.concatenate([packed[i : i + 1] for i in range(8)], axis=1)
         first = line // 16
         row = block_ref[v] * ROWS + iota((ROWS, parents), 0)
@@ -199,9 +239,10 @@
         return base + (jnp.max(local) + ALIGN) // ALIGN * ALIGN
 
     base_ref[blocks] = lax.fori_loop(0, blocks, lay, 0)
-
-
-def seat_rows(source, block, info, per_owner):
+    key_windows(ids_ref, low_ref, count_ref, turn_ref, turned_ref)
+
+
+def seat_rows(source, block, info, ids, per_owner):
     blocks = source.shape[0]
     rows = blocks * ROWS
     return pl.pallas_call(
@@ -210,13 +251,17 @@
             jax.ShapeDtypeStruct((rows + CHUNK, 128), BF),
             jax.ShapeDtypeStruct((blocks, ROWS), jnp.int32),
             jax.ShapeDtypeStruct((blocks + 1,), jnp.int32),
+            jax.ShapeDtypeStruct((blocks,), jnp.int32),
+            jax.ShapeDtypeStruct((blocks,), jnp.int32),
+            jax.ShapeDtypeStruct((ids.shape[0],), jnp.int32),
+            jax.ShapeDtypeStruct(ids.shape, jnp.int32),
         ),
-        in_specs=[SMEM, SMEM, VMEM],
-        out_specs=(VMEM, VMEM, SMEM),
+        in_specs=[SMEM, SMEM, VMEM, VMEM],
+        out_specs=(VMEM, VMEM, SMEM, SMEM, SMEM, SMEM, VMEM),
         scratch_shapes=[pltpu.VMEM((blocks, ROWS), F32)] * 3,
         compiler_params=ROOM,
         cost_estimate=cost(40 * rows * 1024, 8 * rows),
-    )(source, block, info)
+    )(source, block, info, ids)
 
 
 def plan_kernel(round_ref, base_ref, table_ref, code_ref):
@@ -763,29 +808,6 @@
     return both // blocks, both % blocks
 
 
-def key_windows(patch_ids):
-    tiles, span = patch_ids.shape
-    patch = jnp.arange(PATCHES)
-    sizes = jnp.sum(patch_ids[:, None, :] == patch[None, :, None], axis=2)
-    starts = jnp.sum(jnp.where(patch[None, :] < patch[:, None], sizes[:, None, :], 0), axis=2)
-    longest = sizes == jnp.max(sizes, axis=1, keepdims=True)
-    turn = jnp.min(jnp.where(longest, starts, span), axis=1)
-    firsts = (starts - turn[:, None]) % span
-    row = jnp.arange(span)[None, :, None]
-    inside = (row >= firsts[:, None, :]) & (row < (firsts + sizes)[:, None, :])
-    turned = jnp.sum(jnp.where(inside, patch, 0), axis=2)
-    block = jnp.arange(0, span, ROWS)[None, :, None]
-    starts_in = (block >= firsts[:, None, :]) & (block < (firsts + sizes)[:, None, :])
-    ending = block + ROWS - 1
-    ends_in = (ending >= firsts[:, None, :]) & (ending < (firsts + sizes)[:, None, :])
-    low = jnp.sum(jnp.where(starts_in, firsts[:, None, :], 0), axis=2) // ROWS * ROWS
-    high = jnp.sum(jnp.where(ends_in, (firsts + sizes)[:, None, :], 0), axis=2)
-    count = (high - low + WINDOW - 1) // WINDOW
-    low = jnp.minimum(low, span - count * WINDOW)
-    as_int = lambda value: value.astype(jnp.int32)
-    return as_int(low.reshape(-1)), as_int(count.reshape(-1)), as_int(turn), as_int(turned)
-
-
 def local(
     points,
     hil_dest,
@@ -810,19 +832,22 @@
 
     me = lax.axis_index("pts")
     info, span = order_tables(child_counts, parent_order, hil_dest, hil_slot, devices)
-    info, patch_ids = lax.optimization_barrier((info, patch_ids))
     info = swap(info)
     payload = pack_blocks(hil_dest, points, devices, capacity)
     received = exchange(payload, devices)
-    index, block = received_index(info[:, parents // 128, :blocks], blocks, capacity)
+    lines = parents // 256
+    codes = info[:, lines, :blocks]
+    packed = info[:, :lines]
+    info = jnp.concatenate(
+        [packed & 65535, lax.shift_right_logical(packed, jnp.int32(16))], axis=1
+    )
+    index, block = received_index(codes, blocks, capacity)
     source = index // capacity
-    table, local_run, base = seat_rows(
-        source, block, info.reshape(devices * INFO, 128), per_owner
+    table, local_run, base, low, count, turn, turned = seat_rows(
+        source, block, info.reshape(-1, 128), patch_ids, per_owner
     )
     code = plan_seats(jnp.zeros((1,), jnp.int32), base, table)
-    low, count, turn, turned = key_windows(patch_ids)
-    codes = info[:, parents // 128, :blocks]
-    about, rounds = piece_seats(info[:, : parents // 128], codes, blocks, per_owner)
+    about, rounds = piece_seats(info, codes, blocks, per_owner)
     more = jnp.broadcast_to(about[:, 127:], (parents, width))
     index, low, count, turn, turned, base, local_run, code, about, rounds, more = (
         lax.optimization_barrier(

time: 259 us -> 254 us (0.981)
  transfers between devices with their start and end apart: 3 -> 3, of which waited for: 3 -> 3; matrix products, arithmetic and copies ran while one was open for 4% -> 4% of each run, Pallas kernels for 12% -> 13%
where the time goes in v7:
time: 254 us; the launch traced here: 253 us
  Pallas kernels  150 us (59%)
  blocking collectives  59.5 us (23%)
  starting transfers between devices  15.6 us (6%)
  waiting for transfers between devices  14.9 us (6%)
  other arithmetic  8.93 us (4%)
    pallas_call x1, Pallas kernels, attend(): pl.pallas_call(attend_kernel, out_shape=jax.ShapeDtypeStruct((tiles * spa...  103 us
    all_to_all x2, blocking collectives, swap(): return lax.all_to_all(parts, 'pts', split_axis=0, concat_axis=0, tiled=True)  59.5 us
    pallas_call x1, Pallas kernels, seat_rows(): pl.pallas_call(functools.partial(seat_kernel, per_owner), out_shape=(jax....  21.1 us
    all_to_all x3, starting transfers between devices, swap(): return lax.all_to_all(parts, 'pts', split_axis=0, concat_axis=0, tiled=True)  15.6 us
    all_to_all x3, waiting for transfers between devices, swap(): return lax.all_to_all(parts, 'pts', split_axis=0, concat_axis=0, tiled=True)  14.9 us
    pallas_call x1, Pallas kernels, pool(): pl.pallas_call(functools.partial(pool_kernel, parents * SEAT // pieces.sh...  9.42 us
    pallas_call x1, Pallas kernels, spread_grads(): pl.pallas_call(spread_kernel, grid=(rows // chunk,), out_shape=jax.ShapeD...  5.41 us
  transfers between devices with their start and end apart: 3, of which 3 were waited for; matrix products, arithmetic and copies ran while one was open for 4% of the time, Pallas kernels for 13%

profile of v7, /device:TPU:0, one launch (start us, length us, event | category | flops | bytes accessed | tf_op | source)
XLA Modules:
  0.0 253.4 jit_solution(10561748387305286099)
XLA Ops:
  0.7 2.0 shard_map.147
  2.7 7.4 %all-to-all-start.1 = ((s32[16,8,128]{2,1,0:T(8,128)}), s32[16,8,128]{2,1,0:T(8,128)S(1)}, u32[]{:S(2)}, u32[]{:S(2)}) async-start(s32[16,8,128]{2,1,0:T(8,128)} %get-tuple-element.66), calls=%async_computation.1 | async-start | bytes 131072 | tf_op jit(solution)/shard_map/all_to_all | solution.py:790
  10.1 3.7 %shard_map.150 = bf16[4096,256]{1,0:T(8,128)(2,1)} custom-call(s32[32]{0:T(128)} %dest_ref.1, bf16[4096,256]{1,0:T(8,128)(2,1)} %points_ref.1), custom_call_target="tpu_custom_call" | custom-call | bytes 4194304 | tf_op jit(solution)/shard_map/pallas_call | solution.py:122
  13.8 3.2 %all-to-all-done.1 = s32[16,8,128]{2,1,0:T(8,128)S(1)} async-done(((s32[16,8,128]{2,1,0:T(8,128)}), s32[16,8,128]{2,1,0:T(8,128)S(1)}, u32[]{:S(2)}, u32[]{:S(2)}) %all-to-all-start.1) | async-done | bytes 65568 | tf_op jit(solution)/shard_map/all_to_all | solution.py:790
  17.0 0.1 add_select_fusion.9
  17.2 0.0 copy-start.2
  17.2 3.7 %all-to-all-start.2 = ((bf16[16,256,256]{2,1,0:T(8,128)(2,1)}), bf16[16,256,256]{2,1,0:T(8,128)(2,1)S(1)}, u32[]{:S(2)}, u32[]{:S(2)}) async-start(bf16[16,256,256]{2,1,0:T(8,128)(2,1)} %bitcast.42), calls=%async_computation.2 | async-start | bytes 4194304 | tf_op jit(solution)/shard_map/all_to_all | solution.py:790
  20.9 1.0 select_reduce_fusion.1
  22.0 0.1 multiply_select_fusion
  22.0 0.1 reshape.577
  22.1 0.1 reshape.575
  22.2 0.1 add_select_fusion.10
  22.3 0.1 reshape.576
  22.4 0.1 reshape.578
  22.4 0.1 reduce_sum.73
  22.5 0.1 reduce_sum.74
  22.6 0.1 reshape.579
  22.7 0.4 add_select_fusion.5
  23.1 0.7 add_reduce_fusion
  23.8 0.6 reduce_max.9
  25.1 0.1 broadcast_in_dim.115
  25.2 0.1 fusion.27
  25.3 0.3 convert_reduce_fusion.2
  25.7 0.1 add_select_fusion.12
  25.7 0.3 select_reduce_fusion.2
  26.0 0.0 copy-done.2
  26.0 0.0 copy-start
  26.1 0.0 copy-start.1
  26.1 21.1 %shard_map.148 = (bf16[4608,128]{1,0:T(8,128)(2,1)}, s32[32,128]{1,0:T(8,128)S(1)}, s32[33]{0:T(128)S(1)}, s32[32]{0:T(128)S(1)}, s32[32]{0:T(128)S(1)}, /*index=5*/s32[4]{0:T(128)S(1)}, s32[4,1024]{1,0:T(4,128)S(1)}) custom-call(s32[32]{0:T(128)S(1)} %get-tuple-element.109.source_ref, s32[32]{0:T(128)S(1)} %get-tuple-element.124.block_ref, ...), custom_call_target="tpu_custom_call" | custom-call | flops 167772160 | bytes 32768 | tf_op jit(solution)/shard_map/pallas_call | solution.py:248
  47.1 2.0 shard_map.149.code_ref
  49.2 3.3 %convert_reduce_fusion.1 = (s32[1024]{0:T(1024)S(1)}, s32[1024]{0:T(1024)S(1)}) fusion(s32[2048]{0:T(1024)S(1)} %bitcast.51, s32[1024]{0:T(1024)S(1)} %broadcast_multiply_fusion.1, s32[1024]{0:T(1024)S(1)} %reshape.575, s32[1024]{0:T(1024)S(1)} %broadcast_multiply_fusion, s32[1024]{0:T(1024)S(1)} %reshape.578), kind=kLoop, calls=%fused_computation.1 | loop fusion | flops 20969472 | bytes 32768 | tf_op jit(solution)/shard_map/reduce_sum | solution.py:777
  52.5 0.7 select_convert_fusion.about_ref
  53.3 0.4 slice_reduce_fusion
  53.6 1.2 broadcast_in_dim.118
  54.8 7.2 %all-to-all-done.2 = bf16[16,256,256]{2,1,0:T(8,128)(2,1)S(1)} async-done(((bf16[16,256,256]{2,1,0:T(8,128)(2,1)}), bf16[16,256,256]{2,1,0:T(8,128)(2,1)S(1)}, u32[]{:S(2)}, u32[]{:S(2)}) %all-to-all-start.2) | async-done | bytes 2097184 | tf_op jit(solution)/shard_map/all_to_all | solution.py:790
  62.0 103.4 %shard_map.151.sums_ref = bf16[4608,256]{1,0:T(8,128)(2,1)S(1)} custom-call(s32[32]{0:T(128)S(1)} %get-tuple-element.76.index_ref, s32[32]{0:T(128)S(1)} %get-tuple-element.77.low_ref, s32[32]{0:T(128)S(1)} %get-tuple-element.78.count_ref, s32[33]{0:T(128)S(1)} %get-tuple-element.182.base_ref, s32[4]{0:T(128)S(1)} %get-tuple-element.79.turn_ref, ...), custom_call_target="tpu_custom_call" | custom-call | flops 34359738368 | bytes 4194304 | tf_op jit(solution)/shard_map/pallas_call | solution.py:451
  165.4 2.6 %shard_map.152 = bf16[1664,256]{1,0:T(8,128)(2,1)S(1)} custom-call(s32[33]{0:T(128)S(1)} %get-tuple-element.182.base_ref, s32[8,4608]{1,0:T(8,128)S(1)} %shard_map.149.code_ref, bf16[4608,256]{1,0:T(8,128)(2,1)S(1)} %shard_map.151.sums_ref), custom_call_target="tpu_custom_call" | custom-call | flops 1962934272 | bytes 4718592 | tf_op jit(solution)/shard_map/pallas_call | solution.py:492
  167.9 0.3 while.10
  168.2 0.0 copy-start.4
  168.2 32.6 %all_to_all.31 = bf16[16,104,256]{2,1,0:T(8,128)(2,1)} all-to-all(bf16[16,104,256]{2,1,0:T(8,128)(2,1)S(1)} %bitcast.41), channel_id=1, replica_groups=mesh['grp'=2,'pts'=16] {'pts'}, dimensions={0} | all-to-all | bytes 1703936 | tf_op jit(solution)/shard_map/all_to_all | solution.py:790
  200.9 0.0 copy-done.4
  200.9 9.4 %shard_map.153 = (bf16[1024,512]{1,0:T(8,128)(2,1)}, bf16[16,112,256]{2,1,0:T(8,128)(2,1)}) custom-call(bf16[1664,256]{1,0:T(8,128)(2,1)} %bitcast.43, f32[1024,256]{1,0:T(8,128)S(1)} %copy-done.4, f32[1024,128]{1,0:T(8,128)S(1)} %get-tuple-element.205, bf16[256,512]{1,0:T(8,128)(2,1)} %w_ref.3, f32[1,512]{1,0:T(1,128)} %bitcast.52, f32[1,512]{1,0:T(1,128)} %bitcast.53, ...), custom_call_target="tpu_custom_call" | custom-call | flops 805306368 | bytes 4194304 | tf_op jit(solution)/shard_map/pallas_call | solution.py:644
  210.3 26.9 %all_to_all.32.grad_ref.arrived_ref = bf16[16,112,256]{2,1,0:T(8,128)(2,1)S(1)} all-to-all(bf16[16,112,256]{2,1,0:T(8,128)(2,1)} %get-tuple-element.88), channel_id=1, replica_groups=mesh['grp'=2,'pts'=16] {'pts'}, dimensions={0} | all-to-all | bytes 1835008 | tf_op jit(solution)/shard_map/all_to_all | solution.py:790
  237.2 0.8 shard_map.155
  238.0 4.5 %all-to-all-start.5 = ((bf16[16,32,256]{2,1,0:T(8,128)(2,1)}), bf16[16,32,256]{2,1,0:T(8,128)(2,1)S(1)}, u32[]{:S(2)}, u32[]{:S(2)}) async-start(bf16[16,32,256]{2,1,0:T(8,128)(2,1)} %get-tuple-element.89), calls=%async_computation.5 | async-start | bytes 524288 | tf_op jit(solution)/shard_map/all_to_all | solution.py:790
  242.4 5.4 %shard_map.154 = bf16[4096,256]{1,0:T(8,128)(2,1)} custom-call(s32[8,1024]{1,0:T(8,128)S(1)} %copy-done.3, bf16[16,112,256]{2,1,0:T(8,128)(2,1)S(1)} %all_to_all.32.grad_ref.arrived_ref), custom_call_target="tpu_custom_call" | custom-call | flops 2147483648 | bytes 4194304 | tf_op jit(solution)/shard_map/pallas_call | solution.py:696
  247.9 4.6 %all-to-all-done.5 = bf16[16,32,256]{2,1,0:T(8,128)(2,1)S(1)} async-done(((bf16[16,32,256]{2,1,0:T(8,128)(2,1)}), bf16[16,32,256]{2,1,0:T(8,128)(2,1)S(1)}, u32[]{:S(2)}, u32[]{:S(2)}) %all-to-all-start.5) | async-done | bytes 262176 | tf_op jit(solution)/shard_map/all_to_all | solution.py:790
  252.5 0.9 bitcast_convert_fusion
  (26 shorter events, 0.2 us)
Async XLA Ops:
  2.7 14.3 %all-to-all-start.1 = ((s32[16,8,128]{2,1,0:T(8,128)}), s32[16,8,128]{2,1,0:T(8,128)S(1)}, u32[]{:S(2)}, u32[]{:S(2)}) async-start(s32[16,8,128]{2,1,0:T(8,128)} %get-tuple-element.66), calls=%async_computation.1 | async-start | bytes 131072 | tf_op jit(solution)/shard_map/all_to_all | solution.py:790
  17.2 8.9 %copy-start.2 = (s32[4,1024]{1,0:T(4,128)S(1)}, s32[4,1024]{1,0:T(4,128)}, u32[]{:S(2)}) copy-start(s32[4,1024]{1,0:T(4,128)} %ids_ref.1) | copy-start | bytes 49156
  17.2 44.8 %all-to-all-start.2 = ((bf16[16,256,256]{2,1,0:T(8,128)(2,1)}), bf16[16,256,256]{2,1,0:T(8,128)(2,1)S(1)}, u32[]{:S(2)}, u32[]{:S(2)}) async-start(bf16[16,256,256]{2,1,0:T(8,128)(2,1)} %bitcast.42), calls=%async_computation.2 | async-start | bytes 4194304 | tf_op jit(solution)/shard_map/all_to_all | solution.py:790
  26.0 35.9 %copy-start = (bf16[256,768]{1,0:T(8,128)(2,1)S(1)}, bf16[256,768]{1,0:T(8,128)(2,1)}, u32[]{:S(2)}) copy-start(bf16[256,768]{1,0:T(8,128)(2,1)} %w_ref.2) | copy-start | bytes 1179652
  26.1 35.9 %copy-start.1 = (bf16[256,256]{1,0:T(8,128)(2,1)S(1)}, bf16[256,256]{1,0:T(8,128)(2,1)}, u32[]{:S(2)}) copy-start(bf16[256,256]{1,0:T(8,128)(2,1)} %wo_ref.1) | copy-start | bytes 393220
  165.3 2.6 %copy-start.5 = (bf16[4608,256]{1,0:T(8,128)(2,1)}, bf16[4608,256]{1,0:T(8,128)(2,1)S(1)}, u32[]{:S(2)}) copy-start(bf16[4608,256]{1,0:T(8,128)(2,1)S(1)} %shard_map.151.sums_ref) | copy-start | bytes 7077892
  168.2 32.7 %copy-start.4 = (f32[1024,256]{1,0:T(8,128)S(1)}, f32[1024,256]{1,0:T(8,128)}, u32[]{:S(2)}) copy-start(f32[1024,256]{1,0:T(8,128)} %get-tuple-element.85.more_ref) | copy-start | bytes 3145732
  210.3 32.2 %copy-start.3 = (s32[8,1024]{1,0:T(8,128)S(1)}, s32[8,1024]{1,0:T(8,128)}, u32[]{:S(2)}) copy-start(s32[8,1024]{1,0:T(8,128)} %get-tuple-element.87.span_ref) | copy-start | bytes 98308
  238.0 14.5 %all-to-all-start.5 = ((bf16[16,32,256]{2,1,0:T(8,128)(2,1)}), bf16[16,32,256]{2,1,0:T(8,128)(2,1)S(1)}, u32[]{:S(2)}, u32[]{:S(2)}) async-start(bf16[16,32,256]{2,1,0:T(8,128)(2,1)} %get-tuple-element.89), calls=%async_computation.5 | async-start | bytes 524288 | tf_op jit(solution)/shard_map/all_to_all | solution.py:790

commit v8 on v7

--- a/solution.py
+++ b/solution.py
@@ -614,7 +614,6 @@
     @pl.when(step == pl.num_programs(0) - 1)
     def _():
         each = acc.shape[0] // devices
-        tall = whole_tiles(each)
         exact = sums[0:2, :]
         high = exact.astype(BF).astype(F32)
         parts = []
@@ -622,23 +621,22 @@
             for row in range(2):
                 for low in range(0, acc.shape[1], width):
                     parts.append(value[row : row + 1, low : low + width])
-        norm = pad_rows(jnp.concatenate(parts, axis=0)).astype(BF)
+        norm = jnp.concatenate(parts, axis=0)
         for d in range(devices):
-            low = whole_tiles(per_owner)
+            parts = []
             for side in range(0, acc.shape[1], width):
-                part = acc[d * each : (d + 1) * each, side : side + width]
-                sent_ref[d, low : low + tall, :] = pad_rows(part).astype(BF)
-                low += tall
-            sent_ref[d, low:, :] = norm
+                parts.append(pad_rows(acc[d * each : (d + 1) * each, side : side + width]))
+            rest = jnp.concatenate(parts + [norm], axis=0)
+            sent_ref[d, whole_tiles(per_owner) :, :] = rest.astype(BF)
 
 
 def pool(pieces, more, about, w_pool, gain, shift, cotangent):
     parents, width = more.shape
     wide = w_pool.shape[1]
-    chunk = 512
+    chunk = parents
     devices = pieces.shape[0] // SEAT
     tall = whole_tiles(parents // devices) + wide // width * whole_tiles(width // devices)
-    tall += whole_tiles(4 * wide // width)
+    tall += 4 * wide // width
     fixed = lambda i: (0, 0)
     along = lambda i: (i, 0)
     return pl.pallas_call(

time: 254 us -> 252 us (level)
  no operation moved by 1% of the time
where the time goes in v8:
time: 252 us; the launch traced here: 251 us
  Pallas kernels  150 us (60%)
  blocking collectives  58.4 us (23%)
  starting transfers between devices  15.3 us (6%)
  waiting for transfers between devices  14.9 us (6%)
  other arithmetic  8.93 us (4%)
    pallas_call x1, Pallas kernels, attend(): pl.pallas_call(attend_kernel, out_shape=jax.ShapeDtypeStruct((tiles * spa...  103 us
    all_to_all x2, blocking collectives, swap(): return lax.all_to_all(parts, 'pts', split_axis=0, concat_axis=0, tiled=True)  58.4 us
    pallas_call x1, Pallas kernels, seat_rows(): pl.pallas_call(functools.partial(seat_kernel, per_owner), out_shape=(jax....  21.1 us
    all_to_all x3, starting transfers between devices, swap(): return lax.all_to_all(parts, 'pts', split_axis=0, concat_axis=0, tiled=True)  15.3 us
    all_to_all x3, waiting for transfers between devices, swap(): return lax.all_to_all(parts, 'pts', split_axis=0, concat_axis=0, tiled=True)  14.9 us
    pallas_call x1, Pallas kernels, pool(): pl.pallas_call(functools.partial(pool_kernel, parents * SEAT // pieces.sh...  8.74 us
    pallas_call x1, Pallas kernels, spread_grads(): pl.pallas_call(spread_kernel, grid=(rows // chunk,), out_shape=jax.ShapeD...  5.42 us
  transfers between devices with their start and end apart: 3, of which 3 were waited for; matrix products, arithmetic and copies ran while one was open for 4% of the time, Pallas kernels for 13%

profile of v8, /device:TPU:0, one launch (start us, length us, event | category | flops | bytes accessed | tf_op | source)
XLA Modules:
  0.0 251.3 jit_solution(9244547153215550022)
XLA Ops:
  0.7 2.0 shard_map.147
  2.7 7.4 %all-to-all-start.1 = ((s32[16,8,128]{2,1,0:T(8,128)}), s32[16,8,128]{2,1,0:T(8,128)S(1)}, u32[]{:S(2)}, u32[]{:S(2)}) async-start(s32[16,8,128]{2,1,0:T(8,128)} %get-tuple-element.66), calls=%async_computation.1 | async-start | bytes 131072 | tf_op jit(solution)/shard_map/all_to_all | solution.py:788
  10.1 3.7 %shard_map.150 = bf16[4096,256]{1,0:T(8,128)(2,1)} custom-call(s32[32]{0:T(128)} %dest_ref.1, bf16[4096,256]{1,0:T(8,128)(2,1)} %points_ref.1), custom_call_target="tpu_custom_call" | custom-call | bytes 4194304 | tf_op jit(solution)/shard_map/pallas_call | solution.py:122
  13.8 3.2 %all-to-all-done.1 = s32[16,8,128]{2,1,0:T(8,128)S(1)} async-done(((s32[16,8,128]{2,1,0:T(8,128)}), s32[16,8,128]{2,1,0:T(8,128)S(1)}, u32[]{:S(2)}, u32[]{:S(2)}) %all-to-all-start.1) | async-done | bytes 65568 | tf_op jit(solution)/shard_map/all_to_all | solution.py:788
  17.0 0.1 add_select_fusion.9
  17.2 0.0 copy-start.2
  17.2 3.7 %all-to-all-start.2 = ((bf16[16,256,256]{2,1,0:T(8,128)(2,1)}), bf16[16,256,256]{2,1,0:T(8,128)(2,1)S(1)}, u32[]{:S(2)}, u32[]{:S(2)}) async-start(bf16[16,256,256]{2,1,0:T(8,128)(2,1)} %bitcast.42), calls=%async_computation.2 | async-start | bytes 4194304 | tf_op jit(solution)/shard_map/all_to_all | solution.py:788
  20.9 1.0 select_reduce_fusion.1
  22.0 0.1 multiply_select_fusion
  22.0 0.1 reshape.577
  22.1 0.1 reshape.575
  22.2 0.1 add_select_fusion.10
  22.3 0.1 reshape.576
  22.4 0.1 reshape.578
  22.4 0.1 reduce_sum.73
  22.5 0.1 reduce_sum.74
  22.6 0.1 reshape.579
  22.7 0.4 add_select_fusion.5
  23.1 0.7 add_reduce_fusion
  23.8 0.6 reduce_max.9
  25.1 0.1 broadcast_in_dim.115
  25.2 0.1 fusion.27
  25.3 0.3 convert_reduce_fusion.2
  25.7 0.1 add_select_fusion.12
  25.7 0.3 select_reduce_fusion.2
  26.0 0.0 copy-done.2
  26.0 0.0 copy-start
  26.1 0.0 copy-start.1
  26.1 21.1 %shard_map.148 = (bf16[4608,128]{1,0:T(8,128)(2,1)}, s32[32,128]{1,0:T(8,128)S(1)}, s32[33]{0:T(128)S(1)}, s32[32]{0:T(128)S(1)}, s32[32]{0:T(128)S(1)}, /*index=5*/s32[4]{0:T(128)S(1)}, s32[4,1024]{1,0:T(4,128)S(1)}) custom-call(s32[32]{0:T(128)S(1)} %get-tuple-element.109.source_ref, s32[32]{0:T(128)S(1)} %get-tuple-element.124.block_ref, ...), custom_call_target="tpu_custom_call" | custom-call | flops 167772160 | bytes 32768 | tf_op jit(solution)/shard_map/pallas_call | solution.py:248
  47.1 2.0 shard_map.149.code_ref
  49.2 3.3 %convert_reduce_fusion.1 = (s32[1024]{0:T(1024)S(1)}, s32[1024]{0:T(1024)S(1)}) fusion(s32[2048]{0:T(1024)S(1)} %bitcast.51, s32[1024]{0:T(1024)S(1)} %broadcast_multiply_fusion.1, s32[1024]{0:T(1024)S(1)} %reshape.575, s32[1024]{0:T(1024)S(1)} %broadcast_multiply_fusion, s32[1024]{0:T(1024)S(1)} %reshape.578), kind=kLoop, calls=%fused_computation.1 | loop fusion | flops 20969472 | bytes 32768 | tf_op jit(solution)/shard_map/reduce_sum | solution.py:775
  52.5 0.7 select_convert_fusion.about_ref
  53.3 0.4 slice_reduce_fusion
  53.6 1.2 broadcast_in_dim.118
  54.8 7.2 %all-to-all-done.2 = bf16[16,256,256]{2,1,0:T(8,128)(2,1)S(1)} async-done(((bf16[16,256,256]{2,1,0:T(8,128)(2,1)}), bf16[16,256,256]{2,1,0:T(8,128)(2,1)S(1)}, u32[]{:S(2)}, u32[]{:S(2)}) %all-to-all-start.2) | async-done | bytes 2097184 | tf_op jit(solution)/shard_map/all_to_all | solution.py:788
  62.0 103.4 %shard_map.151.sums_ref = bf16[4608,256]{1,0:T(8,128)(2,1)S(1)} custom-call(s32[32]{0:T(128)S(1)} %get-tuple-element.76.index_ref, s32[32]{0:T(128)S(1)} %get-tuple-element.77.low_ref, s32[32]{0:T(128)S(1)} %get-tuple-element.78.count_ref, s32[33]{0:T(128)S(1)} %get-tuple-element.182.base_ref, s32[4]{0:T(128)S(1)} %get-tuple-element.79.turn_ref, ...), custom_call_target="tpu_custom_call" | custom-call | flops 34359738368 | bytes 4194304 | tf_op jit(solution)/shard_map/pallas_call | solution.py:451
  165.4 2.6 %shard_map.152 = bf16[1664,256]{1,0:T(8,128)(2,1)S(1)} custom-call(s32[33]{0:T(128)S(1)} %get-tuple-element.182.base_ref, s32[8,4608]{1,0:T(8,128)S(1)} %shard_map.149.code_ref, bf16[4608,256]{1,0:T(8,128)(2,1)S(1)} %shard_map.151.sums_ref), custom_call_target="tpu_custom_call" | custom-call | flops 1962934272 | bytes 4718592 | tf_op jit(solution)/shard_map/pallas_call | solution.py:492
  167.9 0.3 while.10
  168.2 0.0 copy-start.4
  168.2 32.6 %all_to_all.31 = bf16[16,104,256]{2,1,0:T(8,128)(2,1)} all-to-all(bf16[16,104,256]{2,1,0:T(8,128)(2,1)S(1)} %bitcast.41), channel_id=1, replica_groups=mesh['grp'=2,'pts'=16] {'pts'}, dimensions={0} | all-to-all | bytes 1703936 | tf_op jit(solution)/shard_map/all_to_all | solution.py:788
  200.9 0.0 copy-done.4
  200.9 8.7 %shard_map.153 = (bf16[1024,512]{1,0:T(8,128)(2,1)}, bf16[16,104,256]{2,1,0:T(8,128)(2,1)}) custom-call(bf16[1664,256]{1,0:T(8,128)(2,1)} %bitcast.43, f32[1024,256]{1,0:T(8,128)S(1)} %copy-done.4, f32[1024,128]{1,0:T(8,128)S(1)} %get-tuple-element.205, bf16[256,512]{1,0:T(8,128)(2,1)} %w_ref.3, f32[1,512]{1,0:T(1,128)} %bitcast.52, f32[1,512]{1,0:T(1,128)} %bitcast.53, ...), custom_call_target="tpu_custom_call" | custom-call | flops 805306368 | bytes 4194304 | tf_op jit(solution)/shard_map/pallas_call | solution.py:642
  209.6 25.8 %all_to_all.32.grad_ref.arrived_ref = bf16[16,104,256]{2,1,0:T(8,128)(2,1)S(1)} all-to-all(bf16[16,104,256]{2,1,0:T(8,128)(2,1)} %get-tuple-element.88), channel_id=1, replica_groups=mesh['grp'=2,'pts'=16] {'pts'}, dimensions={0} | all-to-all | bytes 1703936 | tf_op jit(solution)/shard_map/all_to_all | solution.py:788
  235.4 0.8 shard_map.155
  236.1 4.2 %all-to-all-start.5 = ((bf16[16,32,256]{2,1,0:T(8,128)(2,1)}), bf16[16,32,256]{2,1,0:T(8,128)(2,1)S(1)}, u32[]{:S(2)}, u32[]{:S(2)}) async-start(bf16[16,32,256]{2,1,0:T(8,128)(2,1)} %get-tuple-element.89), calls=%async_computation.5 | async-start | bytes 524288 | tf_op jit(solution)/shard_map/all_to_all | solution.py:788
  240.4 5.4 %shard_map.154 = bf16[4096,256]{1,0:T(8,128)(2,1)} custom-call(s32[8,1024]{1,0:T(8,128)S(1)} %copy-done.3, bf16[16,104,256]{2,1,0:T(8,128)(2,1)S(1)} %all_to_all.32.grad_ref.arrived_ref), custom_call_target="tpu_custom_call" | custom-call | flops 2147483648 | bytes 4194304 | tf_op jit(solution)/shard_map/pallas_call | solution.py:694
  245.8 4.6 %all-to-all-done.5 = bf16[16,32,256]{2,1,0:T(8,128)(2,1)S(1)} async-done(((bf16[16,32,256]{2,1,0:T(8,128)(2,1)}), bf16[16,32,256]{2,1,0:T(8,128)(2,1)S(1)}, u32[]{:S(2)}, u32[]{:S(2)}) %all-to-all-start.5) | async-done | bytes 262176 | tf_op jit(solution)/shard_map/all_to_all | solution.py:788
  250.5 0.9 bitcast_convert_fusion
  (26 shorter events, 0.2 us)
Async XLA Ops:
  2.7 14.3 %all-to-all-start.1 = ((s32[16,8,128]{2,1,0:T(8,128)}), s32[16,8,128]{2,1,0:T(8,128)S(1)}, u32[]{:S(2)}, u32[]{:S(2)}) async-start(s32[16,8,128]{2,1,0:T(8,128)} %get-tuple-element.66), calls=%async_computation.1 | async-start | bytes 131072 | tf_op jit(solution)/shard_map/all_to_all | solution.py:788
  17.2 8.9 %copy-start.2 = (s32[4,1024]{1,0:T(4,128)S(1)}, s32[4,1024]{1,0:T(4,128)}, u32[]{:S(2)}) copy-start(s32[4,1024]{1,0:T(4,128)} %ids_ref.1) | copy-start | bytes 49156
  17.2 44.8 %all-to-all-start.2 = ((bf16[16,256,256]{2,1,0:T(8,128)(2,1)}), bf16[16,256,256]{2,1,0:T(8,128)(2,1)S(1)}, u32[]{:S(2)}, u32[]{:S(2)}) async-start(bf16[16,256,256]{2,1,0:T(8,128)(2,1)} %bitcast.42), calls=%async_computation.2 | async-start | bytes 4194304 | tf_op jit(solution)/shard_map/all_to_all | solution.py:788
  26.0 35.9 %copy-start = (bf16[256,768]{1,0:T(8,128)(2,1)S(1)}, bf16[256,768]{1,0:T(8,128)(2,1)}, u32[]{:S(2)}) copy-start(bf16[256,768]{1,0:T(8,128)(2,1)} %w_ref.2) | copy-start | bytes 1179652
  26.1 35.9 %copy-start.1 = (bf16[256,256]{1,0:T(8,128)(2,1)S(1)}, bf16[256,256]{1,0:T(8,128)(2,1)}, u32[]{:S(2)}) copy-start(bf16[256,256]{1,0:T(8,128)(2,1)} %wo_ref.1) | copy-start | bytes 393220
  165.3 2.6 %copy-start.5 = (bf16[4608,256]{1,0:T(8,128)(2,1)}, bf16[4608,256]{1,0:T(8,128)(2,1)S(1)}, u32[]{:S(2)}) copy-start(bf16[4608,256]{1,0:T(8,128)(2,1)S(1)} %shard_map.151.sums_ref) | copy-start | bytes 7077892
  168.2 32.7 %copy-start.4 = (f32[1024,256]{1,0:T(8,128)S(1)}, f32[1024,256]{1,0:T(8,128)}, u32[]{:S(2)}) copy-start(f32[1024,256]{1,0:T(8,128)} %get-tuple-element.85.more_ref) | copy-start | bytes 3145732
  209.6 30.7 %copy-start.3 = (s32[8,1024]{1,0:T(8,128)S(1)}, s32[8,1024]{1,0:T(8,128)}, u32[]{:S(2)}) copy-start(s32[8,1024]{1,0:T(8,128)} %get-tuple-element.87.span_ref) | copy-start | bytes 98308
  236.1 14.3 %all-to-all-start.5 = ((bf16[16,32,256]{2,1,0:T(8,128)(2,1)}), bf16[16,32,256]{2,1,0:T(8,128)(2,1)S(1)}, u32[]{:S(2)}, u32[]{:S(2)}) async-start(bf16[16,32,256]{2,1,0:T(8,128)(2,1)} %get-tuple-element.89), calls=%async_computation.5 | async-start | bytes 524288 | tf_op jit(solution)/shard_map/all_to_all | solution.py:788

commit v9 on v8

--- a/solution.py
+++ b/solution.py
@@ -11,7 +11,7 @@
 HDIM = 16
 HEAD_GROUP = 8
 ROWS = 128
-SEAT = 104
+SEAT = 96
 TURN = 16 * SEAT
 INFO = 8
 ALIGN = 16

time: 252 us -> 250 us (level)
  no operation moved by 1% of the time
where the time goes in v9:
time: 250 us; the launch traced here: 249 us
  Pallas kernels  149 us (60%)
  blocking collectives  57 us (23%)
  starting transfers between devices  15.3 us (6%)
  waiting for transfers between devices  14.9 us (6%)
  other arithmetic  8.93 us (4%)
    pallas_call x1, Pallas kernels, attend(): pl.pallas_call(attend_kernel, out_shape=jax.ShapeDtypeStruct((tiles * spa...  103 us
    all_to_all x2, blocking collectives, swap(): return lax.all_to_all(parts, 'pts', split_axis=0, concat_axis=0, tiled=True)  57 us
    pallas_call x1, Pallas kernels, seat_rows(): pl.pallas_call(functools.partial(seat_kernel, per_owner), out_shape=(jax....  21.1 us
    all_to_all x3, starting transfers between devices, swap(): return lax.all_to_all(parts, 'pts', split_axis=0, concat_axis=0, tiled=True)  15.3 us
    all_to_all x3, waiting for transfers between devices, swap(): return lax.all_to_all(parts, 'pts', split_axis=0, concat_axis=0, tiled=True)  14.9 us
    pallas_call x1, Pallas kernels, pool(): pl.pallas_call(functools.partial(pool_kernel, parents * SEAT // pieces.sh...  8.41 us
    pallas_call x1, Pallas kernels, spread_grads(): pl.pallas_call(spread_kernel, grid=(rows // chunk,), out_shape=jax.ShapeD...  5.42 us
  transfers between devices with their start and end apart: 3, of which 3 were waited for; matrix products, arithmetic and copies ran while one was open for 4% of the time, Pallas kernels for 13%

profile of v9, /device:TPU:0, one launch (start us, length us, event | category | flops | bytes accessed | tf_op | source)
XLA Modules:
  0.0 249.4 jit_solution(7592688078695158640)
XLA Ops:
  0.7 2.0 shard_map.147
  2.7 7.4 %all-to-all-start.1 = ((s32[16,8,128]{2,1,0:T(8,128)}), s32[16,8,128]{2,1,0:T(8,128)S(1)}, u32[]{:S(2)}, u32[]{:S(2)}) async-start(s32[16,8,128]{2,1,0:T(8,128)} %get-tuple-element.66), calls=%async_computation.1 | async-start | bytes 131072 | tf_op jit(solution)/shard_map/all_to_all | solution.py:788
  10.1 3.7 %shard_map.150 = bf16[4096,256]{1,0:T(8,128)(2,1)} custom-call(s32[32]{0:T(128)} %dest_ref.1, bf16[4096,256]{1,0:T(8,128)(2,1)} %points_ref.1), custom_call_target="tpu_custom_call" | custom-call | bytes 4194304 | tf_op jit(solution)/shard_map/pallas_call | solution.py:122
  13.8 3.2 %all-to-all-done.1 = s32[16,8,128]{2,1,0:T(8,128)S(1)} async-done(((s32[16,8,128]{2,1,0:T(8,128)}), s32[16,8,128]{2,1,0:T(8,128)S(1)}, u32[]{:S(2)}, u32[]{:S(2)}) %all-to-all-start.1) | async-done | bytes 65568 | tf_op jit(solution)/shard_map/all_to_all | solution.py:788
  17.0 0.1 add_select_fusion.9
  17.2 0.0 copy-start.2
  17.2 3.7 %all-to-all-start.2 = ((bf16[16,256,256]{2,1,0:T(8,128)(2,1)}), bf16[16,256,256]{2,1,0:T(8,128)(2,1)S(1)}, u32[]{:S(2)}, u32[]{:S(2)}) async-start(bf16[16,256,256]{2,1,0:T(8,128)(2,1)} %bitcast.42), calls=%async_computation.2 | async-start | bytes 4194304 | tf_op jit(solution)/shard_map/all_to_all | solution.py:788
  20.9 1.0 select_reduce_fusion.1
  22.0 0.1 multiply_select_fusion
  22.0 0.1 reshape.577
  22.1 0.1 reshape.575
  22.2 0.1 add_select_fusion.10
  22.3 0.1 reshape.576
  22.4 0.1 reshape.578
  22.4 0.1 reduce_sum.73
  22.5 0.1 reduce_sum.74
  22.6 0.1 reshape.579
  22.7 0.4 add_select_fusion.5
  23.1 0.7 add_reduce_fusion
  23.8 0.6 reduce_max.9
  25.1 0.1 broadcast_in_dim.115
  25.2 0.1 fusion.27
  25.3 0.3 convert_reduce_fusion.2
  25.7 0.1 add_select_fusion.12
  25.7 0.3 select_reduce_fusion.2
  26.0 0.0 copy-done.2
  26.0 0.0 copy-start
  26.1 0.0 copy-start.1
  26.1 21.1 %shard_map.148 = (bf16[4608,128]{1,0:T(8,128)(2,1)}, s32[32,128]{1,0:T(8,128)S(1)}, s32[33]{0:T(128)S(1)}, s32[32]{0:T(128)S(1)}, s32[32]{0:T(128)S(1)}, /*index=5*/s32[4]{0:T(128)S(1)}, s32[4,1024]{1,0:T(4,128)S(1)}) custom-call(s32[32]{0:T(128)S(1)} %get-tuple-element.109.source_ref, s32[32]{0:T(128)S(1)} %get-tuple-element.124.block_ref, ...), custom_call_target="tpu_custom_call" | custom-call | flops 167772160 | bytes 32768 | tf_op jit(solution)/shard_map/pallas_call | solution.py:248
  47.1 2.0 shard_map.149.code_ref
  49.2 3.3 %convert_reduce_fusion.1 = (s32[1024]{0:T(1024)S(1)}, s32[1024]{0:T(1024)S(1)}) fusion(s32[2048]{0:T(1024)S(1)} %bitcast.51, s32[1024]{0:T(1024)S(1)} %broadcast_multiply_fusion.1, s32[1024]{0:T(1024)S(1)} %reshape.575, s32[1024]{0:T(1024)S(1)} %broadcast_multiply_fusion, s32[1024]{0:T(1024)S(1)} %reshape.578), kind=kLoop, calls=%fused_computation.1 | loop fusion | flops 20969472 | bytes 32768 | tf_op jit(solution)/shard_map/reduce_sum | solution.py:775
  52.5 0.7 select_convert_fusion.about_ref
  53.3 0.4 slice_reduce_fusion
  53.6 1.2 broadcast_in_dim.118
  54.8 7.2 %all-to-all-done.2 = bf16[16,256,256]{2,1,0:T(8,128)(2,1)S(1)} async-done(((bf16[16,256,256]{2,1,0:T(8,128)(2,1)}), bf16[16,256,256]{2,1,0:T(8,128)(2,1)S(1)}, u32[]{:S(2)}, u32[]{:S(2)}) %all-to-all-start.2) | async-done | bytes 2097184 | tf_op jit(solution)/shard_map/all_to_all | solution.py:788
  62.0 0.0 copy-done
  62.0 103.4 %shard_map.151.sums_ref = bf16[4608,256]{1,0:T(8,128)(2,1)S(1)} custom-call(s32[32]{0:T(128)S(1)} %get-tuple-element.76.index_ref, s32[32]{0:T(128)S(1)} %get-tuple-element.77.low_ref, s32[32]{0:T(128)S(1)} %get-tuple-element.78.count_ref, s32[33]{0:T(128)S(1)} %get-tuple-element.182.base_ref, s32[4]{0:T(128)S(1)} %get-tuple-element.79.turn_ref, ...), custom_call_target="tpu_custom_call" | custom-call | flops 34359738368 | bytes 4194304 | tf_op jit(solution)/shard_map/pallas_call | solution.py:451
  165.4 2.4 shard_map.152
  167.8 0.3 while.10
  168.1 0.0 copy-start.4
  168.1 31.5 %all_to_all.31 = bf16[16,96,256]{2,1,0:T(8,128)(2,1)} all-to-all(bf16[16,96,256]{2,1,0:T(8,128)(2,1)S(1)} %bitcast.41), channel_id=1, replica_groups=mesh['grp'=2,'pts'=16] {'pts'}, dimensions={0} | all-to-all | bytes 1572864 | tf_op jit(solution)/shard_map/all_to_all | solution.py:788
  199.6 8.4 %shard_map.153 = (bf16[1024,512]{1,0:T(8,128)(2,1)}, bf16[16,104,256]{2,1,0:T(8,128)(2,1)}) custom-call(bf16[1536,256]{1,0:T(8,128)(2,1)} %bitcast.43, f32[1024,256]{1,0:T(8,128)S(1)} %copy-done.4, f32[1024,128]{1,0:T(8,128)S(1)} %get-tuple-element.205, bf16[256,512]{1,0:T(8,128)(2,1)} %w_ref.3, f32[1,512]{1,0:T(1,128)} %bitcast.52, f32[1,512]{1,0:T(1,128)} %bitcast.53, ...), custom_call_target="tpu_custom_call" | custom-call | flops 805306368 | bytes 4194304 | tf_op jit(solution)/shard_map/pallas_call | solution.py:642
  208.0 25.5 %all_to_all.32.grad_ref.arrived_ref = bf16[16,104,256]{2,1,0:T(8,128)(2,1)S(1)} all-to-all(bf16[16,104,256]{2,1,0:T(8,128)(2,1)} %get-tuple-element.88), channel_id=1, replica_groups=mesh['grp'=2,'pts'=16] {'pts'}, dimensions={0} | all-to-all | bytes 1703936 | tf_op jit(solution)/shard_map/all_to_all | solution.py:788
  233.5 0.8 shard_map.155
  234.2 4.2 %all-to-all-start.5 = ((bf16[16,32,256]{2,1,0:T(8,128)(2,1)}), bf16[16,32,256]{2,1,0:T(8,128)(2,1)S(1)}, u32[]{:S(2)}, u32[]{:S(2)}) async-start(bf16[16,32,256]{2,1,0:T(8,128)(2,1)} %get-tuple-element.89), calls=%async_computation.5 | async-start | bytes 524288 | tf_op jit(solution)/shard_map/all_to_all | solution.py:788
  238.5 5.4 %shard_map.154 = bf16[4096,256]{1,0:T(8,128)(2,1)} custom-call(s32[8,1024]{1,0:T(8,128)S(1)} %copy-done.3, bf16[16,104,256]{2,1,0:T(8,128)(2,1)S(1)} %all_to_all.32.grad_ref.arrived_ref), custom_call_target="tpu_custom_call" | custom-call | flops 2147483648 | bytes 4194304 | tf_op jit(solution)/shard_map/pallas_call | solution.py:694
  243.9 4.6 %all-to-all-done.5 = bf16[16,32,256]{2,1,0:T(8,128)(2,1)S(1)} async-done(((bf16[16,32,256]{2,1,0:T(8,128)(2,1)}), bf16[16,32,256]{2,1,0:T(8,128)(2,1)S(1)}, u32[]{:S(2)}, u32[]{:S(2)}) %all-to-all-start.5) | async-done | bytes 262176 | tf_op jit(solution)/shard_map/all_to_all | solution.py:788
  248.6 0.9 bitcast_convert_fusion
  (26 shorter events, 0.2 us)
Async XLA Ops:
  2.7 14.3 %all-to-all-start.1 = ((s32[16,8,128]{2,1,0:T(8,128)}), s32[16,8,128]{2,1,0:T(8,128)S(1)}, u32[]{:S(2)}, u32[]{:S(2)}) async-start(s32[16,8,128]{2,1,0:T(8,128)} %get-tuple-element.66), calls=%async_computation.1 | async-start | bytes 131072 | tf_op jit(solution)/shard_map/all_to_all | solution.py:788
  17.2 8.9 %copy-start.2 = (s32[4,1024]{1,0:T(4,128)S(1)}, s32[4,1024]{1,0:T(4,128)}, u32[]{:S(2)}) copy-start(s32[4,1024]{1,0:T(4,128)} %ids_ref.1) | copy-start | bytes 49156
  17.2 44.8 %all-to-all-start.2 = ((bf16[16,256,256]{2,1,0:T(8,128)(2,1)}), bf16[16,256,256]{2,1,0:T(8,128)(2,1)S(1)}, u32[]{:S(2)}, u32[]{:S(2)}) async-start(bf16[16,256,256]{2,1,0:T(8,128)(2,1)} %bitcast.42), calls=%async_computation.2 | async-start | bytes 4194304 | tf_op jit(solution)/shard_map/all_to_all | solution.py:788
  26.0 35.9 %copy-start = (bf16[256,768]{1,0:T(8,128)(2,1)S(1)}, bf16[256,768]{1,0:T(8,128)(2,1)}, u32[]{:S(2)}) copy-start(bf16[256,768]{1,0:T(8,128)(2,1)} %w_ref.2) | copy-start | bytes 1179652
  26.1 35.9 %copy-start.1 = (bf16[256,256]{1,0:T(8,128)(2,1)S(1)}, bf16[256,256]{1,0:T(8,128)(2,1)}, u32[]{:S(2)}) copy-start(bf16[256,256]{1,0:T(8,128)(2,1)} %wo_ref.1) | copy-start | bytes 393220
  165.4 2.5 copy-start.5
  168.1 31.5 %copy-start.4 = (f32[1024,256]{1,0:T(8,128)S(1)}, f32[1024,256]{1,0:T(8,128)}, u32[]{:S(2)}) copy-start(f32[1024,256]{1,0:T(8,128)} %get-tuple-element.85.more_ref) | copy-start | bytes 3145732
  208.0 30.4 %copy-start.3 = (s32[8,1024]{1,0:T(8,128)S(1)}, s32[8,1024]{1,0:T(8,128)}, u32[]{:S(2)}) copy-start(s32[8,1024]{1,0:T(8,128)} %get-tuple-element.87.span_ref) | copy-start | bytes 98308
  234.2 14.3 %all-to-all-start.5 = ((bf16[16,32,256]{2,1,0:T(8,128)(2,1)}), bf16[16,32,256]{2,1,0:T(8,128)(2,1)S(1)}, u32[]{:S(2)}, u32[]{:S(2)}) async-start(bf16[16,32,256]{2,1,0:T(8,128)(2,1)} %get-tuple-element.89), calls=%async_computation.5 | async-start | bytes 524288 | tf_op jit(solution)/shard_map/all_to_all | solution.py:788
